TPU v7x, 256 devices: a whole 4x4x8 slice. The times are simulated.
256 devices in a mesh: dp: 32 (over x, y, core), expert: 8 (over z).
Axes of the slice: x: 4, y: 4, z: 8, core: 2. Of those that a mesh axis runs over, the one named last changes fastest.
Arguments:
- hidden_rows: bfloat16 [32768, 6, 1536], P(('dp', 'expert')), may hold values from -6 to 6
- out_grads: bfloat16 [32768, 2560], P(('dp', 'expert')), may hold values from -12 to 12
- gates: float32 [32768, 6], P(('dp', 'expert')), may hold values from 0.1 to 1
- routes: int32 [32768, 6], P(('dp', 'expert')), may hold values from 0 to 159, all different within a row; in each aligned block of 128 rows (0 to 127, 128 to 255, ...) at most 6 rows name the same one
- panel_a: float32 [256, 32, 384], P(('dp', 'expert')), may hold values from -6 to 6
- panel_g: float32 [256, 32, 640], P(('dp', 'expert')), may hold values from -6 to 6
Outputs:
- input_cov: float32 [256, 384, 1536], P(('dp', 'expert'))
- grad_cov: float32 [256, 640, 2560], P(('dp', 'expert'))
- input_panel: float32 [256, 32, 384], P(('dp', 'expert'))
- grad_panel: float32 [256, 32, 640], P(('dp', 'expert'))
Inputs may be any that keep to these rules, and one draw needn't show every extreme that they name: `routes`: each row names 6 different experts. Among the 128 rows of one device no expert is named more than 6 times, a bound that some block reaches.
All inputs are finite; a program needn't handle non-finite values.
Results may differ from a plain program's by a relative error of at most 0.0037.
Values may be sent and summed in bfloat16 or wider, within the bound.
No kernel may reach another device: no remote copies, remote signals or barrier semaphores. Data moves between devices by JAX's collectives and lax.ppermute only.
A program may use at most 128 MiB of HBM per device.

v0:
```python
import jax
import jax.numpy as jnp
from jax import lax
from jax.sharding import PartitionSpec as P

ROUTED = 160
OWNERS = 4


def swapped(value, axis, apart):
    mask = 2**apart
    pairs = [(source, source ^ mask) for source in range(lax.axis_size(axis))]
    return lax.ppermute(value, axis, pairs)


def per_device(hidden_rows, out_grads, gates, routes, panel_a, panel_g):
    tok_dev, slots, width_in = hidden_rows.shape
    width_out = out_grads.shape[1]
    expert_count = lax.axis_size("expert")
    data_count = lax.axis_size("dp")
    groups = data_count // OWNERS
    flight = groups * expert_count
    capacity = max(2, tok_dev * slots * 5 // (ROUTED * 4))
    entries = tok_dev * slots
    expert_ids = routes.reshape(entries)
    window = jnp.arange(flight, dtype=jnp.int32)
    one_hot = (expert_ids[:, None] == window[None, :]).astype(jnp.int32)
    before = jnp.cumsum(one_hot, axis=0) - one_hot
    slot_index = jnp.sum(before * one_hot, axis=1)
    target = jnp.where(expert_ids < flight, expert_ids * capacity + slot_index, flight * capacity)
    scaled = (gates[:, :, None] * out_grads[:, None, :].astype(jnp.float32)).astype(jnp.bfloat16)
    slot_rows = jnp.concatenate(
        [hidden_rows.reshape(entries, width_in), scaled.reshape(entries, width_out)], axis=1
    )
    features = width_in + width_out
    packed = (
        jnp.zeros((flight * capacity, features), jnp.bfloat16)
        .at[target]
        .set(slot_rows, mode="drop")
    )
    packed = packed.reshape(groups, expert_count, capacity, features)
    copies = jnp.repeat(packed, OWNERS, axis=0)
    arrived = lax.all_to_all(
        lax.all_to_all(copies, "dp", split_axis=0, concat_axis=0, tiled=True),
        "expert",
        split_axis=1,
        concat_axis=1,
        tiled=True,
    )
    gathered = arrived.reshape(-1, features)
    quarter = lax.axis_index("dp") % OWNERS
    norm_factor = ROUTED / (tok_dev * data_count * expert_count * slots)
    block_in = width_in // OWNERS
    block_out = width_out // OWNERS
    rows_in = lax.dynamic_slice_in_dim(gathered, quarter * block_in, block_in, 1)
    rows_out = lax.dynamic_slice_in_dim(gathered, width_in + quarter * block_out, block_out, 1)
    contract = (((0,), (0,)), ((), ()))
    input_cov = (
        lax.dot_general(
            rows_in, gathered[:, :width_in], contract, preferred_element_type=jnp.float32
        )
        * norm_factor
    )
    grad_cov = (
        lax.dot_general(
            rows_out, gathered[:, width_in:], contract, preferred_element_type=jnp.float32
        )
        * norm_factor
    )
    panel_rows_count = panel_a.shape[1]
    partial_a = jnp.dot(panel_a[0], input_cov, precision=lax.Precision.HIGHEST)
    partial_g = jnp.dot(panel_g[0], grad_cov, precision=lax.Precision.HIGHEST)
    shares_a = partial_a.reshape(panel_rows_count, 2, 2, block_in)
    shares_g = partial_g.reshape(panel_rows_count, 2, 2, block_out)
    for bit_number in (1, 0):
        own_bit = quarter // (1 << bit_number) % 2
        kept_a = lax.dynamic_index_in_dim(shares_a, own_bit, 1, keepdims=False)
        kept_g = lax.dynamic_index_in_dim(shares_g, own_bit, 1, keepdims=False)
        sent_a = lax.dynamic_index_in_dim(shares_a, 1 - own_bit, 1, keepdims=False)
        sent_g = lax.dynamic_index_in_dim(shares_g, 1 - own_bit, 1, keepdims=False)
        got_a, got_g = swapped((sent_a, sent_g), "dp", bit_number)
        shares_a = kept_a + got_a
        shares_g = kept_g + got_g
    input_panel = shares_a[None]
    grad_panel = shares_g[None]
    return (input_cov[None], grad_cov[None], input_panel, grad_panel)


def solution(mesh):
    placed = (
        P(("dp", "expert"), None, None),
        P(("dp", "expert"), None),
        P(("dp", "expert"), None),
        P(("dp", "expert"), None),
        P(("dp", "expert"), None, None),
        P(("dp", "expert"), None, None),
    )
    return jax.shard_map(
        per_device,
        mesh=mesh,
        in_specs=placed,
        out_specs=(
            P(("dp", "expert"), None, None),
            P(("dp", "expert"), None, None),
            P(("dp", "expert"), None, None),
            P(("dp", "expert"), None, None),
        ),
        check_vma=False,
    )
```

profile of v0, /device:TPU:1, one launch (start us, length us, event | category | flops | bytes accessed | tf_op | source)
XLA Modules:
  0.0 580.8 jit_solution(11008821515219067633)
XLA Ops:
  0.6 0.7 broadcast_compare_fusion
  1.4 0.7 broadcast_multiply_fusion
  2.1 0.8 copy.23
  3.7 1.8 reduce-window.6
  5.8 6.4 %mul.61 = f32[128,6,2560]{2,1,0:T(8,128)} broadcast(bf16[128,2560]{1,0:T(8,128)(2,1)} %param.7), dimensions={0,2} | broadcast | bytes 8519680 | tf_op jit(solution)/shard_map/mul | solution.py:31
  12.2 9.5 %mul.62 = f32[768,2560]{1,0:T(8,128)} reshape(f32[128,6,2560]{2,1,0:T(8,128)} %mul.61) | data formatting | bytes 15728640 | tf_op jit(solution)/shard_map/mul | solution.py:31
  22.0 3.0 copy.26
  25.0 2.2 reshape.94
  27.3 5.6 multiply_convert_fusion
  33.0 15.0 %scatter_custom_fusion = bf16[384,4096]{1,0:T(8,128)(2,1)S(1)} fusion(s32[768]{0:T(1024)S(1)} %fusion.30, bf16[768,2560]{1,0:T(8,128)(2,1)} %multiply_convert_fusion, bf16[]{:T(256)} %constant.113, bf16[768,1536]{1,0:T(8,128)(2,1)} %reshape.94, bf16[]{:T(256)} %constant.88.clone.1), kind=kCustom, calls=%fused_computation.4 | custom fusion | flops 12582912 | bytes 9437188 | tf_op jit(solution)/shard_map/scatter | solution.py:39
  48.0 2.8 reshape.95
  50.8 4.0 copy.28
  54.8 6.2 %broadcast_in_dim.28 = bf16[8,4,8,6,4096]{4,2,3,1,0:T(8,128)(2,1)} broadcast(bf16[8,8,6,4096]{3,1,2,0:T(8,128)(2,1)S(1)} %copy.28), dimensions={0,2,3,4} | broadcast | bytes 15728640 | tf_op jit(solution)/shard_map/broadcast_in_dim | solution.py:42
  61.0 149.1 %all_to_all.10 = bf16[32,8,6,4096]{3,1,2,0:T(8,128)(2,1)S(1)} all-to-all(bf16[32,8,6,4096]{3,1,2,0:T(8,128)(2,1)} %bitcast.65), channel_id=1, replica_groups=mesh['dp'=32,'expert'=8] {'dp'}, dimensions={0} | all-to-all | bytes 25165824 | tf_op jit(solution)/shard_map/all_to_all | solution.py:44
  210.1 17.5 %copy.29 = bf16[32,8,6,4096]{3,0,2,1:T(8,128)(2,1)} copy(bf16[32,8,6,4096]{3,1,2,0:T(8,128)(2,1)S(1)} %all_to_all.10) | data formatting | bytes 25165824 | tf_op jit(solution)/shard_map/all_to_all | solution.py:44
  227.5 8.2 %all-to-all-start.1 = ((bf16[32,8,6,4096]{3,0,2,1:T(8,128)(2,1)}), bf16[32,8,6,4096]{3,0,2,1:T(8,128)(2,1)}, u32[]{:S(2)}, u32[]{:S(2)}) async-start(bf16[32,8,6,4096]{3,0,2,1:T(8,128)(2,1)} %copy.29), calls=%async_computation.1 | async-start | bytes 25165824 | tf_op jit(solution)/shard_map/all_to_all | solution.py:43
  235.7 277.3 %all-to-all-done.1 = bf16[32,8,6,4096]{3,0,2,1:T(8,128)(2,1)} async-done(((bf16[32,8,6,4096]{3,0,2,1:T(8,128)(2,1)}), bf16[32,8,6,4096]{3,0,2,1:T(8,128)(2,1)}, u32[]{:S(2)}, u32[]{:S(2)}) %all-to-all-start.1) | async-done | bytes 12582944 | tf_op jit(solution)/shard_map/all_to_all | solution.py:43
  513.0 13.8 %copy.30 = bf16[32,8,6,4096]{3,2,1,0:T(8,128)(2,1)} copy(bf16[32,8,6,4096]{3,0,2,1:T(8,128)(2,1)} %all-to-all-done.1) | data formatting | bytes 25165824 | tf_op jit(solution)/shard_map/all_to_all | solution.py:43
  526.9 18.8 %reshape.97 = bf16[1536,4096]{1,0:T(8,128)(2,1)} reshape(bf16[32,8,6,4096]{3,2,1,0:T(8,128)(2,1)} %copy.30) | data formatting | bytes 25165824 | tf_op jit(solution)/shard_map/reshape | solution.py:50
  545.7 4.7 fusion.14
  550.4 9.3 %fusion = f32[640,2560]{1,0:T(8,128)S(1)} fusion(bf16[1536,4096]{1,0:T(8,128)(2,1)} %reshape.97, s32[]{:T(128)S(6)} %select_n.71), kind=kOutput, calls=%fused_computation.1 | convolution fusion | flops 5033164800 | bytes 16384004 | tf_op jit(solution)/shard_map/dot_general | solution.py:65
  559.8 3.9 multiply_bitcast_fusion
  563.6 0.8 copy-done.1
  564.5 1.5 convolution_bitcast_fusion
  566.3 5.8 fusion.10
  572.4 1.5 collective-permute-start.2
  574.0 1.1 collective-permute-start.1
  575.1 2.7 collective-permute-done.2
  577.8 1.4 collective-permute-start.3
  579.2 0.6 fusion.28
  579.8 0.3 collective-permute-done.3
  580.1 0.6 fusion.26
  (35 shorter events, 2.2 us)
Async XLA Ops:
  0.6 565.7 %copy-start = (f32[1,32,640]{2,1,0:T(8,128)S(1)}, f32[1,32,640]{2,1,0:T(8,128)}, u32[]{:S(2)}) copy-start(f32[1,32,640]{2,1,0:T(8,128)} %param.11) | copy-start | bytes 245764
  12.2 9.5 %copy-start.4 = (f32[128,6]{0,1:T(8,128)S(1)}, f32[128,6]{0,1:T(8,128)}, u32[]{:S(2)}) copy-start(f32[128,6]{0,1:T(8,128)} %param.8) | copy-start | bytes 9220
  227.5 285.5 %all-to-all-start.1 = ((bf16[32,8,6,4096]{3,0,2,1:T(8,128)(2,1)}), bf16[32,8,6,4096]{3,0,2,1:T(8,128)(2,1)}, u32[]{:S(2)}, u32[]{:S(2)}) async-start(bf16[32,8,6,4096]{3,0,2,1:T(8,128)(2,1)} %copy.29), calls=%async_computation.1 | async-start | bytes 25165824 | tf_op jit(solution)/shard_map/all_to_all | solution.py:43
  550.4 13.2 %copy-start.2 = (f32[384,1536]{1,0:T(8,128)}, f32[384,1536]{1,0:T(8,128)S(1)}, u32[]{:S(2)}) copy-start(f32[384,1536]{1,0:T(8,128)S(1)} %fusion.14) | copy-start | bytes 7077892
  559.7 4.7 copy-start.1
  559.8 4.7 copy-start.3
  566.2 7.7 %collective-permute-start = (f32[32,2,384]{2,0,1:T(8,128)S(1)}, f32[32,2,384]{2,0,1:T(8,128)S(1)}, u32[]{:S(2)}, u32[]{:S(2)}) collective-permute-start(f32[32,2,384]{2,0,1:T(8,128)S(1)} %bitcast.68), channel_id=1, source_target_pairs={{0,16},{8,24},{16,0},{24,8},{32,48},{40,56},{48,32},{56,40},{64,80... | collective-permute-start | bytes 294920 | tf_op jit(solution)/shard_map/ppermute | solution.py:13
  572.4 5.4 collective-permute-start.2
  574.0 5.3 collective-permute-start.1
  577.8 2.3 collective-permute-start.3
where the time goes:
time: 582 us; the launch traced here: 581 us
  waiting for transfers between devices  280 us (48%)
  blocking collectives  149 us (26%)
  local copies, waits for them, and re-layouts  87.7 us (15%)
  other arithmetic  29.2 us (5%)
  matrix products  21.3 us (4%)
  starting transfers between devices  12.4 us (2%)
    all_to_all x1, waiting for transfers between devices, per_device(): lax.all_to_all(lax.all_to_all(copies, 'dp', split_axis=0, concat_axis=0,...  277 us
    all_to_all x1, blocking collectives, per_device(): lax.all_to_all(copies, 'dp', split_axis=0, concat_axis=0, tiled=True)  149 us
    reshape x1, local copies, waits for them, and re-layouts, per_device(): gathered = arrived.reshape(-1, features)  18.8 us
    all_to_all x1, local copies, waits for them, and re-layouts, per_device(): lax.all_to_all(copies, 'dp', split_axis=0, concat_axis=0, tiled=True)  17.5 us
    mul x3, local copies, waits for them, and re-layouts, per_device(): gates[:, :, None] * out_grads[:, None, :].astype(jnp.float32)  16 us
    scatter x1, other arithmetic, per_device(): packed = jnp.zeros((flight * capacity, features), jnp.bfloat16).at[target...  15 us
    all_to_all x1, local copies, waits for them, and re-layouts, per_device(): lax.all_to_all(lax.all_to_all(copies, 'dp', split_axis=0, concat_axis=0,...  13.8 us
  transfers between devices with their start and end apart: 5, of which 3 were waited for; matrix products, arithmetic and copies ran while one was open for 1% of the time, Pallas kernels for 0%

commit v1 on v0

v1 whole, which is shorter than its diff:
```python
import functools

import jax
import jax.numpy as jnp
from jax import lax
from jax.experimental import pallas as pl
from jax.experimental.pallas import tpu as pltpu
from jax.sharding import Mesh
from jax.sharding import PartitionSpec as P

ROUTED = 160
OWNERS = 4
CAP = 6
GROUPS = 8
Z = 8
FLIGHT = GROUPS * Z
AXES = ("x", "yh", "yl", "core", "z")
GRAD_CHUNKS = ((0, 2), (2, 6))
HIDDEN_CHUNKS = ((0, 6),)
f32 = jnp.float32
bf16 = jnp.bfloat16


def params(mib):
    return pltpu.CompilerParams(vmem_limit_bytes=mib * 2**20)


VMEM = pl.BlockSpec(memory_space=pltpu.VMEM)
SMEM = pl.BlockSpec(memory_space=pltpu.SMEM)


def slot_table(routes_ref, slots, tok):
    ids = routes_ref[...]
    upper = (
        lax.broadcasted_iota(jnp.int32, (tok, tok), 0) < lax.broadcasted_iota(jnp.int32, (tok, tok), 1)
    ).astype(bf16)
    window = lax.broadcasted_iota(jnp.int32, (FLIGHT, tok), 0)
    seen = jnp.zeros((FLIGHT, 1), f32)
    out = []
    for k in range(slots):
        named = (window == ids[k : k + 1, :]).astype(f32)
        before = jnp.dot(named.astype(bf16), upper, preferred_element_type=f32) + seen
        slot = jnp.sum(named * before, axis=0, keepdims=True)
        seen = seen + jnp.sum(named, axis=1, keepdims=True)
        out.append((ids[k : k + 1, :], slot.astype(jnp.int32)))
    return out


def targets(table, my_z, first, last):
    width = last - first
    out = []
    for ids, slot in table:
        away = (ids - my_z) & (Z - 1)
        group = lax.shift_right_logical(ids, 3)
        place = away * (GROUPS * width) + group * width + slot - first
        ok = (ids < FLIGHT) & (slot >= first) & (slot < last)
        out.append(jnp.where(ok, place, -1))
    return out


def pack_grad_kernel(chunks, z_ref, routes_ref, gates_ref, grads_ref, *outs):
    slots, tok = routes_ref.shape
    table = slot_table(routes_ref, slots, tok)
    for number, (first, last) in enumerate(chunks):
        rows = FLIGHT * (last - first)
        block = GROUPS * (last - first)
        position = lax.broadcasted_iota(jnp.int32, (rows, tok), 0)
        pick = jnp.zeros((rows, tok), f32)
        weight = jnp.zeros((rows, tok), f32)
        for k, target in enumerate(targets(table, z_ref[0, 0], first, last)):
            hit = position == target
            pick = jnp.where(hit, 1.0, pick)
            weight = jnp.where(hit, gates_ref[k : k + 1, :], weight)
        gate = jnp.sum(weight, axis=1, keepdims=True)
        picked = jnp.dot(pick.astype(bf16), grads_ref[...], preferred_element_type=f32)
        scaled = gate * picked
        for away in range(Z):
            outs[number * Z + away][...] = scaled[away * block : (away + 1) * block, :].astype(bf16)


def pack_hidden_kernel(chunks, z_ref, routes_ref, hidden_ref, *outs):
    slots, tok = routes_ref.shape
    table = slot_table(routes_ref, slots, tok)
    for number, (first, last) in enumerate(chunks):
        rows = FLIGHT * (last - first)
        block = GROUPS * (last - first)
        position = lax.broadcasted_iota(jnp.int32, (rows, tok), 0)
        picked = None
        for k, target in enumerate(targets(table, z_ref[0, 0], first, last)):
            hit = (position == target).astype(f32).astype(bf16)
            part = jnp.dot(hit, hidden_ref[k], preferred_element_type=f32)
            picked = part if picked is None else picked + part
        for away in range(Z):
            outs[number * Z + away][...] = picked[away * block : (away + 1) * block, :].astype(bf16)


def packed_shapes(chunks, features):
    return [
        jax.ShapeDtypeStruct((GROUPS * (last - first), features), bf16)
        for first, last in chunks
        for _ in range(Z)
    ]


def arrange_kernel(width, *refs):
    ins, out_ref, held = refs[:Z], refs[Z], refs[Z + 1]
    block = GROUPS * width
    rows = Z * block
    for away in range(Z):
        held[away * block : (away + 1) * block, :] = ins[away][...]
    source = lax.broadcasted_iota(jnp.int32, (1, rows), 1)
    away = source // block
    rest = source - away * block
    group = rest // width
    slot = rest - group * width
    place = group * (Z * width) + away * width + slot
    order = (lax.broadcasted_iota(jnp.int32, (rows, rows), 0) == place).astype(f32).astype(bf16)
    moved = jnp.dot(order, held[...], preferred_element_type=f32)
    for group in range(GROUPS):
        piece = moved[group * block : (group + 1) * block, :].astype(bf16)
        out_ref[2 * group] = piece
        out_ref[2 * group + 1] = piece


def arrange(pieces, width):
    block, features = pieces[0].shape
    return pl.pallas_call(
        functools.partial(arrange_kernel, width),
        out_shape=jax.ShapeDtypeStruct((2 * GROUPS, block, features), bf16),
        in_specs=[VMEM] * Z,
        out_specs=VMEM,
        scratch_shapes=[pltpu.VMEM((Z * block, features), bf16)],
        compiler_params=params(32),
        cost_estimate=pl.CostEstimate(
            flops=2 * (Z * block) ** 2 * features, bytes_accessed=6 * Z * block * features, transcendentals=0
        ),
    )(*pieces)


def thirds(value):
    high = value.astype(bf16)
    rest = value - high.astype(f32)
    middle = rest.astype(bf16)
    low = (rest - middle.astype(f32)).astype(bf16)
    return jnp.concatenate([high, middle, low], axis=0)


def added(value, rows):
    return value[:rows] + value[rows : 2 * rows] + value[2 * rows :]


def stats_kernel(norm, tile, count, q_ref, panel_ref, *refs):
    rows, (cov_ref, out_ref), turned = refs[:count], refs[count : count + 2], refs[count + 2 :]
    block = cov_ref.shape[0]
    features = cov_ref.shape[1]
    panel_rows = out_ref.shape[0]
    own = pl.ds(pl.multiple_of(q_ref[0, 0] * block, 128), block)
    for row, turn in zip(rows, turned):
        turn[...] = row[:, own].T
    for start in range(0, features, tile):
        total = None
        for row, turn in zip(rows, turned):
            part = jnp.dot(turn[...], row[:, start : start + tile], preferred_element_type=f32)
            total = part if total is None else total + part
        cov_ref[:, start : start + tile] = total * norm
    pieces = [thirds(panel_ref[quarter]) for quarter in range(OWNERS)]
    result = jnp.zeros(out_ref.shape, f32)
    for row in rows:
        share = jnp.zeros((3 * panel_rows, row.shape[0]), f32)
        for quarter in range(OWNERS):
            share = share + lax.dot_general(
                pieces[quarter],
                row[:, quarter * block : (quarter + 1) * block],
                (((1,), (1,)), ((), ())),
                preferred_element_type=f32,
            )
        turned_panel = thirds(added(share, panel_rows))
        result = result + added(jnp.dot(turned_panel, row[:, own], preferred_element_type=f32), panel_rows)
    out_ref[...] = result * norm


def stats(quarter, panel, rows, norm, tile):
    features = rows[0].shape[1]
    block = features // OWNERS
    total = sum(row.shape[0] for row in rows)
    return pl.pallas_call(
        functools.partial(stats_kernel, norm, tile, len(rows)),
        out_shape=(
            jax.ShapeDtypeStruct((block, features), f32),
            jax.ShapeDtypeStruct((panel.shape[1], block), f32),
        ),
        in_specs=[SMEM, VMEM] + [VMEM] * len(rows),
        out_specs=(VMEM, VMEM),
        scratch_shapes=[pltpu.VMEM((block, row.shape[0]), bf16) for row in rows],
        compiler_params=params(48),
        cost_estimate=pl.CostEstimate(
            flops=2 * total * features * block,
            bytes_accessed=2 * total * features + 4 * features * block,
            transcendentals=0,
        ),
    )(quarter, panel, *rows)


def through_z(pieces):
    out = [pieces[0]]
    for away in range(1, Z):
        out.append(lax.ppermute(pieces[away], "z", [(i, (i + away) % Z) for i in range(Z)]))
    return out


def through_xy(pieces, width):
    placed = arrange(pieces, width)
    mine = lax.all_to_all(placed, ("x", "yh", "yl"), 0, 0, tiled=True)
    mine = mine.reshape(-1, mine.shape[-1])
    other = lax.ppermute(mine, "core", [(0, 1), (1, 0)])
    return mine, other


def per_device(hidden_rows, out_grads, gates, routes, panel_a, panel_g):
    tok, slots, width_in = hidden_rows.shape
    width_out = out_grads.shape[1]
    norm = ROUTED / (tok * 256 * slots)
    routes_t = routes.T
    my_z = lax.axis_index("z").astype(jnp.int32).reshape(1, 1)
    quarter = (lax.axis_index("yl") * 2 + lax.axis_index("core")).astype(jnp.int32).reshape(1, 1)
    packed_g = pl.pallas_call(
        functools.partial(pack_grad_kernel, GRAD_CHUNKS),
        out_shape=packed_shapes(GRAD_CHUNKS, width_out),
        in_specs=[SMEM, VMEM, VMEM, VMEM],
        out_specs=[VMEM] * (Z * len(GRAD_CHUNKS)),
        compiler_params=params(32),
    )(my_z, routes_t, gates.T, out_grads)
    packed_h = pl.pallas_call(
        functools.partial(pack_hidden_kernel, HIDDEN_CHUNKS),
        out_shape=packed_shapes(HIDDEN_CHUNKS, width_in),
        in_specs=[SMEM, VMEM, VMEM],
        out_specs=[VMEM] * (Z * len(HIDDEN_CHUNKS)),
        compiler_params=params(32),
    )(my_z, routes_t, hidden_rows.transpose(1, 0, 2))
    chunks = [
        (list(packed_g[n * Z : (n + 1) * Z]), last - first) for n, (first, last) in enumerate(GRAD_CHUNKS)
    ] + [(list(packed_h[n * Z : (n + 1) * Z]), last - first) for n, (first, last) in enumerate(HIDDEN_CHUNKS)]
    full_a = lax.all_gather(panel_a[0], ("yl", "core"), axis=0)
    full_g = lax.all_gather(panel_g[0], ("yl", "core"), axis=0)
    arrived = []
    for number, (pieces, width) in enumerate(chunks):
        got = through_z(pieces)
        if number + 1 < len(chunks):
            got, later = lax.optimization_barrier((got, chunks[number + 1][0]))
            chunks[number + 1] = (list(later), chunks[number + 1][1])
        arrived.append(through_xy(got, width))
    rows_g = [part for pair in arrived[: len(GRAD_CHUNKS)] for part in pair]
    rows_h = [part for pair in arrived[len(GRAD_CHUNKS) :] for part in pair]
    grad_cov, grad_panel = stats(quarter, full_g, rows_g, norm, 512)
    input_cov, input_panel = stats(quarter, full_a, rows_h, norm, 512)
    return (input_cov[None], grad_cov[None], input_panel[None], grad_panel[None])


def solution(mesh):
    split = Mesh(mesh.devices.reshape(4, 2, 2, 2, Z), AXES)
    return jax.shard_map(
        per_device,
        mesh=split,
        in_specs=(
            P(AXES, None, None),
            P(AXES, None),
            P(AXES, None),
            P(AXES, None),
            P(AXES, None, None),
            P(AXES, None, None),
        ),
        out_specs=(P(AXES, None, None),) * 4,
        check_vma=False,
    )
```

time: 582 us -> 216 us (0.37)
  waiting for transfers between devices: 280 us -> 79.7 us
  blocking collectives: 149 us -> 11.9 us
  local copies, waits for them, and re-layouts: 87.7 us -> 4.16 us
  starting transfers between devices: 12.4 us -> 85.1 us
  Pallas kernels: 0 us -> 33.1 us
  other arithmetic: 29.2 us -> 0 us
  matrix products: 21.3 us -> 0 us
    all_to_all x1 -> x3, waiting for transfers between devices: 277 us -> 37.4 us  [through_xy(): mine = lax.all_to_all(placed, ('x', 'yh', 'yl'), 0, 0, tiled=True)]
    all_to_all x1 -> x0, blocking collectives: 149 us -> none  [per_device(): lax.all_to_all(copies, 'dp', split_axis=0, concat_axis=0, tiled=True)]
    ppermute x4 -> x24, starting transfers between devices: 4.17 us -> 65.8 us  [the longest x21 54.2 us: through_z(): lax.ppermute(pieces[away], 'z', [(i, (i + away) % Z) for i in range(Z)])]
    ppermute x4 -> x24, waiting for transfers between devices: 2.96 us -> 42.3 us  [the longest x21 42.3 us: through_z(): lax.ppermute(pieces[away], 'z', [(i, (i + away) % Z) for i in range(Z)])]
    pallas_call x0 -> x7, Pallas kernels: none -> 33.1 us  [the longest x2 24.5 us: stats(): pl.pallas_call(functools.partial(stats_kernel, norm, tile, len(rows)), ou...]
    all_to_all x2 -> x0, local copies, waits for them, and re-layouts: 31.3 us -> none  [the longest x1 17.5 us: per_device(): lax.all_to_all(copies, 'dp', split_axis=0, concat_axis=0, tiled=True)]
    reshape x6 -> x0, local copies, waits for them, and re-layouts: 28.2 us -> none  [the longest x1 18.8 us: per_device(): gathered = arrived.reshape(-1, features)]
    dot_general x4 -> x0, matrix products: 21.3 us -> none  [the longest x1 9.33 us: per_device(): lax.dot_general(rows_out, gathered[:, width_in:], contract, preferred_ele...]
  transfers between devices with their start and end apart: 5 -> 27, of which waited for: 3 -> 13; matrix products, arithmetic and copies ran while one was open for 1% -> 0% of each run, Pallas kernels for 0% -> 7%
where the time goes in v1:
time: 216 us; the launch traced here: 215 us
  starting transfers between devices  85.1 us (39%)
  waiting for transfers between devices  79.7 us (37%)
  Pallas kernels  33.1 us (15%)
  blocking collectives  11.9 us (6%)
  local copies, waits for them, and re-layouts  4.16 us (2%)
    ppermute x21, starting transfers between devices, through_z(): lax.ppermute(pieces[away], 'z', [(i, (i + away) % Z) for i in range(Z)])  54.2 us
    ppermute x21, waiting for transfers between devices, through_z(): lax.ppermute(pieces[away], 'z', [(i, (i + away) % Z) for i in range(Z)])  42.3 us
    all_to_all x3, waiting for transfers between devices, through_xy(): mine = lax.all_to_all(placed, ('x', 'yh', 'yl'), 0, 0, tiled=True)  37.4 us
    pallas_call x2, Pallas kernels, stats(): pl.pallas_call(functools.partial(stats_kernel, norm, tile, len(rows)), ou...  24.5 us
    all_to_all x3, starting transfers between devices, through_xy(): mine = lax.all_to_all(placed, ('x', 'yh', 'yl'), 0, 0, tiled=True)  19.3 us
    ppermute x3, starting transfers between devices, through_xy(): other = lax.ppermute(mine, 'core', [(0, 1), (1, 0)])  11.6 us
    all_gather x1, blocking collectives, per_device(): full_g = lax.all_gather(panel_g[0], ('yl', 'core'), axis=0)  6.43 us
    pallas_call x3, Pallas kernels, arrange(): pl.pallas_call(functools.partial(arrange_kernel, width), out_shape=jax.Sh...  5.56 us
  transfers between devices with their start and end apart: 27, of which 13 were waited for; matrix products, arithmetic and copies ran while one was open for 0% of the time, Pallas kernels for 7%

profile of v1, /device:TPU:1, one launch (start us, length us, event | category | flops | bytes accessed | tf_op | source)
XLA Modules:
  0.0 214.8 jit_solution(14824296673634649736)
XLA Ops:
  4.0 2.5 %collective-permute-start = (bf16[16,2560]{1,0:T(8,128)(2,1)S(1)}, bf16[16,2560]{1,0:T(8,128)(2,1)S(1)}, u32[]{:S(2)}, u32[]{:S(2)}) collective-permute-start(bf16[16,2560]{1,0:T(8,128)(2,1)S(1)} %get-tuple-element.65), channel_id=1, source_target_pairs={{0,1},{1,2},{2,3},{3,4},{4,5},{5,6},{6,7},{7,0},{8,9},{9,10},{10,1... | collective-permute-start | bytes 245768 | tf_op jit(solution)/shard_map/ppermute | solution.py:207
  6.5 3.0 %collective-permute-start.1 = (bf16[16,2560]{1,0:T(8,128)(2,1)S(1)}, bf16[16,2560]{1,0:T(8,128)(2,1)S(1)}, u32[]{:S(2)}, u32[]{:S(2)}) collective-permute-start(bf16[16,2560]{1,0:T(8,128)(2,1)S(1)} %get-tuple-element.66), channel_id=1, source_target_pairs={{0,2},{1,3},{2,4},{3,5},{4,6},{5,7},{6,0},{7,1},{8,10},{9,11},{10,... | collective-permute-start | bytes 245768 | tf_op jit(solution)/shard_map/ppermute | solution.py:207
  9.5 3.8 %collective-permute-start.2 = (bf16[16,2560]{1,0:T(8,128)(2,1)S(1)}, bf16[16,2560]{1,0:T(8,128)(2,1)S(1)}, u32[]{:S(2)}, u32[]{:S(2)}) collective-permute-start(bf16[16,2560]{1,0:T(8,128)(2,1)S(1)} %get-tuple-element.67), channel_id=1, source_target_pairs={{0,3},{1,4},{2,5},{3,6},{4,7},{5,0},{6,1},{7,2},{8,11},{9,12},{10,... | collective-permute-start | bytes 245768 | tf_op jit(solution)/shard_map/ppermute | solution.py:207
  13.7 4.5 %collective-permute-start.4 = (bf16[16,2560]{1,0:T(8,128)(2,1)S(1)}, bf16[16,2560]{1,0:T(8,128)(2,1)S(1)}, u32[]{:S(2)}, u32[]{:S(2)}) collective-permute-start(bf16[16,2560]{1,0:T(8,128)(2,1)S(1)} %get-tuple-element.69), channel_id=1, source_target_pairs={{0,5},{1,6},{2,7},{3,0},{4,1},{5,2},{6,3},{7,4},{8,13},{9,14},{10,... | collective-permute-start | bytes 245768 | tf_op jit(solution)/shard_map/ppermute | solution.py:207
  18.2 2.4 %collective-permute-start.5 = (bf16[16,2560]{1,0:T(8,128)(2,1)S(1)}, bf16[16,2560]{1,0:T(8,128)(2,1)S(1)}, u32[]{:S(2)}, u32[]{:S(2)}) collective-permute-start(bf16[16,2560]{1,0:T(8,128)(2,1)S(1)} %get-tuple-element.70), channel_id=1, source_target_pairs={{0,6},{1,7},{2,0},{3,1},{4,2},{5,3},{6,4},{7,5},{8,14},{9,15},{10,... | collective-permute-start | bytes 245768 | tf_op jit(solution)/shard_map/ppermute | solution.py:207
  21.3 2.8 %collective-permute-done.3.refs_4_ = bf16[16,2560]{1,0:T(8,128)(2,1)S(1)} collective-permute-done((bf16[16,2560]{1,0:T(8,128)(2,1)S(1)}, bf16[16,2560]{1,0:T(8,128)(2,1)S(1)}, u32[]{:S(2)}, u32[]{:S(2)}) %collective-permute-start.3) | collective-permute-done | bytes 81952 | tf_op jit(solution)/shard_map/ppermute | solution.py:207
  24.1 6.6 %collective-permute-done.5.refs_6_ = bf16[16,2560]{1,0:T(8,128)(2,1)S(1)} collective-permute-done((bf16[16,2560]{1,0:T(8,128)(2,1)S(1)}, bf16[16,2560]{1,0:T(8,128)(2,1)S(1)}, u32[]{:S(2)}, u32[]{:S(2)}) %collective-permute-start.5) | collective-permute-done | bytes 81952 | tf_op jit(solution)/shard_map/ppermute | solution.py:207
  31.2 2.7 %collective-permute-start.10 = (bf16[32,2560]{1,0:T(8,128)(2,1)S(1)}, bf16[32,2560]{1,0:T(8,128)(2,1)S(1)}, u32[]{:S(2)}, u32[]{:S(2)}) collective-permute-start(bf16[32,2560]{1,0:T(8,128)(2,1)S(1)} %get-tuple-element.84), channel_id=1, source_target_pairs={{0,4},{1,5},{2,6},{3,7},{4,0},{5,1},{6,2},{7,3},{8,12},{9,13},{10,... | collective-permute-start | bytes 491528 | tf_op jit(solution)/shard_map/ppermute | solution.py:207
  33.9 4.0 %collective-permute-start.11 = (bf16[32,2560]{1,0:T(8,128)(2,1)S(1)}, bf16[32,2560]{1,0:T(8,128)(2,1)S(1)}, u32[]{:S(2)}, u32[]{:S(2)}) collective-permute-start(bf16[32,2560]{1,0:T(8,128)(2,1)S(1)} %get-tuple-element.85), channel_id=1, source_target_pairs={{0,5},{1,6},{2,7},{3,0},{4,1},{5,2},{6,3},{7,4},{8,13},{9,14},{10,... | collective-permute-start | bytes 491528 | tf_op jit(solution)/shard_map/ppermute | solution.py:207
  41.5 3.1 %collective-permute-start.8 = (bf16[32,2560]{1,0:T(8,128)(2,1)S(1)}, bf16[32,2560]{1,0:T(8,128)(2,1)S(1)}, u32[]{:S(2)}, u32[]{:S(2)}) collective-permute-start(bf16[32,2560]{1,0:T(8,128)(2,1)S(1)} %get-tuple-element.82), channel_id=1, source_target_pairs={{0,2},{1,3},{2,4},{3,5},{4,6},{5,7},{6,0},{7,1},{8,10},{9,11},{10,... | collective-permute-start | bytes 491528 | tf_op jit(solution)/shard_map/ppermute | solution.py:207
  44.6 5.6 %collective-permute-done.11.refs_5_ = bf16[32,2560]{1,0:T(8,128)(2,1)S(1)} collective-permute-done((bf16[32,2560]{1,0:T(8,128)(2,1)S(1)}, bf16[32,2560]{1,0:T(8,128)(2,1)S(1)}, u32[]{:S(2)}, u32[]{:S(2)}) %collective-permute-start.11) | collective-permute-done | bytes 163872 | tf_op jit(solution)/shard_map/ppermute | solution.py:207
  50.2 8.3 %collective-permute-start.9 = (bf16[32,2560]{1,0:T(8,128)(2,1)S(1)}, bf16[32,2560]{1,0:T(8,128)(2,1)S(1)}, u32[]{:S(2)}, u32[]{:S(2)}) collective-permute-start(bf16[32,2560]{1,0:T(8,128)(2,1)S(1)} %get-tuple-element.83), channel_id=1, source_target_pairs={{0,3},{1,4},{2,5},{3,6},{4,7},{5,0},{6,1},{7,2},{8,11},{9,12},{10,... | collective-permute-start | bytes 491528 | tf_op jit(solution)/shard_map/ppermute | solution.py:207
  62.6 3.1 %collective-permute-done.9.refs_3_ = bf16[32,2560]{1,0:T(8,128)(2,1)S(1)} collective-permute-done((bf16[32,2560]{1,0:T(8,128)(2,1)S(1)}, bf16[32,2560]{1,0:T(8,128)(2,1)S(1)}, u32[]{:S(2)}, u32[]{:S(2)}) %collective-permute-start.9) | collective-permute-done | bytes 163872 | tf_op jit(solution)/shard_map/ppermute | solution.py:207
  67.8 6.8 %all-to-all-start.2 = ((bf16[16,32,2560]{2,1,0:T(8,128)(2,1)}), bf16[16,32,2560]{2,1,0:T(8,128)(2,1)S(1)}, u32[]{:S(2)}, u32[]{:S(2)}) async-start(bf16[16,32,2560]{2,1,0:T(8,128)(2,1)} %shard_map.98), calls=%async_computation.2 | async-start | bytes 5242880 | tf_op jit(solution)/shard_map/all_to_all | solution.py:213
  74.5 3.9 %collective-permute-start.14 = (bf16[48,1536]{1,0:T(8,128)(2,1)}, bf16[48,1536]{1,0:T(8,128)(2,1)S(1)}, u32[]{:S(2)}, u32[]{:S(2)}) collective-permute-start(bf16[48,1536]{1,0:T(8,128)(2,1)} %copy-done.10), channel_id=1, source_target_pairs={{0,1},{1,2},{2,3},{3,4},{4,5},{5,6},{6,7},{7,0},{8,9},{9,10},{10,1... | collective-permute-start | bytes 442376 | tf_op jit(solution)/shard_map/ppermute | solution.py:207
  78.4 3.5 %collective-permute-start.15 = (bf16[48,1536]{1,0:T(8,128)(2,1)}, bf16[48,1536]{1,0:T(8,128)(2,1)S(1)}, u32[]{:S(2)}, u32[]{:S(2)}) collective-permute-start(bf16[48,1536]{1,0:T(8,128)(2,1)} %copy-done.9), channel_id=1, source_target_pairs={{0,2},{1,3},{2,4},{3,5},{4,6},{5,7},{6,0},{7,1},{8,10},{9,11},{10,... | collective-permute-start | bytes 442376 | tf_op jit(solution)/shard_map/ppermute | solution.py:207
  83.9 3.7 %collective-permute-start.18 = (bf16[48,1536]{1,0:T(8,128)(2,1)}, bf16[48,1536]{1,0:T(8,128)(2,1)S(1)}, u32[]{:S(2)}, u32[]{:S(2)}) collective-permute-start(bf16[48,1536]{1,0:T(8,128)(2,1)} %copy-done.6), channel_id=1, source_target_pairs={{0,5},{1,6},{2,7},{3,0},{4,1},{5,2},{6,3},{7,4},{8,13},{9,14},{10,... | collective-permute-start | bytes 442376 | tf_op jit(solution)/shard_map/ppermute | solution.py:207
  91.0 4.8 %collective-permute-done.16.refs_3_ = bf16[48,1536]{1,0:T(8,128)(2,1)S(1)} collective-permute-done((bf16[48,1536]{1,0:T(8,128)(2,1)}, bf16[48,1536]{1,0:T(8,128)(2,1)S(1)}, u32[]{:S(2)}, u32[]{:S(2)}) %collective-permute-start.16) | collective-permute-done | bytes 147488 | tf_op jit(solution)/shard_map/ppermute | solution.py:207
  95.7 6.1 %collective-permute-done.17.refs_4_ = bf16[48,1536]{1,0:T(8,128)(2,1)S(1)} collective-permute-done((bf16[48,1536]{1,0:T(8,128)(2,1)}, bf16[48,1536]{1,0:T(8,128)(2,1)S(1)}, u32[]{:S(2)}, u32[]{:S(2)}) %collective-permute-start.17) | collective-permute-done | bytes 147488 | tf_op jit(solution)/shard_map/ppermute | solution.py:207
  101.8 8.5 %collective-permute-done.19.refs_6_ = bf16[48,1536]{1,0:T(8,128)(2,1)S(1)} collective-permute-done((bf16[48,1536]{1,0:T(8,128)(2,1)}, bf16[48,1536]{1,0:T(8,128)(2,1)S(1)}, u32[]{:S(2)}, u32[]{:S(2)}) %collective-permute-start.19) | collective-permute-done | bytes 147488 | tf_op jit(solution)/shard_map/ppermute | solution.py:207
  110.4 2.9 %collective-permute-done.20.refs_7_ = bf16[48,1536]{1,0:T(8,128)(2,1)S(1)} collective-permute-done((bf16[48,1536]{1,0:T(8,128)(2,1)}, bf16[48,1536]{1,0:T(8,128)(2,1)S(1)}, u32[]{:S(2)}, u32[]{:S(2)}) %collective-permute-start.20) | collective-permute-done | bytes 147488 | tf_op jit(solution)/shard_map/ppermute | solution.py:207
  113.2 2.2 %shard_map.95 = bf16[16,48,1536]{2,1,0:T(8,128)(2,1)} custom-call(bf16[48,1536]{1,0:T(8,128)(2,1)S(1)} %get-tuple-element.96.refs_0_, bf16[48,1536]{1,0:T(8,128)(2,1)S(1)} %collective-permute-done.14.refs_1_, bf16[48,1536]{1,0:T(8,128)(2,1)S(1)} %collective-permute-done.15.refs_2_, bf16[48,1536]{1,0:T(8,128)(2,1)S(1)} %collective-permute-done.16.refs_3_, ...), custom_call_target="tpu_custom_call" | custom-call | flops 452984832 | bytes 3538944 | tf_op jit(solution)/shard_map/pallas_call | solution.py:127
  115.4 6.6 %all-to-all-start = ((bf16[16,48,1536]{2,1,0:T(8,128)(2,1)}), bf16[16,48,1536]{2,1,0:T(8,128)(2,1)}, u32[]{:S(2)}, u32[]{:S(2)}) async-start(bf16[16,48,1536]{2,1,0:T(8,128)(2,1)} %shard_map.95), calls=%async_computation | async-start | bytes 4718592 | tf_op jit(solution)/shard_map/all_to_all | solution.py:213
  125.1 25.6 %all-to-all-done = bf16[16,48,1536]{2,1,0:T(8,128)(2,1)} async-done(((bf16[16,48,1536]{2,1,0:T(8,128)(2,1)}), bf16[16,48,1536]{2,1,0:T(8,128)(2,1)}, u32[]{:S(2)}, u32[]{:S(2)}) %all-to-all-start) | async-done | bytes 2359328 | tf_op jit(solution)/shard_map/all_to_all | solution.py:213
  150.6 5.9 %all-to-all-start.1 = ((bf16[16,16,2560]{2,1,0:T(8,128)(2,1)}), bf16[16,16,2560]{2,1,0:T(8,128)(2,1)}, u32[]{:S(2)}, u32[]{:S(2)}) async-start(bf16[16,16,2560]{2,1,0:T(8,128)(2,1)} %shard_map.97), calls=%async_computation.1 | async-start | bytes 2621440 | tf_op jit(solution)/shard_map/all_to_all | solution.py:213
  156.5 4.2 %collective-permute-start.21 = (bf16[768,1536]{1,0:T(8,128)(2,1)}, bf16[768,1536]{1,0:T(8,128)(2,1)}, u32[]{:S(2)}, u32[]{:S(2)}) collective-permute-start(bf16[768,1536]{1,0:T(8,128)(2,1)} %bitcast.5.refs_0_), channel_id=1, source_target_pairs={{0,8},{8,0},{1,9},{9,1},{2,10},{10,2},{3,11},{11,3},{4,12},{12,4},... | collective-permute-start | bytes 7077896 | tf_op jit(solution)/shard_map/ppermute | solution.py:215
  160.7 11.8 %all-to-all-done.1 = bf16[16,16,2560]{2,1,0:T(8,128)(2,1)} async-done(((bf16[16,16,2560]{2,1,0:T(8,128)(2,1)}), bf16[16,16,2560]{2,1,0:T(8,128)(2,1)}, u32[]{:S(2)}, u32[]{:S(2)}) %all-to-all-start.1) | async-done | bytes 1310752 | tf_op jit(solution)/shard_map/all_to_all | solution.py:213
  172.6 5.8 %collective-permute-start.22 = (bf16[256,2560]{1,0:T(8,128)(2,1)}, bf16[256,2560]{1,0:T(8,128)(2,1)}, u32[]{:S(2)}, u32[]{:S(2)}) collective-permute-start(bf16[256,2560]{1,0:T(8,128)(2,1)} %bitcast.7.refs_0_), channel_id=1, source_target_pairs={{0,8},{8,0},{1,9},{9,1},{2,10},{10,2},{3,11},{11,3},{4,12},{12,4},... | collective-permute-start | bytes 3932168 | tf_op jit(solution)/shard_map/ppermute | solution.py:215
  178.3 5.5 %all_gather.6.panel_ref = f32[4,32,384]{2,1,0:T(8,128)S(1)} all-gather(f32[1,32,384]{2,1,0:T(8,128)S(1)} %copy-done.12), channel_id=1, replica_groups=mesh['x'=4,'yh'=2,'yl'=2,'core'=2,'z'=8] {'yl','core'}, dimensions={0}, use_global_device_ids=true | all-gather | bytes 245760 | tf_op jit(solution)/shard_map/all_gather | solution.py:243
  183.8 6.4 %all_gather.7.panel_ref = f32[4,32,640]{2,1,0:T(8,128)S(1)} all-gather(f32[1,32,640]{2,1,0:T(8,128)S(1)} %copy-done.11), channel_id=1, replica_groups=mesh['x'=4,'yh'=2,'yl'=2,'core'=2,'z'=8] {'yl','core'}, dimensions={0}, use_global_device_ids=true | all-gather | bytes 409600 | tf_op jit(solution)/shard_map/all_gather | solution.py:244
  190.2 8.6 %shard_map.96 = (f32[384,1536]{1,0:T(8,128)}, f32[32,384]{1,0:T(8,128)}) custom-call(s32[1,1]{1,0:T(1,128)} %bitcast.q_ref, f32[4,32,384]{2,1,0:T(8,128)S(1)} %all_gather.6.panel_ref, bf16[768,1536]{1,0:T(8,128)(2,1)} %bitcast.5.refs_0_, bf16[768,1536]{1,0:T(8,128)(2,1)} %collective-permute-done.21.refs_1_), custom_call_target="tpu_custom_call" | custom-call | flops 1811939328 | bytes 7077888 | tf_op jit(solution)/shard_map/pallas_call | solution.py:186
  198.9 15.9 %shard_map.99 = (f32[640,2560]{1,0:T(8,128)}, f32[32,640]{1,0:T(8,128)}) custom-call(s32[1,1]{1,0:T(1,128)} %bitcast.q_ref, f32[4,32,640]{2,1,0:T(8,128)S(1)} %all_gather.7.panel_ref, bf16[256,2560]{1,0:T(8,128)(2,1)} %bitcast.7.refs_0_, bf16[256,2560]{1,0:T(8,128)(2,1)} %collective-permute-done.22.refs_1_, bf16[512,2560]{1,0:T(8,128)(2,1)S(1)} %bitcast.13, ...), custom_call_target="tpu_custom_call" | custom-call | flops 5033164800 | bytes 14417920 | tf_op jit(solution)/shard_map/pallas_call | solution.py:186
  (57 shorter events, 23.0 us)
Async XLA Ops:
  4.0 14.2 %collective-permute-start = (bf16[16,2560]{1,0:T(8,128)(2,1)S(1)}, bf16[16,2560]{1,0:T(8,128)(2,1)S(1)}, u32[]{:S(2)}, u32[]{:S(2)}) collective-permute-start(bf16[16,2560]{1,0:T(8,128)(2,1)S(1)} %get-tuple-element.65), channel_id=1, source_target_pairs={{0,1},{1,2},{2,3},{3,4},{4,5},{5,6},{6,7},{7,0},{8,9},{9,10},{10,1... | collective-permute-start | bytes 245768 | tf_op jit(solution)/shard_map/ppermute | solution.py:207
  6.5 14.1 %collective-permute-start.1 = (bf16[16,2560]{1,0:T(8,128)(2,1)S(1)}, bf16[16,2560]{1,0:T(8,128)(2,1)S(1)}, u32[]{:S(2)}, u32[]{:S(2)}) collective-permute-start(bf16[16,2560]{1,0:T(8,128)(2,1)S(1)} %get-tuple-element.66), channel_id=1, source_target_pairs={{0,2},{1,3},{2,4},{3,5},{4,6},{5,7},{6,0},{7,1},{8,10},{9,11},{10,... | collective-permute-start | bytes 245768 | tf_op jit(solution)/shard_map/ppermute | solution.py:207
  9.5 11.8 %collective-permute-start.2 = (bf16[16,2560]{1,0:T(8,128)(2,1)S(1)}, bf16[16,2560]{1,0:T(8,128)(2,1)S(1)}, u32[]{:S(2)}, u32[]{:S(2)}) collective-permute-start(bf16[16,2560]{1,0:T(8,128)(2,1)S(1)} %get-tuple-element.67), channel_id=1, source_target_pairs={{0,3},{1,4},{2,5},{3,6},{4,7},{5,0},{6,1},{7,2},{8,11},{9,12},{10,... | collective-permute-start | bytes 245768 | tf_op jit(solution)/shard_map/ppermute | solution.py:207
  13.3 10.8 %collective-permute-start.3 = (bf16[16,2560]{1,0:T(8,128)(2,1)S(1)}, bf16[16,2560]{1,0:T(8,128)(2,1)S(1)}, u32[]{:S(2)}, u32[]{:S(2)}) collective-permute-start(bf16[16,2560]{1,0:T(8,128)(2,1)S(1)} %get-tuple-element.68), channel_id=1, source_target_pairs={{0,4},{1,5},{2,6},{3,7},{4,0},{5,1},{6,2},{7,3},{8,12},{9,13},{10,... | collective-permute-start | bytes 245768 | tf_op jit(solution)/shard_map/ppermute | solution.py:207
  13.7 10.4 %collective-permute-start.4 = (bf16[16,2560]{1,0:T(8,128)(2,1)S(1)}, bf16[16,2560]{1,0:T(8,128)(2,1)S(1)}, u32[]{:S(2)}, u32[]{:S(2)}) collective-permute-start(bf16[16,2560]{1,0:T(8,128)(2,1)S(1)} %get-tuple-element.69), channel_id=1, source_target_pairs={{0,5},{1,6},{2,7},{3,0},{4,1},{5,2},{6,3},{7,4},{8,13},{9,14},{10,... | collective-permute-start | bytes 245768 | tf_op jit(solution)/shard_map/ppermute | solution.py:207
  18.2 12.5 %collective-permute-start.5 = (bf16[16,2560]{1,0:T(8,128)(2,1)S(1)}, bf16[16,2560]{1,0:T(8,128)(2,1)S(1)}, u32[]{:S(2)}, u32[]{:S(2)}) collective-permute-start(bf16[16,2560]{1,0:T(8,128)(2,1)S(1)} %get-tuple-element.70), channel_id=1, source_target_pairs={{0,6},{1,7},{2,0},{3,1},{4,2},{5,3},{6,4},{7,5},{8,14},{9,15},{10,... | collective-permute-start | bytes 245768 | tf_op jit(solution)/shard_map/ppermute | solution.py:207
  20.6 10.6 %collective-permute-start.6 = (bf16[16,2560]{1,0:T(8,128)(2,1)S(1)}, bf16[16,2560]{1,0:T(8,128)(2,1)S(1)}, u32[]{:S(2)}, u32[]{:S(2)}) collective-permute-start(bf16[16,2560]{1,0:T(8,128)(2,1)S(1)} %get-tuple-element.71), channel_id=1, source_target_pairs={{0,7},{1,0},{2,1},{3,2},{4,3},{5,4},{6,5},{7,6},{8,15},{9,8},{10,9... | collective-permute-start | bytes 245768 | tf_op jit(solution)/shard_map/ppermute | solution.py:207
  31.2 10.3 %collective-permute-start.10 = (bf16[32,2560]{1,0:T(8,128)(2,1)S(1)}, bf16[32,2560]{1,0:T(8,128)(2,1)S(1)}, u32[]{:S(2)}, u32[]{:S(2)}) collective-permute-start(bf16[32,2560]{1,0:T(8,128)(2,1)S(1)} %get-tuple-element.84), channel_id=1, source_target_pairs={{0,4},{1,5},{2,6},{3,7},{4,0},{5,1},{6,2},{7,3},{8,12},{9,13},{10,... | collective-permute-start | bytes 491528 | tf_op jit(solution)/shard_map/ppermute | solution.py:207
  33.9 16.3 %collective-permute-start.11 = (bf16[32,2560]{1,0:T(8,128)(2,1)S(1)}, bf16[32,2560]{1,0:T(8,128)(2,1)S(1)}, u32[]{:S(2)}, u32[]{:S(2)}) collective-permute-start(bf16[32,2560]{1,0:T(8,128)(2,1)S(1)} %get-tuple-element.85), channel_id=1, source_target_pairs={{0,5},{1,6},{2,7},{3,0},{4,1},{5,2},{6,3},{7,4},{8,13},{9,14},{10,... | collective-permute-start | bytes 491528 | tf_op jit(solution)/shard_map/ppermute | solution.py:207
  37.9 24.5 %collective-permute-start.12 = (bf16[32,2560]{1,0:T(8,128)(2,1)S(1)}, bf16[32,2560]{1,0:T(8,128)(2,1)S(1)}, u32[]{:S(2)}, u32[]{:S(2)}) collective-permute-start(bf16[32,2560]{1,0:T(8,128)(2,1)S(1)} %get-tuple-element.86), channel_id=1, source_target_pairs={{0,6},{1,7},{2,0},{3,1},{4,2},{5,3},{6,4},{7,5},{8,14},{9,15},{10,... | collective-permute-start | bytes 491528 | tf_op jit(solution)/shard_map/ppermute | solution.py:207
  38.8 23.8 %collective-permute-start.13 = (bf16[32,2560]{1,0:T(8,128)(2,1)S(1)}, bf16[32,2560]{1,0:T(8,128)(2,1)S(1)}, u32[]{:S(2)}, u32[]{:S(2)}) collective-permute-start(bf16[32,2560]{1,0:T(8,128)(2,1)S(1)} %get-tuple-element.87), channel_id=1, source_target_pairs={{0,7},{1,0},{2,1},{3,2},{4,3},{5,4},{6,5},{7,6},{8,15},{9,8},{10,9... | collective-permute-start | bytes 491528 | tf_op jit(solution)/shard_map/ppermute | solution.py:207
  38.8 23.8 %collective-permute-start.7 = (bf16[32,2560]{1,0:T(8,128)(2,1)S(1)}, bf16[32,2560]{1,0:T(8,128)(2,1)S(1)}, u32[]{:S(2)}, u32[]{:S(2)}) collective-permute-start(bf16[32,2560]{1,0:T(8,128)(2,1)S(1)} %get-tuple-element.81), channel_id=1, source_target_pairs={{0,1},{1,2},{2,3},{3,4},{4,5},{5,6},{6,7},{7,0},{8,9},{9,10},{10,1... | collective-permute-start | bytes 491528 | tf_op jit(solution)/shard_map/ppermute | solution.py:207
  41.5 21.1 %collective-permute-start.8 = (bf16[32,2560]{1,0:T(8,128)(2,1)S(1)}, bf16[32,2560]{1,0:T(8,128)(2,1)S(1)}, u32[]{:S(2)}, u32[]{:S(2)}) collective-permute-start(bf16[32,2560]{1,0:T(8,128)(2,1)S(1)} %get-tuple-element.82), channel_id=1, source_target_pairs={{0,2},{1,3},{2,4},{3,5},{4,6},{5,7},{6,0},{7,1},{8,10},{9,11},{10,... | collective-permute-start | bytes 491528 | tf_op jit(solution)/shard_map/ppermute | solution.py:207
  50.2 15.6 %collective-permute-start.9 = (bf16[32,2560]{1,0:T(8,128)(2,1)S(1)}, bf16[32,2560]{1,0:T(8,128)(2,1)S(1)}, u32[]{:S(2)}, u32[]{:S(2)}) collective-permute-start(bf16[32,2560]{1,0:T(8,128)(2,1)S(1)} %get-tuple-element.83), channel_id=1, source_target_pairs={{0,3},{1,4},{2,5},{3,6},{4,7},{5,0},{6,1},{7,2},{8,11},{9,12},{10,... | collective-permute-start | bytes 491528 | tf_op jit(solution)/shard_map/ppermute | solution.py:207
  62.3 5.5 %copy-start.4 = (bf16[48,1536]{1,0:T(8,128)(2,1)}, bf16[48,1536]{1,0:T(8,128)(2,1)S(1)}, u32[]{:S(2)}) copy-start(bf16[48,1536]{1,0:T(8,128)(2,1)S(1)} %get-tuple-element.103) | copy-start | bytes 442372
  62.3 5.4 %copy-start.5 = (bf16[48,1536]{1,0:T(8,128)(2,1)}, bf16[48,1536]{1,0:T(8,128)(2,1)S(1)}, u32[]{:S(2)}) copy-start(bf16[48,1536]{1,0:T(8,128)(2,1)S(1)} %get-tuple-element.102) | copy-start | bytes 442372
  62.3 5.4 %copy-start.6 = (bf16[48,1536]{1,0:T(8,128)(2,1)}, bf16[48,1536]{1,0:T(8,128)(2,1)S(1)}, u32[]{:S(2)}) copy-start(bf16[48,1536]{1,0:T(8,128)(2,1)S(1)} %get-tuple-element.101) | copy-start | bytes 442372
  67.8 47.7 %all-to-all-start.2 = ((bf16[16,32,2560]{2,1,0:T(8,128)(2,1)}), bf16[16,32,2560]{2,1,0:T(8,128)(2,1)S(1)}, u32[]{:S(2)}, u32[]{:S(2)}) async-start(bf16[16,32,2560]{2,1,0:T(8,128)(2,1)} %shard_map.98), calls=%async_computation.2 | async-start | bytes 5242880 | tf_op jit(solution)/shard_map/all_to_all | solution.py:213
  74.5 13.1 %collective-permute-start.14 = (bf16[48,1536]{1,0:T(8,128)(2,1)}, bf16[48,1536]{1,0:T(8,128)(2,1)S(1)}, u32[]{:S(2)}, u32[]{:S(2)}) collective-permute-start(bf16[48,1536]{1,0:T(8,128)(2,1)} %copy-done.10), channel_id=1, source_target_pairs={{0,1},{1,2},{2,3},{3,4},{4,5},{5,6},{6,7},{7,0},{8,9},{9,10},{10,1... | collective-permute-start | bytes 442376 | tf_op jit(solution)/shard_map/ppermute | solution.py:207
  78.4 11.3 %collective-permute-start.15 = (bf16[48,1536]{1,0:T(8,128)(2,1)}, bf16[48,1536]{1,0:T(8,128)(2,1)S(1)}, u32[]{:S(2)}, u32[]{:S(2)}) collective-permute-start(bf16[48,1536]{1,0:T(8,128)(2,1)} %copy-done.9), channel_id=1, source_target_pairs={{0,2},{1,3},{2,4},{3,5},{4,6},{5,7},{6,0},{7,1},{8,10},{9,11},{10,... | collective-permute-start | bytes 442376 | tf_op jit(solution)/shard_map/ppermute | solution.py:207
  81.9 13.8 %collective-permute-start.16 = (bf16[48,1536]{1,0:T(8,128)(2,1)}, bf16[48,1536]{1,0:T(8,128)(2,1)S(1)}, u32[]{:S(2)}, u32[]{:S(2)}) collective-permute-start(bf16[48,1536]{1,0:T(8,128)(2,1)} %copy-done.8), channel_id=1, source_target_pairs={{0,3},{1,4},{2,5},{3,6},{4,7},{5,0},{6,1},{7,2},{8,11},{9,12},{10,... | collective-permute-start | bytes 442376 | tf_op jit(solution)/shard_map/ppermute | solution.py:207
  81.9 19.9 %collective-permute-start.17 = (bf16[48,1536]{1,0:T(8,128)(2,1)}, bf16[48,1536]{1,0:T(8,128)(2,1)S(1)}, u32[]{:S(2)}, u32[]{:S(2)}) collective-permute-start(bf16[48,1536]{1,0:T(8,128)(2,1)} %copy-done.7), channel_id=1, source_target_pairs={{0,4},{1,5},{2,6},{3,7},{4,0},{5,1},{6,2},{7,3},{8,12},{9,13},{10,... | collective-permute-start | bytes 442376 | tf_op jit(solution)/shard_map/ppermute | solution.py:207
  83.9 18.0 %collective-permute-start.18 = (bf16[48,1536]{1,0:T(8,128)(2,1)}, bf16[48,1536]{1,0:T(8,128)(2,1)S(1)}, u32[]{:S(2)}, u32[]{:S(2)}) collective-permute-start(bf16[48,1536]{1,0:T(8,128)(2,1)} %copy-done.6), channel_id=1, source_target_pairs={{0,5},{1,6},{2,7},{3,0},{4,1},{5,2},{6,3},{7,4},{8,13},{9,14},{10,... | collective-permute-start | bytes 442376 | tf_op jit(solution)/shard_map/ppermute | solution.py:207
  87.6 22.8 %collective-permute-start.19 = (bf16[48,1536]{1,0:T(8,128)(2,1)}, bf16[48,1536]{1,0:T(8,128)(2,1)S(1)}, u32[]{:S(2)}, u32[]{:S(2)}) collective-permute-start(bf16[48,1536]{1,0:T(8,128)(2,1)} %copy-done.5), channel_id=1, source_target_pairs={{0,6},{1,7},{2,0},{3,1},{4,2},{5,3},{6,4},{7,5},{8,14},{9,15},{10,... | collective-permute-start | bytes 442376 | tf_op jit(solution)/shard_map/ppermute | solution.py:207
  89.7 23.5 %collective-permute-start.20 = (bf16[48,1536]{1,0:T(8,128)(2,1)}, bf16[48,1536]{1,0:T(8,128)(2,1)S(1)}, u32[]{:S(2)}, u32[]{:S(2)}) collective-permute-start(bf16[48,1536]{1,0:T(8,128)(2,1)} %copy-done.4), channel_id=1, source_target_pairs={{0,7},{1,0},{2,1},{3,2},{4,3},{5,4},{6,5},{7,6},{8,15},{9,8},{10,9... | collective-permute-start | bytes 442376 | tf_op jit(solution)/shard_map/ppermute | solution.py:207
  115.4 35.2 %all-to-all-start = ((bf16[16,48,1536]{2,1,0:T(8,128)(2,1)}), bf16[16,48,1536]{2,1,0:T(8,128)(2,1)}, u32[]{:S(2)}, u32[]{:S(2)}) async-start(bf16[16,48,1536]{2,1,0:T(8,128)(2,1)} %shard_map.95), calls=%async_computation | async-start | bytes 4718592 | tf_op jit(solution)/shard_map/all_to_all | solution.py:213
  122.1 56.2 %copy-start.12 = (f32[1,32,384]{2,1,0:T(8,128)S(1)}, f32[1,32,384]{2,1,0:T(8,128)}, u32[]{:S(2)}) copy-start(f32[1,32,384]{2,1,0:T(8,128)} %param.10) | copy-start | bytes 147460
  122.1 61.7 %copy-start.11 = (f32[1,32,640]{2,1,0:T(8,128)S(1)}, f32[1,32,640]{2,1,0:T(8,128)}, u32[]{:S(2)}) copy-start(f32[1,32,640]{2,1,0:T(8,128)} %param.11) | copy-start | bytes 245764
  122.1 76.8 %collective-permute-start.23 = (bf16[512,2560]{1,0:T(8,128)(2,1)S(1)}, bf16[512,2560]{1,0:T(8,128)(2,1)}, u32[]{:S(2)}, u32[]{:S(2)}) collective-permute-start(bf16[512,2560]{1,0:T(8,128)(2,1)S(1)} %bitcast.12), channel_id=1, source_target_pairs={{0,8},{8,0},{1,9},{9,1},{2,10},{10,2},{3,11},{11,3},{4,12},{12,4},... | collective-permute-start | bytes 7864328 | tf_op jit(solution)/shard_map/ppermute | solution.py:215
  150.6 21.9 %all-to-all-start.1 = ((bf16[16,16,2560]{2,1,0:T(8,128)(2,1)}), bf16[16,16,2560]{2,1,0:T(8,128)(2,1)}, u32[]{:S(2)}, u32[]{:S(2)}) async-start(bf16[16,16,2560]{2,1,0:T(8,128)(2,1)} %shard_map.97), calls=%async_computation.1 | async-start | bytes 2621440 | tf_op jit(solution)/shard_map/all_to_all | solution.py:213
  156.5 33.7 %collective-permute-start.21 = (bf16[768,1536]{1,0:T(8,128)(2,1)}, bf16[768,1536]{1,0:T(8,128)(2,1)}, u32[]{:S(2)}, u32[]{:S(2)}) collective-permute-start(bf16[768,1536]{1,0:T(8,128)(2,1)} %bitcast.5.refs_0_), channel_id=1, source_target_pairs={{0,8},{8,0},{1,9},{9,1},{2,10},{10,2},{3,11},{11,3},{4,12},{12,4},... | collective-permute-start | bytes 7077896 | tf_op jit(solution)/shard_map/ppermute | solution.py:215
  172.6 26.3 %collective-permute-start.22 = (bf16[256,2560]{1,0:T(8,128)(2,1)}, bf16[256,2560]{1,0:T(8,128)(2,1)}, u32[]{:S(2)}, u32[]{:S(2)}) collective-permute-start(bf16[256,2560]{1,0:T(8,128)(2,1)} %bitcast.7.refs_0_), channel_id=1, source_target_pairs={{0,8},{8,0},{1,9},{9,1},{2,10},{10,2},{3,11},{11,3},{4,12},{12,4},... | collective-permute-start | bytes 3932168 | tf_op jit(solution)/shard_map/ppermute | solution.py:215
  (8 other events, 25.8 us)

commit v2 on v1

v2 whole, which is shorter than its diff:
```python
import functools

import jax
import jax.numpy as jnp
from jax import lax
from jax.experimental import pallas as pl
from jax.experimental.pallas import tpu as pltpu
from jax.sharding import Mesh
from jax.sharding import PartitionSpec as P

ROUTED = 160
OWNERS = 4
Z = 8
DESTS = 32
FLIGHT = 64
AXES = ("x", "yh", "yl", "core", "z")
SPLITS = {2: (4, 1), 4: (2, 2), 6: (4, 2)}
GRAD_CHUNKS = ((0, 4), (4, 6))
HIDDEN_CHUNKS = ((0, 6),)
f32 = jnp.float32
bf16 = jnp.bfloat16
VMEM = pl.BlockSpec(memory_space=pltpu.VMEM)
SMEM = pl.BlockSpec(memory_space=pltpu.SMEM)
ANY = pl.BlockSpec(memory_space=pl.ANY)


def params(mib):
    return pltpu.CompilerParams(vmem_limit_bytes=mib * 2**20)


def one_hot(rows, target):
    position = lax.broadcasted_iota(jnp.int32, (rows, target.shape[1]), 0)
    return (position == target).astype(f32).astype(bf16)


def slot_table(routes_ref):
    slots, tok = routes_ref.shape
    ids = routes_ref[...]
    upper = (
        lax.broadcasted_iota(jnp.int32, (tok, tok), 0) < lax.broadcasted_iota(jnp.int32, (tok, tok), 1)
    ).astype(f32).astype(bf16)
    window = lax.broadcasted_iota(jnp.int32, (FLIGHT, tok), 0)
    seen = jnp.zeros((FLIGHT, 1), f32)
    out = []
    for k in range(slots):
        named = (window == ids[k : k + 1, :]).astype(f32)
        before = jnp.dot(named.astype(bf16), upper, preferred_element_type=f32) + seen
        slot = jnp.sum(named * before, axis=0, keepdims=True)
        seen = seen + jnp.sum(named, axis=1, keepdims=True)
        out.append((ids[k : k + 1, :], slot.astype(jnp.int32)))
    return out


def targets(table, my_half, first, last):
    width = last - first
    out = []
    for ids, slot in table:
        dest = lax.shift_right_logical(ids, 4) * Z + (ids & (Z - 1))
        across = (lax.shift_right_logical(ids, 3) & 1) ^ my_half
        place = dest * (2 * width) + across * width + slot - first
        ok = (ids < FLIGHT) & (slot >= first) & (slot < last)
        out.append(jnp.where(ok, place, -1))
    return out


def spread(compact, width, out_ref):
    cuts, groups = SPLITS[width]
    block = cuts * 2 * width
    per = DESTS // groups
    lanes = out_ref.shape[2]
    source = lax.broadcasted_iota(jnp.int32, (1, per * 2 * width), 1)
    dest = lax.div(source, 2 * width)
    start = dest * block + source - dest * (2 * width)
    moves = [one_hot(per * block, start + cut * 2 * width) for cut in range(cuts)]
    for group in range(groups):
        total = None
        for cut, move in enumerate(moves):
            piece = compact[group * per * 2 * width : (group + 1) * per * 2 * width, cut * lanes : (cut + 1) * lanes]
            part = jnp.dot(move, piece, preferred_element_type=f32)
            total = part if total is None else total + part
        out_ref[group * per : (group + 1) * per] = total.astype(bf16).reshape(per, block, lanes)


def pack_grad_kernel(half_ref, routes_ref, gates_ref, grads_ref, *outs):
    tok = routes_ref.shape[1]
    table = slot_table(routes_ref)
    for (first, last), out_ref in zip(GRAD_CHUNKS, outs):
        rows = FLIGHT * (last - first)
        position = lax.broadcasted_iota(jnp.int32, (rows, tok), 0)
        pick = jnp.zeros((rows, tok), f32)
        weight = jnp.zeros((rows, tok), f32)
        for k, target in enumerate(targets(table, half_ref[0, 0], first, last)):
            hit = position == target
            pick = jnp.where(hit, 1.0, pick)
            weight = jnp.where(hit, gates_ref[k : k + 1, :], weight)
        gate = jnp.sum(weight, axis=1, keepdims=True)
        picked = jnp.dot(pick.astype(bf16), grads_ref[...], preferred_element_type=f32)
        spread((gate * picked).astype(bf16), last - first, out_ref)


def pack_hidden_kernel(half_ref, routes_ref, hidden_ref, *outs):
    table = slot_table(routes_ref)
    for (first, last), out_ref in zip(HIDDEN_CHUNKS, outs):
        rows = FLIGHT * (last - first)
        picked = None
        for k, target in enumerate(targets(table, half_ref[0, 0], first, last)):
            part = jnp.dot(one_hot(rows, target), hidden_ref[k], preferred_element_type=f32)
            picked = part if picked is None else picked + part
        spread(picked.astype(bf16), last - first, out_ref)


def packed_shapes(chunks, features):
    out = []
    for first, last in chunks:
        cuts = SPLITS[last - first][0]
        out.append(jax.ShapeDtypeStruct((DESTS, cuts * 2 * (last - first), features // cuts), bf16))
    return out


def gather_kernel(width, in_ref, own_ref, across_ref):
    cuts, groups = SPLITS[width]
    block = cuts * 2 * width
    per = DESTS // groups
    lanes = in_ref.shape[2]
    source = lax.broadcasted_iota(jnp.int32, (1, per * block), 1)
    sender = lax.div(source, block)
    rest = source - sender * block
    cut_of = lax.div(rest, 2 * width)
    rest = rest - cut_of * (2 * width)
    half = lax.div(rest, width)
    place = half * (per * width) + sender * width + rest - half * width
    moves = [one_hot(2 * per * width, jnp.where(cut_of == cut, place, -1)) for cut in range(cuts)]
    for group in range(groups):
        piece = in_ref[group * per : (group + 1) * per].reshape(per * block, lanes)
        for cut, move in enumerate(moves):
            moved = jnp.dot(move, piece, preferred_element_type=f32).astype(bf16)
            here = slice(group * per * width, (group + 1) * per * width)
            there = slice(cut * lanes, (cut + 1) * lanes)
            own_ref[here, there] = moved[: per * width]
            across_ref[here, there] = moved[per * width :]


def gathered(arrived, width, features):
    rows = DESTS * width
    return pl.pallas_call(
        functools.partial(gather_kernel, width),
        out_shape=(jax.ShapeDtypeStruct((rows, features), bf16),) * 2,
        in_specs=[VMEM],
        out_specs=(VMEM, VMEM),
        compiler_params=params(32),
        cost_estimate=pl.CostEstimate(
            flops=4 * rows * rows * features, bytes_accessed=8 * rows * features, transcendentals=0
        ),
    )(arrived)


def thirds(value):
    high = value.astype(bf16)
    rest = value - high.astype(f32)
    middle = rest.astype(bf16)
    low = (rest - middle.astype(f32)).astype(bf16)
    return jnp.concatenate([high, middle, low], axis=0)


def added(value, rows):
    return value[:rows] + value[rows : 2 * rows] + value[2 * rows :]


def stats_kernel(norm, offset, count, q_ref, *refs):
    panels, rows = refs[:OWNERS], refs[OWNERS : OWNERS + count]
    cov_ref, out_ref, held, turned, sems = refs[OWNERS + count :]
    block, tile = cov_ref.shape
    panel_rows = out_ref.shape[0]
    step = pl.program_id(0)
    quarter = q_ref[0, 0]

    def columns(away):
        return pl.ds(pl.multiple_of((quarter ^ away) * block, 128), block)

    @pl.when(step == 0)
    def _():
        copies = []
        at = 0
        for number, row in enumerate(rows):
            size = row.shape[0]
            copy = pltpu.make_async_copy(row, held.at[at : at + size, :], sems.at[number])
            copy.start()
            copies.append((copy, at, size))
            at += size
        for copy, at, size in copies:
            copy.wait()
        turned[...] = held[:, columns(0)].T

    tile_at = pl.ds(pl.multiple_of(step * tile, 128), tile)
    cov_ref[...] = jnp.dot(turned[...], held[:, tile_at], preferred_element_type=f32) * norm

    @pl.when(step == pl.num_programs(0) - 1)
    def _():
        share = None
        for away in range(OWNERS):
            part = lax.dot_general(
                thirds(panels[away][:, offset : offset + block]),
                held[:, columns(away)],
                (((1,), (1,)), ((), ())),
                preferred_element_type=f32,
            )
            share = part if share is None else share + part
        product = jnp.dot(thirds(added(share, panel_rows)), held[:, columns(0)], preferred_element_type=f32)
        out_ref[...] = added(product, panel_rows) * norm


def stats(quarter, panels, offset, rows, norm, tile):
    features = rows[0].shape[1]
    block = features // OWNERS
    total = sum(row.shape[0] for row in rows)
    panel_rows, panel_width = panels[0].shape
    return pl.pallas_call(
        functools.partial(stats_kernel, norm, offset, len(rows)),
        grid=(features // tile,),
        out_shape=(
            jax.ShapeDtypeStruct((block, features), f32),
            jax.ShapeDtypeStruct((panel_rows, block), f32),
        ),
        in_specs=[SMEM] + [pl.BlockSpec((panel_rows, panel_width), lambda n: (0, 0))] * OWNERS + [ANY] * len(rows),
        out_specs=(
            pl.BlockSpec((block, tile), lambda n: (0, n)),
            pl.BlockSpec((panel_rows, block), lambda n: (0, 0)),
        ),
        scratch_shapes=[
            pltpu.VMEM((total, features), bf16),
            pltpu.VMEM((block, total), bf16),
            pltpu.SemaphoreType.DMA((len(rows),)),
        ],
        compiler_params=params(40),
        cost_estimate=pl.CostEstimate(
            flops=2 * total * features * block,
            bytes_accessed=2 * total * features + 4 * features * block,
            transcendentals=0,
        ),
    )(quarter, *panels, *rows)


def core_swapped(value):
    return lax.ppermute(value, "core", [(0, 1), (1, 0)])


def y_moved(value, flip):
    return lax.ppermute(value, ("yh", "yl"), [(i, i ^ flip) for i in range(4)])


def along_y(own, across):
    pieces = [own, y_moved(own, 1), y_moved(across, 3), y_moved(across, 2)]
    return pieces + [core_swapped(piece) for piece in pieces]


def per_device(hidden_rows, out_grads, gates, routes, panel_a, panel_g):
    tok, slots, width_in = hidden_rows.shape
    width_out = out_grads.shape[1]
    norm = ROUTED / (tok * 256 * slots)
    routes_t = routes.T
    my_half = lax.axis_index("yh").astype(jnp.int32).reshape(1, 1)
    quarter = (lax.axis_index("yl") * 2 + lax.axis_index("core")).astype(jnp.int32).reshape(1, 1)
    packed_h = pl.pallas_call(
        pack_hidden_kernel,
        out_shape=packed_shapes(HIDDEN_CHUNKS, width_in),
        in_specs=[SMEM, VMEM, VMEM],
        out_specs=[VMEM] * len(HIDDEN_CHUNKS),
        compiler_params=params(32),
    )(my_half, routes_t, hidden_rows.transpose(1, 0, 2))
    packed_g = pl.pallas_call(
        pack_grad_kernel,
        out_shape=packed_shapes(GRAD_CHUNKS, width_out),
        in_specs=[SMEM, VMEM, VMEM, VMEM],
        out_specs=[VMEM] * len(GRAD_CHUNKS),
        compiler_params=params(32),
    )(my_half, routes_t, gates.T, out_grads)
    panel = jnp.concatenate([panel_a[0], panel_g[0]], axis=1)
    panels = [panel] + [
        lax.ppermute(panel, ("yl", "core"), [(i, i ^ away) for i in range(OWNERS)]) for away in range(1, OWNERS)
    ]
    chunks = [(packed_h[n], last - first, width_in) for n, (first, last) in enumerate(HIDDEN_CHUNKS)]
    chunks += [(packed_g[n], last - first, width_out) for n, (first, last) in enumerate(GRAD_CHUNKS)]
    rows = []
    before = None
    for sent, width, features in chunks:
        if before is not None:
            before, sent = lax.optimization_barrier((before, sent))
            rows.append(along_y(*gathered(before, *held)))
        before = lax.all_to_all(sent, ("x", "z"), 0, 0, tiled=True)
        held = (width, features)
    rows.append(along_y(*gathered(before, *held)))
    rows_h = [piece for part in rows[: len(HIDDEN_CHUNKS)] for piece in part]
    rows_g = [piece for part in rows[len(HIDDEN_CHUNKS) :] for piece in part]
    input_cov, input_panel = stats(quarter, panels, 0, rows_h, norm, 512)
    grad_cov, grad_panel = stats(quarter, panels, width_in // OWNERS, rows_g, norm, 512)
    return (input_cov[None], grad_cov[None], input_panel[None], grad_panel[None])


def solution(mesh):
    split = Mesh(mesh.devices.reshape(4, 2, 2, 2, Z), AXES)
    return jax.shard_map(
        per_device,
        mesh=split,
        in_specs=(
            P(AXES, None, None),
            P(AXES, None),
            P(AXES, None),
            P(AXES, None),
            P(AXES, None, None),
            P(AXES, None, None),
        ),
        out_specs=(P(AXES, None, None),) * 4,
        check_vma=False,
    )
```

time: 216 us -> 185 us (0.86)
  starting transfers between devices: 85.1 us -> 63.6 us
  blocking collectives: 11.9 us -> 0 us
  local copies, waits for them, and re-layouts: 4.16 us -> 12.6 us
  waiting for transfers between devices: 79.7 us -> 73.2 us
    ppermute x24, starting transfers between devices: 65.8 us -> 35.3 us  [the longest x12 18.1 us: core_swapped(): return lax.ppermute(value, 'core', [(0, 1), (1, 0)])]
    ppermute x24, waiting for transfers between devices: 42.3 us -> 29.2 us  [the longest x9 29.1 us: y_moved(): return lax.ppermute(value, ('yh', 'yl'), [(i, i ^ flip) for i in range(4)])]
    all_gather x2 -> x0, blocking collectives: 11.9 us -> none  [the longest x1 6.43 us: per_device(): full_g = lax.all_gather(panel_g[0], ('yl', 'core'), axis=0)]
    all_to_all x3, starting transfers between devices: 19.3 us -> 28.3 us  [per_device(): before = lax.all_to_all(sent, ('x', 'z'), 0, 0, tiled=True)]
    unnamed x26 -> x40, local copies, waits for them, and re-layouts: 4.16 us -> 12.6 us
    all_to_all x3, waiting for transfers between devices: 37.4 us -> 44 us  [per_device(): before = lax.all_to_all(sent, ('x', 'z'), 0, 0, tiled=True)]
  transfers between devices with their start and end apart: 27 -> 27, of which waited for: 13 -> 6; matrix products, arithmetic and copies ran while one was open for 0% -> 0% of each run, Pallas kernels for 7% -> 8%
where the time goes in v2:
time: 185 us
  waiting for transfers between devices  73.2 us (40%)
  starting transfers between devices  63.6 us (34%)
  Pallas kernels  34.2 us (18%)
  local copies, waits for them, and re-layouts  12.6 us (7%)
    all_to_all x3, waiting for transfers between devices, per_device(): before = lax.all_to_all(sent, ('x', 'z'), 0, 0, tiled=True)  44 us
    ppermute x9, waiting for transfers between devices, y_moved(): return lax.ppermute(value, ('yh', 'yl'), [(i, i ^ flip) for i in range(4)])  29.1 us
    all_to_all x3, starting transfers between devices, per_device(): before = lax.all_to_all(sent, ('x', 'z'), 0, 0, tiled=True)  28.3 us
    pallas_call x2, Pallas kernels, stats(): pl.pallas_call(functools.partial(stats_kernel, norm, offset, len(rows)),...  21.4 us
    ppermute x12, starting transfers between devices, core_swapped(): return lax.ppermute(value, 'core', [(0, 1), (1, 0)])  18.1 us
    ppermute x9, starting transfers between devices, y_moved(): return lax.ppermute(value, ('yh', 'yl'), [(i, i ^ flip) for i in range(4)])  13 us
    unnamed x40, local copies, waits for them, and re-layouts  12.6 us
    pallas_call x3, Pallas kernels, gathered(): pl.pallas_call(functools.partial(gather_kernel, width), out_shape=(jax.Sh...  4.9 us
  transfers between devices with their start and end apart: 27, of which 6 were waited for; matrix products, arithmetic and copies ran while one was open for 0% of the time, Pallas kernels for 8%

profile of v2, /device:TPU:1, one launch (start us, length us, event | category | flops | bytes accessed | tf_op | source)
XLA Modules:
  0.0 184.7 jit_solution(12280887607586971363)
XLA Ops:
  0.6 1.7 copy-done
  3.0 4.8 %shard_map.93 = bf16[32,48,384]{2,1,0:T(8,128)(2,1)} custom-call(s32[1,1]{1,0:T(1,128)} %bitcast.3.half_ref, s32[6,128]{1,0:T(8,128)S(1)} %bitcast.12, bf16[6,128,1536]{2,1,0:T(8,128)(2,1)S(1)} %bitcast.11), custom_call_target="tpu_custom_call" | custom-call | tf_op jit(solution)/shard_map/pallas_call | solution.py:263
  7.8 12.0 %all-to-all-start = ((bf16[32,48,384]{2,1,0:T(8,128)(2,1)}), bf16[32,48,384]{2,1,0:T(8,128)(2,1)S(1)}, u32[]{:S(2)}, u32[]{:S(2)}) async-start(bf16[32,48,384]{2,1,0:T(8,128)(2,1)} %shard_map.93), calls=%async_computation | async-start | bytes 2359296 | tf_op jit(solution)/shard_map/all_to_all | solution.py:289
  19.8 3.1 %shard_map.94 = (bf16[32,16,1280]{2,1,0:T(8,128)(2,1)S(1)}, bf16[32,16,640]{2,1,0:T(8,128)(2,1)}) custom-call(s32[1,1]{1,0:T(1,128)} %bitcast.3.half_ref, s32[6,128]{1,0:T(8,128)S(1)} %bitcast.13, f32[6,128]{1,0:T(8,128)S(1)} %bitcast.14, bf16[128,2560]{1,0:T(8,128)(2,1)S(1)} %copy-done.2), custom_call_target="tpu_custom_call" | custom-call | tf_op jit(solution)/shard_map/pallas_call | solution.py:270
  24.0 23.3 %all-to-all-done.in_ref = bf16[32,48,384]{2,1,0:T(8,128)(2,1)S(1)} async-done(((bf16[32,48,384]{2,1,0:T(8,128)(2,1)}), bf16[32,48,384]{2,1,0:T(8,128)(2,1)S(1)}, u32[]{:S(2)}, u32[]{:S(2)}) %all-to-all-start) | async-done | bytes 1179680 | tf_op jit(solution)/shard_map/all_to_all | solution.py:289
  47.3 8.6 %all-to-all-start.1 = ((bf16[32,16,1280]{2,1,0:T(8,128)(2,1)}), bf16[32,16,1280]{2,1,0:T(8,128)(2,1)S(1)}, u32[]{:S(2)}, u32[]{:S(2)}) async-start(bf16[32,16,1280]{2,1,0:T(8,128)(2,1)} %copy-done.1), calls=%async_computation.1 | async-start | bytes 2621440 | tf_op jit(solution)/shard_map/all_to_all | solution.py:289
  55.9 2.2 %shard_map.95 = (bf16[192,1536]{1,0:T(8,128)(2,1)S(1)}, bf16[192,1536]{1,0:T(8,128)(2,1)}) custom-call(bf16[32,48,384]{2,1,0:T(8,128)(2,1)S(1)} %all-to-all-done.in_ref), custom_call_target="tpu_custom_call" | custom-call | flops 226492416 | bytes 2359296 | tf_op jit(solution)/shard_map/pallas_call | solution.py:145
  58.2 1.3 collective-permute-start.3
  59.5 1.9 %collective-permute-start.4 = (bf16[192,1536]{1,0:T(8,128)(2,1)}, bf16[192,1536]{1,0:T(8,128)(2,1)}, u32[]{:S(2)}, u32[]{:S(2)}) collective-permute-start(bf16[192,1536]{1,0:T(8,128)(2,1)} %get-tuple-element.23), channel_id=1, source_target_pairs={{0,48},{16,32},{32,16},{48,0},{1,49},{17,33},{33,17},{49,1},{2,50}... | collective-permute-start | bytes 1769480 | tf_op jit(solution)/shard_map/ppermute | solution.py:248
  62.1 2.1 %collective-permute-start = (f32[32,1024]{1,0:T(8,128)S(1)}, f32[32,1024]{1,0:T(8,128)S(1)}, u32[]{:S(2)}, u32[]{:S(2)}) collective-permute-start(f32[32,1024]{1,0:T(8,128)S(1)} %pad_maximum_fusion.refs_0_), channel_id=1, source_target_pairs={{0,8},{8,0},{16,24},{24,16},{1,9},{9,1},{17,25},{25,17},{2,10},{10... | collective-permute-start | bytes 393224 | tf_op jit(solution)/shard_map/ppermute | solution.py:279
  65.2 1.2 collective-permute-start.2
  66.4 20.7 %all-to-all-done.1.in_ref = bf16[32,16,1280]{2,1,0:T(8,128)(2,1)S(1)} async-done(((bf16[32,16,1280]{2,1,0:T(8,128)(2,1)}), bf16[32,16,1280]{2,1,0:T(8,128)(2,1)S(1)}, u32[]{:S(2)}, u32[]{:S(2)}) %all-to-all-start.1) | async-done | bytes 1310752 | tf_op jit(solution)/shard_map/all_to_all | solution.py:289
  87.1 1.4 shard_map.97
  88.4 1.3 collective-permute-start.10
  89.7 7.7 %all-to-all-start.2 = ((bf16[32,16,640]{2,1,0:T(8,128)(2,1)}), bf16[32,16,640]{2,1,0:T(8,128)(2,1)S(1)}, u32[]{:S(2)}, u32[]{:S(2)}) async-start(bf16[32,16,640]{2,1,0:T(8,128)(2,1)} %get-tuple-element.30), calls=%async_computation.2 | async-start | bytes 1310720 | tf_op jit(solution)/shard_map/all_to_all | solution.py:289
  98.1 5.3 %collective-permute-start.6 = (bf16[192,1536]{1,0:T(8,128)(2,1)S(1)}, bf16[192,1536]{1,0:T(8,128)(2,1)S(1)}, u32[]{:S(2)}, u32[]{:S(2)}) collective-permute-start(bf16[192,1536]{1,0:T(8,128)(2,1)S(1)} %get-tuple-element.22.refs_4_), channel_id=1, source_target_pairs={{0,8},{8,0},{1,9},{9,1},{2,10},{10,2},{3,11},{11,3},{4,12},{12,4},... | collective-permute-start | bytes 1769480 | tf_op jit(solution)/shard_map/ppermute | solution.py:244
  103.9 1.9 %collective-permute-start.11 = (bf16[128,2560]{1,0:T(8,128)(2,1)}, bf16[128,2560]{1,0:T(8,128)(2,1)S(1)}, u32[]{:S(2)}, u32[]{:S(2)}) collective-permute-start(bf16[128,2560]{1,0:T(8,128)(2,1)} %get-tuple-element.29), channel_id=1, source_target_pairs={{0,48},{16,32},{32,16},{48,0},{1,49},{17,33},{33,17},{49,1},{2,50}... | collective-permute-start | bytes 1966088 | tf_op jit(solution)/shard_map/ppermute | solution.py:248
  106.6 2.6 %collective-permute-start.12 = (bf16[128,2560]{1,0:T(8,128)(2,1)}, bf16[128,2560]{1,0:T(8,128)(2,1)S(1)}, u32[]{:S(2)}, u32[]{:S(2)}) collective-permute-start(bf16[128,2560]{1,0:T(8,128)(2,1)} %get-tuple-element.29), channel_id=1, source_target_pairs={{0,32},{16,48},{32,0},{48,16},{1,33},{17,49},{33,1},{49,17},{2,34}... | collective-permute-start | bytes 1966088 | tf_op jit(solution)/shard_map/ppermute | solution.py:248
  112.0 23.6 %collective-permute-done.11.refs_6_ = bf16[128,2560]{1,0:T(8,128)(2,1)S(1)} collective-permute-done((bf16[128,2560]{1,0:T(8,128)(2,1)}, bf16[128,2560]{1,0:T(8,128)(2,1)S(1)}, u32[]{:S(2)}, u32[]{:S(2)}) %collective-permute-start.11) | collective-permute-done | bytes 655392 | tf_op jit(solution)/shard_map/ppermute | solution.py:248
  136.5 1.3 shard_map.98
  137.9 1.9 %collective-permute-start.18 = (bf16[64,2560]{1,0:T(8,128)(2,1)S(1)}, bf16[64,2560]{1,0:T(8,128)(2,1)}, u32[]{:S(2)}, u32[]{:S(2)}) collective-permute-start(bf16[64,2560]{1,0:T(8,128)(2,1)S(1)} %get-tuple-element.32), channel_id=1, source_target_pairs={{0,48},{16,32},{32,16},{48,0},{1,49},{17,33},{33,17},{49,1},{2,50}... | collective-permute-start | bytes 983048 | tf_op jit(solution)/shard_map/ppermute | solution.py:248
  139.9 1.3 collective-permute-start.19
  141.2 1.3 collective-permute-start.20
  142.4 4.7 %collective-permute-done.17.refs_13_ = bf16[64,2560]{1,0:T(8,128)(2,1)} collective-permute-done((bf16[64,2560]{1,0:T(8,128)(2,1)}, bf16[64,2560]{1,0:T(8,128)(2,1)}, u32[]{:S(2)}, u32[]{:S(2)}) %collective-permute-start.17) | collective-permute-done | bytes 327712 | tf_op jit(solution)/shard_map/ppermute | solution.py:248
  147.1 2.1 %collective-permute-start.21 = (bf16[64,2560]{1,0:T(8,128)(2,1)}, bf16[64,2560]{1,0:T(8,128)(2,1)}, u32[]{:S(2)}, u32[]{:S(2)}) collective-permute-start(bf16[64,2560]{1,0:T(8,128)(2,1)} %collective-permute-done.17.refs_13_), channel_id=1, source_target_pairs={{0,8},{8,0},{1,9},{9,1},{2,10},{10,2},{3,11},{11,3},{4,12},{12,4},... | collective-permute-start | bytes 983048 | tf_op jit(solution)/shard_map/ppermute | solution.py:244
  149.2 5.6 %collective-permute-start.22 = (bf16[64,2560]{1,0:T(8,128)(2,1)}, bf16[64,2560]{1,0:T(8,128)(2,1)}, u32[]{:S(2)}, u32[]{:S(2)}) collective-permute-start(bf16[64,2560]{1,0:T(8,128)(2,1)} %collective-permute-done.18.refs_14_), channel_id=1, source_target_pairs={{0,8},{8,0},{1,9},{9,1},{2,10},{10,2},{3,11},{11,3},{4,12},{12,4},... | collective-permute-start | bytes 983048 | tf_op jit(solution)/shard_map/ppermute | solution.py:244
  155.7 1.3 collective-permute-start.23
  157.0 1.1 copy-done.7
  159.1 1.1 copy-done.11
  160.2 1.1 copy-done.13
  163.0 7.4 %shard_map.96 = (f32[384,1536]{1,0:T(8,128)}, f32[32,384]{1,0:T(8,128)}) custom-call(s32[1,1]{1,0:T(1,128)} %bitcast.q_ref, f32[32,1024]{1,0:T(8,128)S(1)} %pad_maximum_fusion.refs_0_, f32[32,1024]{1,0:T(8,128)S(1)} %collective-permute-done.refs_1_, f32[32,1024]{1,0:T(8,128)S(1)} %copy-done.15, f32[32,1024]{1,0:T(8,128)S(1)} %copy-done.17, ...), custom_call_target="tpu_custom_call" | custom-call | flops 1811939328 | bytes 7077888 | tf_op jit(solution)/shard_map/pallas_call | solution.py:217
  170.5 14.0 %shard_map.99 = (f32[640,2560]{1,0:T(8,128)}, f32[32,640]{1,0:T(8,128)}) custom-call(s32[1,1]{1,0:T(1,128)} %bitcast.q_ref, f32[32,1024]{1,0:T(8,128)S(1)} %pad_maximum_fusion.refs_0_, f32[32,1024]{1,0:T(8,128)S(1)} %collective-permute-done.refs_1_, f32[32,1024]{1,0:T(8,128)S(1)} %copy-done.15, f32[32,1024]{1,0:T(8,128)S(1)} %copy-done.17, ...), custom_call_target="tpu_custom_call" | custom-call | flops 5033164800 | bytes 14417920 | tf_op jit(solution)/shard_map/pallas_call | solution.py:217
  (70 shorter events, 13.0 us)
Async XLA Ops:
  7.8 12.0 %copy-start.5 = (f32[128,6]{0,1:T(8,128)S(1)}, f32[128,6]{0,1:T(8,128)}, u32[]{:S(2)}) copy-start(f32[128,6]{0,1:T(8,128)} %param.8) | copy-start | bytes 9220
  7.8 39.5 %all-to-all-start = ((bf16[32,48,384]{2,1,0:T(8,128)(2,1)}), bf16[32,48,384]{2,1,0:T(8,128)(2,1)S(1)}, u32[]{:S(2)}, u32[]{:S(2)}) async-start(bf16[32,48,384]{2,1,0:T(8,128)(2,1)} %shard_map.93), calls=%async_computation | async-start | bytes 2359296 | tf_op jit(solution)/shard_map/all_to_all | solution.py:289
  47.3 14.8 %copy-start.18 = (f32[1,32,640]{2,1,0:T(8,128)S(1)}, f32[1,32,640]{2,1,0:T(8,128)}, u32[]{:S(2)}) copy-start(f32[1,32,640]{2,1,0:T(8,128)} %param.11) | copy-start | bytes 245764
  47.3 14.8 %copy-start.19 = (f32[1,32,384]{2,1,0:T(8,128)S(1)}, f32[1,32,384]{2,1,0:T(8,128)}, u32[]{:S(2)}) copy-start(f32[1,32,384]{2,1,0:T(8,128)} %param.10) | copy-start | bytes 147460
  47.3 39.8 %all-to-all-start.1 = ((bf16[32,16,1280]{2,1,0:T(8,128)(2,1)}), bf16[32,16,1280]{2,1,0:T(8,128)(2,1)S(1)}, u32[]{:S(2)}, u32[]{:S(2)}) async-start(bf16[32,16,1280]{2,1,0:T(8,128)(2,1)} %copy-done.1), calls=%async_computation.1 | async-start | bytes 2621440 | tf_op jit(solution)/shard_map/all_to_all | solution.py:289
  58.2 39.3 %copy-start.6 = (bf16[192,1536]{1,0:T(8,128)(2,1)}, bf16[192,1536]{1,0:T(8,128)(2,1)S(1)}, u32[]{:S(2)}) copy-start(bf16[192,1536]{1,0:T(8,128)(2,1)S(1)} %get-tuple-element.22.refs_4_) | copy-start | bytes 1769476
  58.2 45.2 %collective-permute-start.3 = (bf16[192,1536]{1,0:T(8,128)(2,1)S(1)}, bf16[192,1536]{1,0:T(8,128)(2,1)}, u32[]{:S(2)}, u32[]{:S(2)}) collective-permute-start(bf16[192,1536]{1,0:T(8,128)(2,1)S(1)} %get-tuple-element.22.refs_4_), channel_id=1, source_target_pairs={{0,16},{16,0},{32,48},{48,32},{1,17},{17,1},{33,49},{49,33},{2,18}... | collective-permute-start | bytes 1769480 | tf_op jit(solution)/shard_map/ppermute | solution.py:248
  59.5 43.9 %collective-permute-start.4 = (bf16[192,1536]{1,0:T(8,128)(2,1)}, bf16[192,1536]{1,0:T(8,128)(2,1)}, u32[]{:S(2)}, u32[]{:S(2)}) collective-permute-start(bf16[192,1536]{1,0:T(8,128)(2,1)} %get-tuple-element.23), channel_id=1, source_target_pairs={{0,48},{16,32},{32,16},{48,0},{1,49},{17,33},{33,17},{49,1},{2,50}... | collective-permute-start | bytes 1769480 | tf_op jit(solution)/shard_map/ppermute | solution.py:248
  61.4 42.5 %collective-permute-start.5 = (bf16[192,1536]{1,0:T(8,128)(2,1)}, bf16[192,1536]{1,0:T(8,128)(2,1)}, u32[]{:S(2)}, u32[]{:S(2)}) collective-permute-start(bf16[192,1536]{1,0:T(8,128)(2,1)} %get-tuple-element.23), channel_id=1, source_target_pairs={{0,32},{16,48},{32,0},{48,16},{1,33},{17,49},{33,1},{49,17},{2,34}... | collective-permute-start | bytes 1769480 | tf_op jit(solution)/shard_map/ppermute | solution.py:248
  62.1 3.1 %collective-permute-start = (f32[32,1024]{1,0:T(8,128)S(1)}, f32[32,1024]{1,0:T(8,128)S(1)}, u32[]{:S(2)}, u32[]{:S(2)}) collective-permute-start(f32[32,1024]{1,0:T(8,128)S(1)} %pad_maximum_fusion.refs_0_), channel_id=1, source_target_pairs={{0,8},{8,0},{16,24},{24,16},{1,9},{9,1},{17,25},{25,17},{2,10},{10... | collective-permute-start | bytes 393224 | tf_op jit(solution)/shard_map/ppermute | solution.py:279
  64.2 24.2 %collective-permute-start.1 = (f32[32,1024]{1,0:T(8,128)S(1)}, f32[32,1024]{1,0:T(8,128)S(1)}, u32[]{:S(2)}, u32[]{:S(2)}) collective-permute-start(f32[32,1024]{1,0:T(8,128)S(1)} %pad_maximum_fusion.refs_0_), channel_id=1, source_target_pairs={{0,16},{8,24},{16,0},{24,8},{1,17},{9,25},{17,1},{25,9},{2,18},{10... | collective-permute-start | bytes 393224 | tf_op jit(solution)/shard_map/ppermute | solution.py:279
  65.2 32.2 %collective-permute-start.2 = (f32[32,1024]{1,0:T(8,128)S(1)}, f32[32,1024]{1,0:T(8,128)S(1)}, u32[]{:S(2)}, u32[]{:S(2)}) collective-permute-start(f32[32,1024]{1,0:T(8,128)S(1)} %pad_maximum_fusion.refs_0_), channel_id=1, source_target_pairs={{0,24},{8,16},{16,8},{24,0},{1,25},{9,17},{17,9},{25,1},{2,26},{10... | collective-permute-start | bytes 393224 | tf_op jit(solution)/shard_map/ppermute | solution.py:279
  88.4 15.4 %copy-start.14 = (f32[32,1024]{1,0:T(8,128)}, f32[32,1024]{1,0:T(8,128)S(1)}, u32[]{:S(2)}) copy-start(f32[32,1024]{1,0:T(8,128)S(1)} %collective-permute-done.1.refs_2_) | copy-start | bytes 393220
  88.4 22.2 %collective-permute-start.10 = (bf16[128,2560]{1,0:T(8,128)(2,1)S(1)}, bf16[128,2560]{1,0:T(8,128)(2,1)S(1)}, u32[]{:S(2)}, u32[]{:S(2)}) collective-permute-start(bf16[128,2560]{1,0:T(8,128)(2,1)S(1)} %get-tuple-element.28.refs_4_), channel_id=1, source_target_pairs={{0,16},{16,0},{32,48},{48,32},{1,17},{17,1},{33,49},{49,33},{2,18}... | collective-permute-start | bytes 1966088 | tf_op jit(solution)/shard_map/ppermute | solution.py:248
  89.7 46.8 %all-to-all-start.2 = ((bf16[32,16,640]{2,1,0:T(8,128)(2,1)}), bf16[32,16,640]{2,1,0:T(8,128)(2,1)S(1)}, u32[]{:S(2)}, u32[]{:S(2)}) async-start(bf16[32,16,640]{2,1,0:T(8,128)(2,1)} %get-tuple-element.30), calls=%async_computation.2 | async-start | bytes 1310720 | tf_op jit(solution)/shard_map/all_to_all | solution.py:289
  98.1 7.7 %collective-permute-start.6 = (bf16[192,1536]{1,0:T(8,128)(2,1)S(1)}, bf16[192,1536]{1,0:T(8,128)(2,1)S(1)}, u32[]{:S(2)}, u32[]{:S(2)}) collective-permute-start(bf16[192,1536]{1,0:T(8,128)(2,1)S(1)} %get-tuple-element.22.refs_4_), channel_id=1, source_target_pairs={{0,8},{8,0},{1,9},{9,1},{2,10},{10,2},{3,11},{11,3},{4,12},{12,4},... | collective-permute-start | bytes 1769480 | tf_op jit(solution)/shard_map/ppermute | solution.py:244
  103.4 5.8 %collective-permute-start.7 = (bf16[192,1536]{1,0:T(8,128)(2,1)}, bf16[192,1536]{1,0:T(8,128)(2,1)S(1)}, u32[]{:S(2)}, u32[]{:S(2)}) collective-permute-start(bf16[192,1536]{1,0:T(8,128)(2,1)} %collective-permute-done.3.refs_5_), channel_id=1, source_target_pairs={{0,8},{8,0},{1,9},{9,1},{2,10},{10,2},{3,11},{11,3},{4,12},{12,4},... | collective-permute-start | bytes 1769480 | tf_op jit(solution)/shard_map/ppermute | solution.py:244
  103.4 7.3 %collective-permute-start.8 = (bf16[192,1536]{1,0:T(8,128)(2,1)}, bf16[192,1536]{1,0:T(8,128)(2,1)S(1)}, u32[]{:S(2)}, u32[]{:S(2)}) collective-permute-start(bf16[192,1536]{1,0:T(8,128)(2,1)} %collective-permute-done.4.refs_6_), channel_id=1, source_target_pairs={{0,8},{8,0},{1,9},{9,1},{2,10},{10,2},{3,11},{11,3},{4,12},{12,4},... | collective-permute-start | bytes 1769480 | tf_op jit(solution)/shard_map/ppermute | solution.py:244
  103.9 31.8 %collective-permute-start.11 = (bf16[128,2560]{1,0:T(8,128)(2,1)}, bf16[128,2560]{1,0:T(8,128)(2,1)S(1)}, u32[]{:S(2)}, u32[]{:S(2)}) collective-permute-start(bf16[128,2560]{1,0:T(8,128)(2,1)} %get-tuple-element.29), channel_id=1, source_target_pairs={{0,48},{16,32},{32,16},{48,0},{1,49},{17,33},{33,17},{49,1},{2,50}... | collective-permute-start | bytes 1966088 | tf_op jit(solution)/shard_map/ppermute | solution.py:248
  106.6 31.3 %collective-permute-start.12 = (bf16[128,2560]{1,0:T(8,128)(2,1)}, bf16[128,2560]{1,0:T(8,128)(2,1)S(1)}, u32[]{:S(2)}, u32[]{:S(2)}) collective-permute-start(bf16[128,2560]{1,0:T(8,128)(2,1)} %get-tuple-element.29), channel_id=1, source_target_pairs={{0,32},{16,48},{32,0},{48,16},{1,33},{17,49},{33,1},{49,17},{2,34}... | collective-permute-start | bytes 1966088 | tf_op jit(solution)/shard_map/ppermute | solution.py:248
  110.0 27.9 %collective-permute-start.13 = (bf16[128,2560]{1,0:T(8,128)(2,1)S(1)}, bf16[128,2560]{1,0:T(8,128)(2,1)}, u32[]{:S(2)}, u32[]{:S(2)}) collective-permute-start(bf16[128,2560]{1,0:T(8,128)(2,1)S(1)} %get-tuple-element.28.refs_4_), channel_id=1, source_target_pairs={{0,8},{8,0},{1,9},{9,1},{2,10},{10,2},{3,11},{11,3},{4,12},{12,4},... | collective-permute-start | bytes 1966088 | tf_op jit(solution)/shard_map/ppermute | solution.py:244
  110.7 29.2 %collective-permute-start.14 = (bf16[128,2560]{1,0:T(8,128)(2,1)S(1)}, bf16[128,2560]{1,0:T(8,128)(2,1)}, u32[]{:S(2)}, u32[]{:S(2)}) collective-permute-start(bf16[128,2560]{1,0:T(8,128)(2,1)S(1)} %collective-permute-done.10.refs_5_), channel_id=1, source_target_pairs={{0,8},{8,0},{1,9},{9,1},{2,10},{10,2},{3,11},{11,3},{4,12},{12,4},... | collective-permute-start | bytes 1966088 | tf_op jit(solution)/shard_map/ppermute | solution.py:244
  111.5 26.3 %collective-permute-start.9 = (bf16[192,1536]{1,0:T(8,128)(2,1)}, bf16[192,1536]{1,0:T(8,128)(2,1)}, u32[]{:S(2)}, u32[]{:S(2)}) collective-permute-start(bf16[192,1536]{1,0:T(8,128)(2,1)} %collective-permute-done.5.refs_7_), channel_id=1, source_target_pairs={{0,8},{8,0},{1,9},{9,1},{2,10},{10,2},{3,11},{11,3},{4,12},{12,4},... | collective-permute-start | bytes 1769480 | tf_op jit(solution)/shard_map/ppermute | solution.py:244
  135.6 5.6 %collective-permute-start.15 = (bf16[128,2560]{1,0:T(8,128)(2,1)S(1)}, bf16[128,2560]{1,0:T(8,128)(2,1)}, u32[]{:S(2)}, u32[]{:S(2)}) collective-permute-start(bf16[128,2560]{1,0:T(8,128)(2,1)S(1)} %collective-permute-done.11.refs_6_), channel_id=1, source_target_pairs={{0,8},{8,0},{1,9},{9,1},{2,10},{10,2},{3,11},{11,3},{4,12},{12,4},... | collective-permute-start | bytes 1966088 | tf_op jit(solution)/shard_map/ppermute | solution.py:244
  137.8 32.6 %collective-permute-start.16 = (bf16[128,2560]{1,0:T(8,128)(2,1)S(1)}, bf16[128,2560]{1,0:T(8,128)(2,1)S(1)}, u32[]{:S(2)}, u32[]{:S(2)}) collective-permute-start(bf16[128,2560]{1,0:T(8,128)(2,1)S(1)} %collective-permute-done.12.refs_7_), channel_id=1, source_target_pairs={{0,8},{8,0},{1,9},{9,1},{2,10},{10,2},{3,11},{11,3},{4,12},{12,4},... | collective-permute-start | bytes 1966088 | tf_op jit(solution)/shard_map/ppermute | solution.py:244
  137.8 9.3 %collective-permute-start.17 = (bf16[64,2560]{1,0:T(8,128)(2,1)}, bf16[64,2560]{1,0:T(8,128)(2,1)}, u32[]{:S(2)}, u32[]{:S(2)}) collective-permute-start(bf16[64,2560]{1,0:T(8,128)(2,1)} %get-tuple-element.31.refs_12_), channel_id=1, source_target_pairs={{0,16},{16,0},{32,48},{48,32},{1,17},{17,1},{33,49},{49,33},{2,18}... | collective-permute-start | bytes 983048 | tf_op jit(solution)/shard_map/ppermute | solution.py:248
  137.9 11.3 %collective-permute-start.18 = (bf16[64,2560]{1,0:T(8,128)(2,1)S(1)}, bf16[64,2560]{1,0:T(8,128)(2,1)}, u32[]{:S(2)}, u32[]{:S(2)}) collective-permute-start(bf16[64,2560]{1,0:T(8,128)(2,1)S(1)} %get-tuple-element.32), channel_id=1, source_target_pairs={{0,48},{16,32},{32,16},{48,0},{1,49},{17,33},{33,17},{49,1},{2,50}... | collective-permute-start | bytes 983048 | tf_op jit(solution)/shard_map/ppermute | solution.py:248
  139.9 15.8 %collective-permute-start.19 = (bf16[64,2560]{1,0:T(8,128)(2,1)S(1)}, bf16[64,2560]{1,0:T(8,128)(2,1)}, u32[]{:S(2)}, u32[]{:S(2)}) collective-permute-start(bf16[64,2560]{1,0:T(8,128)(2,1)S(1)} %get-tuple-element.32), channel_id=1, source_target_pairs={{0,32},{16,48},{32,0},{48,16},{1,33},{17,49},{33,1},{49,17},{2,34}... | collective-permute-start | bytes 983048 | tf_op jit(solution)/shard_map/ppermute | solution.py:248
  141.2 29.3 %collective-permute-start.20 = (bf16[64,2560]{1,0:T(8,128)(2,1)}, bf16[64,2560]{1,0:T(8,128)(2,1)}, u32[]{:S(2)}, u32[]{:S(2)}) collective-permute-start(bf16[64,2560]{1,0:T(8,128)(2,1)} %get-tuple-element.31.refs_12_), channel_id=1, source_target_pairs={{0,8},{8,0},{1,9},{9,1},{2,10},{10,2},{3,11},{11,3},{4,12},{12,4},... | collective-permute-start | bytes 983048 | tf_op jit(solution)/shard_map/ppermute | solution.py:244
  147.1 23.4 %collective-permute-start.21 = (bf16[64,2560]{1,0:T(8,128)(2,1)}, bf16[64,2560]{1,0:T(8,128)(2,1)}, u32[]{:S(2)}, u32[]{:S(2)}) collective-permute-start(bf16[64,2560]{1,0:T(8,128)(2,1)} %collective-permute-done.17.refs_13_), channel_id=1, source_target_pairs={{0,8},{8,0},{1,9},{9,1},{2,10},{10,2},{3,11},{11,3},{4,12},{12,4},... | collective-permute-start | bytes 983048 | tf_op jit(solution)/shard_map/ppermute | solution.py:244
  149.2 21.3 %collective-permute-start.22 = (bf16[64,2560]{1,0:T(8,128)(2,1)}, bf16[64,2560]{1,0:T(8,128)(2,1)}, u32[]{:S(2)}, u32[]{:S(2)}) collective-permute-start(bf16[64,2560]{1,0:T(8,128)(2,1)} %collective-permute-done.18.refs_14_), channel_id=1, source_target_pairs={{0,8},{8,0},{1,9},{9,1},{2,10},{10,2},{3,11},{11,3},{4,12},{12,4},... | collective-permute-start | bytes 983048 | tf_op jit(solution)/shard_map/ppermute | solution.py:244
  155.7 14.8 %collective-permute-start.23 = (bf16[64,2560]{1,0:T(8,128)(2,1)}, bf16[64,2560]{1,0:T(8,128)(2,1)}, u32[]{:S(2)}, u32[]{:S(2)}) collective-permute-start(bf16[64,2560]{1,0:T(8,128)(2,1)} %collective-permute-done.19.refs_15_), channel_id=1, source_target_pairs={{0,8},{8,0},{1,9},{9,1},{2,10},{10,2},{3,11},{11,3},{4,12},{12,4},... | collective-permute-start | bytes 983048 | tf_op jit(solution)/shard_map/ppermute | solution.py:244
  (15 other events, 36.6 us)

commit v3 on v2

v3 whole, which is shorter than its diff:
```python
import functools

import jax
import jax.numpy as jnp
from jax import lax
from jax.experimental import pallas as pl
from jax.experimental.pallas import tpu as pltpu
from jax.sharding import Mesh
from jax.sharding import PartitionSpec as P

ROUTED = 160
OWNERS = 4
Z = 8
DESTS = 32
FLIGHT = 64
AXES = ("x", "yh", "yl", "core", "z")
SPLITS = {2: (4, 1), 4: (2, 2), 6: (4, 2)}
GRAD_FIRST = (0, 4)
GRAD_LAST = (4, 6)
HIDDEN_FIRST = (0, 4)
HIDDEN_LAST = (4, 6)
f32 = jnp.float32
bf16 = jnp.bfloat16
VMEM = pl.BlockSpec(memory_space=pltpu.VMEM)
SMEM = pl.BlockSpec(memory_space=pltpu.SMEM)
HBM = pl.BlockSpec(memory_space=pltpu.HBM)


def params(mib):
    return pltpu.CompilerParams(vmem_limit_bytes=mib * 2**20)


def one_hot(rows, target):
    position = lax.broadcasted_iota(jnp.int32, (rows, target.shape[1]), 0)
    return (position == target).astype(f32).astype(bf16)


def slot_table(routes_ref):
    slots, tok = routes_ref.shape
    ids = routes_ref[...]
    upper = (
        lax.broadcasted_iota(jnp.int32, (tok, tok), 0) < lax.broadcasted_iota(jnp.int32, (tok, tok), 1)
    ).astype(f32).astype(bf16)
    window = lax.broadcasted_iota(jnp.int32, (FLIGHT, tok), 0)
    seen = jnp.zeros((FLIGHT, 1), f32)
    out = []
    for k in range(slots):
        named = (window == ids[k : k + 1, :]).astype(f32)
        before = jnp.dot(named.astype(bf16), upper, preferred_element_type=f32) + seen
        slot = jnp.sum(named * before, axis=0, keepdims=True)
        seen = seen + jnp.sum(named, axis=1, keepdims=True)
        out.append((ids[k : k + 1, :], slot.astype(jnp.int32)))
    return out


def targets(table, my_half, first, last):
    width = last - first
    out = []
    for ids, slot in table:
        dest = lax.shift_right_logical(ids, 4) * Z + (ids & (Z - 1))
        across = (lax.shift_right_logical(ids, 3) & 1) ^ my_half
        place = across * (DESTS * width) + dest * width + slot - first
        ok = (ids < FLIGHT) & (slot >= first) & (slot < last)
        out.append(jnp.where(ok, place, -1))
    return out


def spread(own, across, width, out_ref):
    cuts, groups = SPLITS[width]
    block = cuts * 2 * width
    per = DESTS // groups
    lanes = out_ref.shape[2]
    source = lax.broadcasted_iota(jnp.int32, (1, 2 * per * width), 1)
    half = lax.div(source, per * width)
    rest = source - half * (per * width)
    dest = lax.div(rest, width)
    start = dest * block + half * width + rest - dest * width
    moves = [one_hot(per * block, start + cut * 2 * width) for cut in range(cuts)]
    for group in range(groups):
        here = slice(group * per * width, (group + 1) * per * width)
        both = jnp.concatenate([own[here, :], across[here, :]], axis=0)
        total = None
        for cut, move in enumerate(moves):
            part = jnp.dot(move, both[:, cut * lanes : (cut + 1) * lanes], preferred_element_type=f32)
            total = part if total is None else total + part
        out_ref[group * per : (group + 1) * per] = total.astype(bf16).reshape(per, block, lanes)


def packed_grads(table, half_ref, gates_ref, grads_ref, first, last):
    rows = FLIGHT * (last - first)
    position = lax.broadcasted_iota(jnp.int32, (rows, grads_ref.shape[0]), 0)
    pick = jnp.zeros(position.shape, f32)
    weight = jnp.zeros(position.shape, f32)
    for k, target in enumerate(targets(table, half_ref[0, 0], first, last)):
        hit = position == target
        pick = jnp.where(hit, 1.0, pick)
        weight = jnp.where(hit, gates_ref[k : k + 1, :], weight)
    gate = jnp.sum(weight, axis=1, keepdims=True)
    picked = jnp.dot(pick.astype(bf16), grads_ref[...], preferred_element_type=f32)
    return (gate * picked).astype(bf16)


def first_grads_kernel(half_ref, routes_ref, gates_ref, grads_ref, out_ref):
    packed = packed_grads(slot_table(routes_ref), half_ref, gates_ref, grads_ref, *GRAD_FIRST)
    rows = packed.shape[0] // 2
    spread(packed[:rows], packed[rows:], GRAD_FIRST[1] - GRAD_FIRST[0], out_ref)


def last_grads_kernel(half_ref, routes_ref, gates_ref, grads_ref, own_ref, across_ref):
    packed = packed_grads(slot_table(routes_ref), half_ref, gates_ref, grads_ref, *GRAD_LAST)
    rows = own_ref.shape[0]
    own_ref[...] = packed[:rows]
    across_ref[...] = packed[rows:]


def hidden_kernel(half_ref, routes_ref, hidden_ref, *outs):
    table = slot_table(routes_ref)
    for number, (first, last) in enumerate((HIDDEN_FIRST, HIDDEN_LAST)):
        rows = DESTS * (last - first)
        picked = None
        for k, target in enumerate(targets(table, half_ref[0, 0], first, last)):
            part = jnp.dot(one_hot(2 * rows, target), hidden_ref[k], preferred_element_type=f32)
            picked = part if picked is None else picked + part
        outs[2 * number][...] = picked[:rows].astype(bf16)
        outs[2 * number + 1][...] = picked[rows:].astype(bf16)


def block_shape(width, features):
    cuts = SPLITS[width][0]
    return jax.ShapeDtypeStruct((DESTS, cuts * 2 * width, features // cuts), bf16)


def rows_shape(width, features):
    return jax.ShapeDtypeStruct((DESTS * width, features), bf16)


def spread_kernel(width, own_ref, across_ref, out_ref):
    spread(own_ref, across_ref, width, out_ref)


def spread_rows(own, across, width):
    rows, features = own.shape
    return pl.pallas_call(
        functools.partial(spread_kernel, width),
        out_shape=block_shape(width, features),
        in_specs=[VMEM, VMEM],
        out_specs=VMEM,
        compiler_params=params(32),
        cost_estimate=pl.CostEstimate(flops=1, bytes_accessed=1, transcendentals=0),
    )(own, across)


def gather_kernel(width, in_ref, *outs):
    cuts, groups = SPLITS[width]
    block = cuts * 2 * width
    per = DESTS // groups
    lanes = in_ref.shape[2]
    source = lax.broadcasted_iota(jnp.int32, (1, per * block), 1)
    sender = lax.div(source, block)
    rest = source - sender * block
    cut_of = lax.div(rest, 2 * width)
    rest = rest - cut_of * (2 * width)
    half = lax.div(rest, width)
    place = half * (per * width) + sender * width + rest - half * width
    moves = [one_hot(2 * per * width, jnp.where(cut_of == cut, place, -1)) for cut in range(cuts)]
    for group in range(groups):
        piece = in_ref[group * per : (group + 1) * per].reshape(per * block, lanes)
        for cut, move in enumerate(moves):
            moved = jnp.dot(move, piece, preferred_element_type=f32).astype(bf16)
            there = slice(cut * lanes, (cut + 1) * lanes)
            if len(outs) == 2:
                here = slice(group * per * width, (group + 1) * per * width)
                outs[0][here, there] = moved[: per * width]
                outs[1][here, there] = moved[per * width :]
            else:
                outs[0][group * 2 * per * width : (group + 1) * 2 * per * width, there] = moved


def gathered(arrived, width, features, parts):
    rows = DESTS * width
    return pl.pallas_call(
        functools.partial(gather_kernel, width),
        out_shape=(jax.ShapeDtypeStruct((2 * rows // parts, features), bf16),) * parts,
        in_specs=[VMEM],
        out_specs=(VMEM,) * parts,
        compiler_params=params(32),
        cost_estimate=pl.CostEstimate(flops=1, bytes_accessed=1, transcendentals=0),
    )(arrived)


def thirds(value):
    high = value.astype(bf16)
    rest = value - high.astype(f32)
    middle = rest.astype(bf16)
    low = (rest - middle.astype(f32)).astype(bf16)
    return jnp.concatenate([high, middle, low], axis=0)


def added(value, rows):
    return value[:rows] + value[rows : 2 * rows] + value[2 * rows :]


def stats_kernel(norm, offset, count, more, q_ref, *refs):
    panels, rows = refs[:OWNERS], refs[OWNERS : OWNERS + count]
    before = refs[OWNERS + count : OWNERS + count + 2] if more else None
    cov_ref, out_ref, held, turned, sems = refs[-5:]
    block, tile = cov_ref.shape
    panel_rows = out_ref.shape[0]
    step = pl.program_id(0)
    quarter = q_ref[0, 0]

    def columns(away):
        return pl.ds(pl.multiple_of((quarter ^ away) * block, 128), block)

    @pl.when(step == 0)
    def _():
        copies = []
        at = 0
        for number, row in enumerate(rows):
            size = row.shape[0]
            copy = pltpu.make_async_copy(row, held.at[at : at + size, :], sems.at[number])
            copy.start()
            copies.append((copy, at, size))
            at += size
        for copy, at, size in copies:
            copy.wait()
        turned[...] = held[:, columns(0)].T

    tile_at = pl.ds(pl.multiple_of(step * tile, 128), tile)
    cov = jnp.dot(turned[...], held[:, tile_at], preferred_element_type=f32) * norm
    cov_ref[...] = cov + before[0][...] if more else cov

    @pl.when(step == pl.num_programs(0) - 1)
    def _():
        share = None
        for away in range(OWNERS):
            part = lax.dot_general(
                thirds(panels[away][:, offset : offset + block]),
                held[:, columns(away)],
                (((1,), (1,)), ((), ())),
                preferred_element_type=f32,
            )
            share = part if share is None else share + part
        product = jnp.dot(thirds(added(share, panel_rows)), held[:, columns(0)], preferred_element_type=f32)
        result = added(product, panel_rows) * norm
        out_ref[...] = result + before[1][...] if more else result


def stats(quarter, panels, offset, rows, norm, tile, before=None):
    features = rows[0].shape[1]
    block = features // OWNERS
    total = sum(row.shape[0] for row in rows)
    panel_rows, panel_width = panels[0].shape
    cov_spec = pl.BlockSpec((block, tile), lambda n: (0, n))
    out_spec = pl.BlockSpec((panel_rows, block), lambda n: (0, 0))
    more = before is not None
    return pl.pallas_call(
        functools.partial(stats_kernel, norm, offset, len(rows), more),
        grid=(features // tile,),
        out_shape=(
            jax.ShapeDtypeStruct((block, features), f32),
            jax.ShapeDtypeStruct((panel_rows, block), f32),
        ),
        in_specs=[SMEM]
        + [pl.BlockSpec((panel_rows, panel_width), lambda n: (0, 0))] * OWNERS
        + [HBM] * len(rows)
        + ([cov_spec, out_spec] if more else []),
        out_specs=(cov_spec, out_spec),
        scratch_shapes=[
            pltpu.VMEM((total, features), bf16),
            pltpu.VMEM((block, total), bf16),
            pltpu.SemaphoreType.DMA((len(rows),)),
        ],
        compiler_params=params(40),
        cost_estimate=pl.CostEstimate(flops=1, bytes_accessed=1, transcendentals=0),
    )(quarter, *panels, *rows, *(before or ()))


def core_swapped(value):
    return lax.ppermute(value, "core", [(0, 1), (1, 0)])


def y_moved(value, flip):
    return lax.ppermute(value, ("yh", "yl"), [(i, i ^ flip) for i in range(4)])


def along_xz(value):
    return lax.all_to_all(value, ("x", "z"), 0, 0, tiled=True)


def per_device(hidden_rows, out_grads, gates, routes, panel_a, panel_g):
    tok, slots, width_in = hidden_rows.shape
    width_out = out_grads.shape[1]
    norm = ROUTED / (tok * 256 * slots)
    routes_t = routes.T
    gates_t = gates.T
    my_half = lax.axis_index("yh").astype(jnp.int32).reshape(1, 1)
    quarter = (lax.axis_index("yl") * 2 + lax.axis_index("core")).astype(jnp.int32).reshape(1, 1)
    first, last = GRAD_FIRST[1] - GRAD_FIRST[0], GRAD_LAST[1] - GRAD_LAST[0]
    begin, rest = HIDDEN_FIRST[1] - HIDDEN_FIRST[0], HIDDEN_LAST[1] - HIDDEN_LAST[0]
    sent_a = pl.pallas_call(
        first_grads_kernel,
        out_shape=block_shape(first, width_out),
        in_specs=[SMEM, VMEM, VMEM, VMEM],
        out_specs=VMEM,
        compiler_params=params(32),
    )(my_half, routes_t, gates_t, out_grads)
    own_b, across_b = pl.pallas_call(
        last_grads_kernel,
        out_shape=(rows_shape(last, width_out),) * 2,
        in_specs=[SMEM, VMEM, VMEM, VMEM],
        out_specs=(VMEM, VMEM),
        compiler_params=params(32),
    )(my_half, routes_t, gates_t, out_grads)
    own_c, across_c, own_d, across_d = pl.pallas_call(
        hidden_kernel,
        out_shape=(rows_shape(begin, width_in),) * 2 + (rows_shape(rest, width_in),) * 2,
        in_specs=[SMEM, VMEM, VMEM],
        out_specs=(VMEM,) * 4,
        compiler_params=params(32),
    )(my_half, routes_t, hidden_rows.transpose(1, 0, 2))
    panel = jnp.concatenate([panel_a[0], panel_g[0]], axis=1)
    panels = [panel] + [
        lax.ppermute(panel, ("yl", "core"), [(i, i ^ away) for i in range(OWNERS)]) for away in range(1, OWNERS)
    ]
    sent_b = spread_rows(own_b, y_moved(across_b, 3), last)
    sent_c = spread_rows(own_c, y_moved(across_c, 3), begin)
    sent_d = spread_rows(own_d, y_moved(across_d, 3), rest)
    tie = lax.optimization_barrier

    got_a = along_xz(sent_a)
    got_a, sent_b, sent_c, sent_d, panels = tie((got_a, sent_b, sent_c, sent_d, panels))
    got_b = along_xz(sent_b)
    own_a, across_a = gathered(got_a, first, width_out, 2)
    beside_a, crossed_a = y_moved(own_a, 1), y_moved(across_a, 3)
    got_b, sent_c, beside_a, crossed_a = tie((got_b, sent_c, beside_a, crossed_a))
    got_c = along_xz(sent_c)
    relayed_a = y_moved(crossed_a, 1)
    (own_b,) = gathered(got_b, last, width_out, 1)
    beside_b = y_moved(own_b, 1)
    got_c, sent_d, relayed_a = tie((got_c, sent_d, relayed_a))
    got_d = along_xz(sent_d)
    rows_g = [own_a, beside_a, crossed_a, relayed_a, own_b, beside_b]
    rows_g = rows_g + [core_swapped(piece) for piece in rows_g]
    (own_c,) = gathered(got_c, begin, width_in, 1)
    beside_c = y_moved(own_c, 1)
    grad_cov, grad_panel = stats(quarter, panels, width_in // OWNERS, rows_g, norm, 1280)
    got_d, grad_cov, grad_panel = tie((got_d, grad_cov, grad_panel))
    (own_d,) = gathered(got_d, rest, width_in, 1)
    beside_d = y_moved(own_d, 1)
    rows_c = [own_c, beside_c, core_swapped(own_c), core_swapped(beside_c)]
    own_d, rows_c = tie((own_d, rows_c))
    partial = stats(quarter, panels, 0, rows_c, norm, 768)
    beside_d, partial = tie((beside_d, partial))
    rows_d = [own_d, beside_d, core_swapped(own_d), core_swapped(beside_d)]
    input_cov, input_panel = stats(quarter, panels, 0, rows_d, norm, 768, partial)
    return (input_cov[None], grad_cov[None], input_panel[None], grad_panel[None])


def solution(mesh):
    split = Mesh(mesh.devices.reshape(4, 2, 2, 2, Z), AXES)
    return jax.shard_map(
        per_device,
        mesh=split,
        in_specs=(
            P(AXES, None, None),
            P(AXES, None),
            P(AXES, None),
            P(AXES, None),
            P(AXES, None, None),
            P(AXES, None, None),
        ),
        out_specs=(P(AXES, None, None),) * 4,
        check_vma=False,
    )
```

time: 185 us -> 172 us (0.930)
  waiting for transfers between devices: 73.2 us -> 61 us
  local copies, waits for them, and re-layouts: 12.6 us -> 7.13 us
  starting transfers between devices: 63.6 us -> 67.3 us
    all_to_all x3 -> x4, waiting for transfers between devices: 44 us -> 4.32 us  [along_xz(): return lax.all_to_all(value, ('x', 'z'), 0, 0, tiled=True)]
    ppermute x9, waiting for transfers between devices: 29.1 us -> 54.8 us  [y_moved(): return lax.ppermute(value, ('yh', 'yl'), [(i, i ^ flip) for i in range(4)])]
    all_to_all x3 -> x4, starting transfers between devices: 28.3 us -> 35 us  [along_xz(): return lax.all_to_all(value, ('x', 'z'), 0, 0, tiled=True)]
    unnamed x40 -> x22, local copies, waits for them, and re-layouts: 12.6 us -> 7.13 us
    pallas_call x4 -> x9, Pallas kernels: 29.3 us -> 32.1 us  [the longest x3 22.5 us: stats(): pl.pallas_call(functools.partial(stats_kernel, norm, offset, len(rows), m...]
    ppermute x12 -> x10, starting transfers between devices: 18.1 us -> 15.9 us  [core_swapped(): return lax.ppermute(value, 'core', [(0, 1), (1, 0)])]
    pallas_call x3 -> x4, Pallas kernels: 4.9 us -> 2.73 us  [gathered(): pl.pallas_call(functools.partial(gather_kernel, width), out_shape=(jax.Sh...]
    ppermute x12 -> x10, waiting for transfers between devices: 0.03 us -> 1.93 us  [core_swapped(): return lax.ppermute(value, 'core', [(0, 1), (1, 0)])]
  transfers between devices with their start and end apart: 27 -> 26, of which waited for: 6 -> 9; matrix products, arithmetic and copies ran while one was open for 0% -> 0% of each run, Pallas kernels for 8% -> 17%
where the time goes in v3:
time: 172 us; the launch traced here: 171 us
  starting transfers between devices  67.3 us (39%)
  waiting for transfers between devices  61 us (35%)
  Pallas kernels  34.9 us (20%)
  local copies, waits for them, and re-layouts  7.13 us (4%)
    ppermute x9, waiting for transfers between devices, y_moved(): return lax.ppermute(value, ('yh', 'yl'), [(i, i ^ flip) for i in range(4)])  54.8 us
    all_to_all x4, starting transfers between devices, along_xz(): return lax.all_to_all(value, ('x', 'z'), 0, 0, tiled=True)  35 us
    pallas_call x3, Pallas kernels, stats(): pl.pallas_call(functools.partial(stats_kernel, norm, offset, len(rows), m...  22.5 us
    ppermute x10, starting transfers between devices, core_swapped(): return lax.ppermute(value, 'core', [(0, 1), (1, 0)])  15.9 us
    ppermute x9, starting transfers between devices, y_moved(): return lax.ppermute(value, ('yh', 'yl'), [(i, i ^ flip) for i in range(4)])  11.5 us
    unnamed x22, local copies, waits for them, and re-layouts  7.13 us
    ppermute x3, starting transfers between devices, per_device(): lax.ppermute(panel, ('yl', 'core'), [(i, i ^ away) for i in range(OWNERS)])  5.01 us
    pallas_call x3, Pallas kernels, spread_rows(): pl.pallas_call(functools.partial(spread_kernel, width), out_shape=block_s...  4.48 us
  transfers between devices with their start and end apart: 26, of which 9 were waited for; matrix products, arithmetic and copies ran while one was open for 0% of the time, Pallas kernels for 17%

profile of v3, /device:TPU:1, one launch (start us, length us, event | category | flops | bytes accessed | tf_op | source)
XLA Modules:
  0.0 171.3 jit_solution(1614754393594719404)
XLA Ops:
  3.1 2.5 %shard_map.93 = bf16[32,16,1280]{2,1,0:T(8,128)(2,1)} custom-call(s32[1,1]{1,0:T(1,128)} %bitcast.1.half_ref, s32[6,128]{1,0:T(8,128)S(1)} %bitcast.12, f32[6,128]{1,0:T(8,128)S(1)} %bitcast.15, bf16[128,2560]{1,0:T(8,128)(2,1)S(1)} %copy-done), custom_call_target="tpu_custom_call" | custom-call | tf_op jit(solution)/shard_map/pallas_call | solution.py:301
  5.6 12.0 %all-to-all-start = ((bf16[32,16,1280]{2,1,0:T(8,128)(2,1)}), bf16[32,16,1280]{2,1,0:T(8,128)(2,1)S(1)}, u32[]{:S(2)}, u32[]{:S(2)}) async-start(bf16[32,16,1280]{2,1,0:T(8,128)(2,1)} %shard_map.93), calls=%async_computation | async-start | bytes 2621440 | tf_op jit(solution)/shard_map/all_to_all | solution.py:288
  17.6 1.7 copy-done.2
  19.3 2.1 %shard_map.96 = (bf16[128,1536]{1,0:T(8,128)(2,1)S(1)}, bf16[128,1536]{1,0:T(8,128)(2,1)S(1)}, bf16[64,1536]{1,0:T(8,128)(2,1)S(1)}, bf16[64,1536]{1,0:T(8,128)(2,1)S(1)}) custom-call(s32[1,1]{1,0:T(1,128)} %bitcast.1.half_ref, s32[6,128]{1,0:T(8,128)S(1)} %bitcast.13, bf16[6,128,1536]{2,1,0:T(8,128)(2,1)S(1)} %bitcast.11), custom_call_target="tpu_custom_call" | custom-call | tf_op jit(solution)/shard_map/pallas_call | solution.py:315
  21.4 2.8 %collective-permute-start.1 = (bf16[128,1536]{1,0:T(8,128)(2,1)S(1)}, bf16[128,1536]{1,0:T(8,128)(2,1)S(1)}, u32[]{:S(2)}, u32[]{:S(2)}) collective-permute-start(bf16[128,1536]{1,0:T(8,128)(2,1)S(1)} %get-tuple-element.47), channel_id=1, source_target_pairs={{0,48},{16,32},{32,16},{48,0},{1,49},{17,33},{33,17},{49,1},{2,50}... | collective-permute-start | bytes 1179656 | tf_op jit(solution)/shard_map/ppermute | solution.py:284
  24.9 2.7 %collective-permute-start.2 = (bf16[64,1536]{1,0:T(8,128)(2,1)S(1)}, bf16[64,1536]{1,0:T(8,128)(2,1)S(1)}, u32[]{:S(2)}, u32[]{:S(2)}) collective-permute-start(bf16[64,1536]{1,0:T(8,128)(2,1)S(1)} %get-tuple-element.49), channel_id=1, source_target_pairs={{0,48},{16,32},{32,16},{48,0},{1,49},{17,33},{33,17},{49,1},{2,50}... | collective-permute-start | bytes 589832 | tf_op jit(solution)/shard_map/ppermute | solution.py:284
  28.0 2.8 %collective-permute-start.4 = (f32[32,1024]{1,0:T(8,128)S(1)}, f32[32,1024]{1,0:T(8,128)S(1)}, u32[]{:S(2)}, u32[]{:S(2)}) collective-permute-start(f32[32,1024]{1,0:T(8,128)S(1)} %pad_maximum_fusion.refs_0_), channel_id=1, source_target_pairs={{0,16},{8,24},{16,0},{24,8},{1,17},{9,25},{17,1},{25,9},{2,18},{10... | collective-permute-start | bytes 393224 | tf_op jit(solution)/shard_map/ppermute | solution.py:324
  30.8 13.0 %collective-permute-done.2.across_ref = bf16[64,1536]{1,0:T(8,128)(2,1)S(1)} collective-permute-done((bf16[64,1536]{1,0:T(8,128)(2,1)S(1)}, bf16[64,1536]{1,0:T(8,128)(2,1)S(1)}, u32[]{:S(2)}, u32[]{:S(2)}) %collective-permute-start.2) | collective-permute-done | bytes 196640 | tf_op jit(solution)/shard_map/ppermute | solution.py:284
  43.8 1.8 %collective-permute-start.3 = (f32[32,1024]{1,0:T(8,128)S(1)}, f32[32,1024]{1,0:T(8,128)S(1)}, u32[]{:S(2)}, u32[]{:S(2)}) collective-permute-start(f32[32,1024]{1,0:T(8,128)S(1)} %pad_maximum_fusion.refs_0_), channel_id=1, source_target_pairs={{0,8},{8,0},{16,24},{24,16},{1,9},{9,1},{17,25},{25,17},{2,10},{10... | collective-permute-start | bytes 393224 | tf_op jit(solution)/shard_map/ppermute | solution.py:324
  45.5 1.4 shard_map.98
  46.9 1.7 shard_map.95
  48.6 1.4 shard_map.97
  50.0 9.2 %all-to-all-start.1 = ((bf16[32,16,640]{2,1,0:T(8,128)(2,1)}), bf16[32,16,640]{2,1,0:T(8,128)(2,1)S(1)}, u32[]{:S(2)}, u32[]{:S(2)}) async-start(bf16[32,16,640]{2,1,0:T(8,128)(2,1)} %shard_map.95), calls=%async_computation.1 | async-start | bytes 1310720 | tf_op jit(solution)/shard_map/all_to_all | solution.py:288
  59.3 1.3 shard_map.99
  60.6 2.7 %collective-permute-start.7 = (bf16[128,2560]{1,0:T(8,128)(2,1)S(1)}, bf16[128,2560]{1,0:T(8,128)(2,1)S(1)}, u32[]{:S(2)}, u32[]{:S(2)}) collective-permute-start(bf16[128,2560]{1,0:T(8,128)(2,1)S(1)} %get-tuple-element.58), channel_id=1, source_target_pairs={{0,48},{16,32},{32,16},{48,0},{1,49},{17,33},{33,17},{49,1},{2,50}... | collective-permute-start | bytes 1966088 | tf_op jit(solution)/shard_map/ppermute | solution.py:284
  63.3 14.6 %collective-permute-done.7.refs_6_ = bf16[128,2560]{1,0:T(8,128)(2,1)S(1)} collective-permute-done((bf16[128,2560]{1,0:T(8,128)(2,1)S(1)}, bf16[128,2560]{1,0:T(8,128)(2,1)S(1)}, u32[]{:S(2)}, u32[]{:S(2)}) %collective-permute-start.7) | collective-permute-done | bytes 655392 | tf_op jit(solution)/shard_map/ppermute | solution.py:284
  77.9 1.3 collective-permute-done.6.refs_5_
  80.1 8.9 %all-to-all-start.2 = ((bf16[32,16,768]{2,1,0:T(8,128)(2,1)}), bf16[32,16,768]{2,1,0:T(8,128)(2,1)S(1)}, u32[]{:S(2)}, u32[]{:S(2)}) async-start(bf16[32,16,768]{2,1,0:T(8,128)(2,1)} %shard_map.97), calls=%async_computation.2 | async-start | bytes 1572864 | tf_op jit(solution)/shard_map/all_to_all | solution.py:288
  89.4 2.0 %collective-permute-start.10 = (bf16[128,2560]{1,0:T(8,128)(2,1)}, bf16[128,2560]{1,0:T(8,128)(2,1)}, u32[]{:S(2)}, u32[]{:S(2)}) collective-permute-start(bf16[128,2560]{1,0:T(8,128)(2,1)} %get-tuple-element.57.refs_4_), channel_id=1, source_target_pairs={{0,8},{8,0},{1,9},{9,1},{2,10},{10,2},{3,11},{11,3},{4,12},{12,4},... | collective-permute-start | bytes 1966088 | tf_op jit(solution)/shard_map/ppermute | solution.py:280
  92.0 1.6 collective-permute-start.9
  93.8 9.6 %collective-permute-done.8.refs_7_ = bf16[128,2560]{1,0:T(8,128)(2,1)} collective-permute-done((bf16[128,2560]{1,0:T(8,128)(2,1)S(1)}, bf16[128,2560]{1,0:T(8,128)(2,1)}, u32[]{:S(2)}, u32[]{:S(2)}) %collective-permute-start.8) | collective-permute-done | bytes 655392 | tf_op jit(solution)/shard_map/ppermute | solution.py:284
  103.4 4.3 %all-to-all-done.2.in_ref = bf16[32,16,768]{2,1,0:T(8,128)(2,1)S(1)} async-done(((bf16[32,16,768]{2,1,0:T(8,128)(2,1)}), bf16[32,16,768]{2,1,0:T(8,128)(2,1)S(1)}, u32[]{:S(2)}, u32[]{:S(2)}) %all-to-all-start.2) | async-done | bytes 786464 | tf_op jit(solution)/shard_map/all_to_all | solution.py:288
  108.7 5.6 %collective-permute-start.11 = (bf16[128,2560]{1,0:T(8,128)(2,1)}, bf16[128,2560]{1,0:T(8,128)(2,1)}, u32[]{:S(2)}, u32[]{:S(2)}) collective-permute-start(bf16[128,2560]{1,0:T(8,128)(2,1)} %copy-done.5), channel_id=1, source_target_pairs={{0,8},{8,0},{1,9},{9,1},{2,10},{10,2},{3,11},{11,3},{4,12},{12,4},... | collective-permute-start | bytes 1966088 | tf_op jit(solution)/shard_map/ppermute | solution.py:280
  114.3 4.8 %all-to-all-start.3 = ((bf16[32,16,384]{2,1,0:T(8,128)(2,1)}), bf16[32,16,384]{2,1,0:T(8,128)(2,1)S(1)}, u32[]{:S(2)}, u32[]{:S(2)}) async-start(bf16[32,16,384]{2,1,0:T(8,128)(2,1)} %shard_map.98), calls=%async_computation.3 | async-start | bytes 786432 | tf_op jit(solution)/shard_map/all_to_all | solution.py:288
  119.5 3.4 %collective-permute-start.15 = (bf16[128,2560]{1,0:T(8,128)(2,1)}, bf16[128,2560]{1,0:T(8,128)(2,1)}, u32[]{:S(2)}, u32[]{:S(2)}) collective-permute-start(bf16[128,2560]{1,0:T(8,128)(2,1)} %collective-permute-done.9.refs_9_), channel_id=1, source_target_pairs={{0,8},{8,0},{1,9},{9,1},{2,10},{10,2},{3,11},{11,3},{4,12},{12,4},... | collective-permute-start | bytes 1966088 | tf_op jit(solution)/shard_map/ppermute | solution.py:280
  123.4 10.7 %collective-permute-done.16.refs_5_ = bf16[256,1536]{1,0:T(8,128)(2,1)S(1)} collective-permute-done((bf16[256,1536]{1,0:T(8,128)(2,1)S(1)}, bf16[256,1536]{1,0:T(8,128)(2,1)S(1)}, u32[]{:S(2)}, u32[]{:S(2)}) %collective-permute-start.16) | collective-permute-done | bytes 786464 | tf_op jit(solution)/shard_map/ppermute | solution.py:284
  134.1 3.0 %collective-permute-start.18 = (bf16[256,1536]{1,0:T(8,128)(2,1)S(1)}, bf16[256,1536]{1,0:T(8,128)(2,1)}, u32[]{:S(2)}, u32[]{:S(2)}) collective-permute-start(bf16[256,1536]{1,0:T(8,128)(2,1)S(1)} %collective-permute-done.16.refs_5_), channel_id=1, source_target_pairs={{0,8},{8,0},{1,9},{9,1},{2,10},{10,2},{3,11},{11,3},{4,12},{12,4},... | collective-permute-start | bytes 2359304 | tf_op jit(solution)/shard_map/ppermute | solution.py:280
  139.3 13.7 %shard_map.101 = (f32[640,2560]{1,0:T(8,128)}, f32[32,640]{1,0:T(8,128)}) custom-call(s32[1,1]{1,0:T(1,128)} %bitcast.q_ref, f32[32,1024]{1,0:T(8,128)S(1)} %pad_maximum_fusion.refs_0_, f32[32,1024]{1,0:T(8,128)S(1)} %collective-permute-done.3.refs_1_, f32[32,1024]{1,0:T(8,128)S(1)} %collective-permute-done.4.refs_2_, ...), custom_call_target="tpu_custom_call" | custom-call | flops 1 | bytes 1 | tf_op jit(solution)/shard_map/pallas_call | solution.py:257
  154.1 4.9 %shard_map.104 = (f32[384,1536]{1,0:T(8,128)S(1)}, f32[32,384]{1,0:T(8,128)S(1)}) custom-call(s32[1,1]{1,0:T(1,128)} %bitcast.q_ref, f32[32,1024]{1,0:T(8,128)S(1)} %pad_maximum_fusion.refs_0_, f32[32,1024]{1,0:T(8,128)S(1)} %collective-permute-done.3.refs_1_, f32[32,1024]{1,0:T(8,128)S(1)} %collective-permute-done.4.refs_2_, ...), custom_call_target="tpu_custom_call" | custom-call | flops 1 | bytes 1 | tf_op jit(solution)/shard_map/pallas_call | solution.py:257
  158.9 5.6 %collective-permute-done.19.refs_5_ = bf16[128,1536]{1,0:T(8,128)(2,1)S(1)} collective-permute-done((bf16[128,1536]{1,0:T(8,128)(2,1)S(1)}, bf16[128,1536]{1,0:T(8,128)(2,1)S(1)}, u32[]{:S(2)}, u32[]{:S(2)}) %collective-permute-start.19) | collective-permute-done | bytes 393248 | tf_op jit(solution)/shard_map/ppermute | solution.py:284
  165.3 1.3 collective-permute-done.21.refs_7_
  167.2 4.0 %shard_map.105 = (f32[384,1536]{1,0:T(8,128)}, f32[32,384]{1,0:T(8,128)}) custom-call(s32[1,1]{1,0:T(1,128)} %bitcast.q_ref, f32[32,1024]{1,0:T(8,128)S(1)} %pad_maximum_fusion.refs_0_, f32[32,1024]{1,0:T(8,128)S(1)} %collective-permute-done.3.refs_1_, f32[32,1024]{1,0:T(8,128)S(1)} %collective-permute-done.4.refs_2_, ...), custom_call_target="tpu_custom_call" | custom-call | flops 1 | bytes 1 | tf_op jit(solution)/shard_map/pallas_call | solution.py:257
  (56 shorter events, 12.1 us)
Async XLA Ops:
  0.6 1.1 copy-start
  5.6 18.6 %copy-start.1 = (bf16[128,2560]{1,0:T(8,128)(2,1)S(1)}, bf16[128,2560]{1,0:T(8,128)(2,1)}, u32[]{:S(2)}) copy-start(bf16[128,2560]{1,0:T(8,128)(2,1)} %grads_ref.3) | copy-start | bytes 1966084
  5.6 21.9 %copy-start.9 = (f32[1,32,640]{2,1,0:T(8,128)S(1)}, f32[1,32,640]{2,1,0:T(8,128)}, u32[]{:S(2)}) copy-start(f32[1,32,640]{2,1,0:T(8,128)} %param.11) | copy-start | bytes 245764
  5.6 21.9 %copy-start.10 = (f32[1,32,384]{2,1,0:T(8,128)S(1)}, f32[1,32,384]{2,1,0:T(8,128)}, u32[]{:S(2)}) copy-start(f32[1,32,384]{2,1,0:T(8,128)} %param.10) | copy-start | bytes 147460
  5.6 44.4 %all-to-all-start = ((bf16[32,16,1280]{2,1,0:T(8,128)(2,1)}), bf16[32,16,1280]{2,1,0:T(8,128)(2,1)S(1)}, u32[]{:S(2)}, u32[]{:S(2)}) async-start(bf16[32,16,1280]{2,1,0:T(8,128)(2,1)} %shard_map.93), calls=%async_computation | async-start | bytes 2621440 | tf_op jit(solution)/shard_map/all_to_all | solution.py:288
  17.6 1.7 copy-start.2
  21.4 27.2 %collective-permute-start.1 = (bf16[128,1536]{1,0:T(8,128)(2,1)S(1)}, bf16[128,1536]{1,0:T(8,128)(2,1)S(1)}, u32[]{:S(2)}, u32[]{:S(2)}) collective-permute-start(bf16[128,1536]{1,0:T(8,128)(2,1)S(1)} %get-tuple-element.47), channel_id=1, source_target_pairs={{0,48},{16,32},{32,16},{48,0},{1,49},{17,33},{33,17},{49,1},{2,50}... | collective-permute-start | bytes 1179656 | tf_op jit(solution)/shard_map/ppermute | solution.py:284
  24.8 22.1 %collective-permute-start = (bf16[64,2560]{1,0:T(8,128)(2,1)S(1)}, bf16[64,2560]{1,0:T(8,128)(2,1)S(1)}, u32[]{:S(2)}, u32[]{:S(2)}) collective-permute-start(bf16[64,2560]{1,0:T(8,128)(2,1)S(1)} %get-tuple-element.45), channel_id=1, source_target_pairs={{0,48},{16,32},{32,16},{48,0},{1,49},{17,33},{33,17},{49,1},{2,50}... | collective-permute-start | bytes 983048 | tf_op jit(solution)/shard_map/ppermute | solution.py:284
  24.9 18.9 %collective-permute-start.2 = (bf16[64,1536]{1,0:T(8,128)(2,1)S(1)}, bf16[64,1536]{1,0:T(8,128)(2,1)S(1)}, u32[]{:S(2)}, u32[]{:S(2)}) collective-permute-start(bf16[64,1536]{1,0:T(8,128)(2,1)S(1)} %get-tuple-element.49), channel_id=1, source_target_pairs={{0,48},{16,32},{32,16},{48,0},{1,49},{17,33},{33,17},{49,1},{2,50}... | collective-permute-start | bytes 589832 | tf_op jit(solution)/shard_map/ppermute | solution.py:284
  27.5 22.5 %collective-permute-start.5 = (f32[32,1024]{1,0:T(8,128)S(1)}, f32[32,1024]{1,0:T(8,128)S(1)}, u32[]{:S(2)}, u32[]{:S(2)}) collective-permute-start(f32[32,1024]{1,0:T(8,128)S(1)} %pad_maximum_fusion.refs_0_), channel_id=1, source_target_pairs={{0,24},{8,16},{16,8},{24,0},{1,25},{9,17},{17,9},{25,1},{2,26},{10... | collective-permute-start | bytes 393224 | tf_op jit(solution)/shard_map/ppermute | solution.py:324
  28.0 22.1 %collective-permute-start.4 = (f32[32,1024]{1,0:T(8,128)S(1)}, f32[32,1024]{1,0:T(8,128)S(1)}, u32[]{:S(2)}, u32[]{:S(2)}) collective-permute-start(f32[32,1024]{1,0:T(8,128)S(1)} %pad_maximum_fusion.refs_0_), channel_id=1, source_target_pairs={{0,16},{8,24},{16,0},{24,8},{1,17},{9,25},{17,1},{25,9},{2,18},{10... | collective-permute-start | bytes 393224 | tf_op jit(solution)/shard_map/ppermute | solution.py:324
  43.8 6.3 %collective-permute-start.3 = (f32[32,1024]{1,0:T(8,128)S(1)}, f32[32,1024]{1,0:T(8,128)S(1)}, u32[]{:S(2)}, u32[]{:S(2)}) collective-permute-start(f32[32,1024]{1,0:T(8,128)S(1)} %pad_maximum_fusion.refs_0_), channel_id=1, source_target_pairs={{0,8},{8,0},{16,24},{24,16},{1,9},{9,1},{17,25},{25,17},{2,10},{10... | collective-permute-start | bytes 393224 | tf_op jit(solution)/shard_map/ppermute | solution.py:324
  50.0 29.2 %all-to-all-start.1 = ((bf16[32,16,640]{2,1,0:T(8,128)(2,1)}), bf16[32,16,640]{2,1,0:T(8,128)(2,1)S(1)}, u32[]{:S(2)}, u32[]{:S(2)}) async-start(bf16[32,16,640]{2,1,0:T(8,128)(2,1)} %shard_map.95), calls=%async_computation.1 | async-start | bytes 1310720 | tf_op jit(solution)/shard_map/all_to_all | solution.py:288
  60.6 17.2 %collective-permute-start.7 = (bf16[128,2560]{1,0:T(8,128)(2,1)S(1)}, bf16[128,2560]{1,0:T(8,128)(2,1)S(1)}, u32[]{:S(2)}, u32[]{:S(2)}) collective-permute-start(bf16[128,2560]{1,0:T(8,128)(2,1)S(1)} %get-tuple-element.58), channel_id=1, source_target_pairs={{0,48},{16,32},{32,16},{48,0},{1,49},{17,33},{33,17},{49,1},{2,50}... | collective-permute-start | bytes 1966088 | tf_op jit(solution)/shard_map/ppermute | solution.py:284
  63.3 15.9 %collective-permute-start.6 = (bf16[128,2560]{1,0:T(8,128)(2,1)}, bf16[128,2560]{1,0:T(8,128)(2,1)S(1)}, u32[]{:S(2)}, u32[]{:S(2)}) collective-permute-start(bf16[128,2560]{1,0:T(8,128)(2,1)} %get-tuple-element.57.refs_4_), channel_id=1, source_target_pairs={{0,16},{16,0},{32,48},{48,32},{1,17},{17,1},{33,49},{49,33},{2,18}... | collective-permute-start | bytes 1966088 | tf_op jit(solution)/shard_map/ppermute | solution.py:284
  77.9 25.5 %copy-start.3 = (bf16[128,2560]{1,0:T(8,128)(2,1)}, bf16[128,2560]{1,0:T(8,128)(2,1)S(1)}, u32[]{:S(2)}) copy-start(bf16[128,2560]{1,0:T(8,128)(2,1)S(1)} %collective-permute-done.7.refs_6_) | copy-start | bytes 1966084
  80.1 27.6 %all-to-all-start.2 = ((bf16[32,16,768]{2,1,0:T(8,128)(2,1)}), bf16[32,16,768]{2,1,0:T(8,128)(2,1)S(1)}, u32[]{:S(2)}, u32[]{:S(2)}) async-start(bf16[32,16,768]{2,1,0:T(8,128)(2,1)} %shard_map.97), calls=%async_computation.2 | async-start | bytes 1572864 | tf_op jit(solution)/shard_map/all_to_all | solution.py:288
  89.0 14.4 %collective-permute-start.8 = (bf16[128,2560]{1,0:T(8,128)(2,1)S(1)}, bf16[128,2560]{1,0:T(8,128)(2,1)}, u32[]{:S(2)}, u32[]{:S(2)}) collective-permute-start(bf16[128,2560]{1,0:T(8,128)(2,1)S(1)} %collective-permute-done.7.refs_6_), channel_id=1, source_target_pairs={{0,16},{16,0},{32,48},{48,32},{1,17},{17,1},{33,49},{49,33},{2,18}... | collective-permute-start | bytes 1966088 | tf_op jit(solution)/shard_map/ppermute | solution.py:284
  89.4 29.8 %collective-permute-start.10 = (bf16[128,2560]{1,0:T(8,128)(2,1)}, bf16[128,2560]{1,0:T(8,128)(2,1)}, u32[]{:S(2)}, u32[]{:S(2)}) collective-permute-start(bf16[128,2560]{1,0:T(8,128)(2,1)} %get-tuple-element.57.refs_4_), channel_id=1, source_target_pairs={{0,8},{8,0},{1,9},{9,1},{2,10},{10,2},{3,11},{11,3},{4,12},{12,4},... | collective-permute-start | bytes 1966088 | tf_op jit(solution)/shard_map/ppermute | solution.py:280
  92.0 27.6 %collective-permute-start.9 = (bf16[128,2560]{1,0:T(8,128)(2,1)S(1)}, bf16[128,2560]{1,0:T(8,128)(2,1)}, u32[]{:S(2)}, u32[]{:S(2)}) collective-permute-start(bf16[128,2560]{1,0:T(8,128)(2,1)S(1)} %shard_map.100.refs_8_), channel_id=1, source_target_pairs={{0,16},{16,0},{32,48},{48,32},{1,17},{17,1},{33,49},{49,33},{2,18}... | collective-permute-start | bytes 1966088 | tf_op jit(solution)/shard_map/ppermute | solution.py:284
  93.5 29.4 %collective-permute-start.14 = (bf16[128,2560]{1,0:T(8,128)(2,1)S(1)}, bf16[128,2560]{1,0:T(8,128)(2,1)}, u32[]{:S(2)}, u32[]{:S(2)}) collective-permute-start(bf16[128,2560]{1,0:T(8,128)(2,1)S(1)} %shard_map.100.refs_8_), channel_id=1, source_target_pairs={{0,8},{8,0},{1,9},{9,1},{2,10},{10,2},{3,11},{11,3},{4,12},{12,4},... | collective-permute-start | bytes 1966088 | tf_op jit(solution)/shard_map/ppermute | solution.py:280
  108.1 26.1 %collective-permute-start.16 = (bf16[256,1536]{1,0:T(8,128)(2,1)S(1)}, bf16[256,1536]{1,0:T(8,128)(2,1)S(1)}, u32[]{:S(2)}, u32[]{:S(2)}) collective-permute-start(bf16[256,1536]{1,0:T(8,128)(2,1)S(1)} %shard_map.103.refs_4_), channel_id=1, source_target_pairs={{0,16},{16,0},{32,48},{48,32},{1,17},{17,1},{33,49},{49,33},{2,18}... | collective-permute-start | bytes 2359304 | tf_op jit(solution)/shard_map/ppermute | solution.py:284
  108.7 14.3 %collective-permute-start.11 = (bf16[128,2560]{1,0:T(8,128)(2,1)}, bf16[128,2560]{1,0:T(8,128)(2,1)}, u32[]{:S(2)}, u32[]{:S(2)}) collective-permute-start(bf16[128,2560]{1,0:T(8,128)(2,1)} %copy-done.5), channel_id=1, source_target_pairs={{0,8},{8,0},{1,9},{9,1},{2,10},{10,2},{3,11},{11,3},{4,12},{12,4},... | collective-permute-start | bytes 1966088 | tf_op jit(solution)/shard_map/ppermute | solution.py:280
  114.3 38.7 %all-to-all-start.3 = ((bf16[32,16,384]{2,1,0:T(8,128)(2,1)}), bf16[32,16,384]{2,1,0:T(8,128)(2,1)S(1)}, u32[]{:S(2)}, u32[]{:S(2)}) async-start(bf16[32,16,384]{2,1,0:T(8,128)(2,1)} %shard_map.98), calls=%async_computation.3 | async-start | bytes 786432 | tf_op jit(solution)/shard_map/all_to_all | solution.py:288
  119.2 18.0 %collective-permute-start.12 = (bf16[128,2560]{1,0:T(8,128)(2,1)}, bf16[128,2560]{1,0:T(8,128)(2,1)}, u32[]{:S(2)}, u32[]{:S(2)}) collective-permute-start(bf16[128,2560]{1,0:T(8,128)(2,1)} %copy-done.3), channel_id=1, source_target_pairs={{0,8},{8,0},{1,9},{9,1},{2,10},{10,2},{3,11},{11,3},{4,12},{12,4},... | collective-permute-start | bytes 1966088 | tf_op jit(solution)/shard_map/ppermute | solution.py:280
  119.5 17.6 %collective-permute-start.15 = (bf16[128,2560]{1,0:T(8,128)(2,1)}, bf16[128,2560]{1,0:T(8,128)(2,1)}, u32[]{:S(2)}, u32[]{:S(2)}) collective-permute-start(bf16[128,2560]{1,0:T(8,128)(2,1)} %collective-permute-done.9.refs_9_), channel_id=1, source_target_pairs={{0,8},{8,0},{1,9},{9,1},{2,10},{10,2},{3,11},{11,3},{4,12},{12,4},... | collective-permute-start | bytes 1966088 | tf_op jit(solution)/shard_map/ppermute | solution.py:280
  122.9 14.2 %collective-permute-start.13 = (bf16[128,2560]{1,0:T(8,128)(2,1)}, bf16[128,2560]{1,0:T(8,128)(2,1)}, u32[]{:S(2)}, u32[]{:S(2)}) collective-permute-start(bf16[128,2560]{1,0:T(8,128)(2,1)} %collective-permute-done.8.refs_7_), channel_id=1, source_target_pairs={{0,8},{8,0},{1,9},{9,1},{2,10},{10,2},{3,11},{11,3},{4,12},{12,4},... | collective-permute-start | bytes 1966088 | tf_op jit(solution)/shard_map/ppermute | solution.py:280
  122.9 31.1 %collective-permute-start.17 = (bf16[256,1536]{1,0:T(8,128)(2,1)S(1)}, bf16[256,1536]{1,0:T(8,128)(2,1)}, u32[]{:S(2)}, u32[]{:S(2)}) collective-permute-start(bf16[256,1536]{1,0:T(8,128)(2,1)S(1)} %shard_map.103.refs_4_), channel_id=1, source_target_pairs={{0,8},{8,0},{1,9},{9,1},{2,10},{10,2},{3,11},{11,3},{4,12},{12,4},... | collective-permute-start | bytes 2359304 | tf_op jit(solution)/shard_map/ppermute | solution.py:280
  134.1 19.9 %collective-permute-start.18 = (bf16[256,1536]{1,0:T(8,128)(2,1)S(1)}, bf16[256,1536]{1,0:T(8,128)(2,1)}, u32[]{:S(2)}, u32[]{:S(2)}) collective-permute-start(bf16[256,1536]{1,0:T(8,128)(2,1)S(1)} %collective-permute-done.16.refs_5_), channel_id=1, source_target_pairs={{0,8},{8,0},{1,9},{9,1},{2,10},{10,2},{3,11},{11,3},{4,12},{12,4},... | collective-permute-start | bytes 2359304 | tf_op jit(solution)/shard_map/ppermute | solution.py:280
  153.4 11.1 %collective-permute-start.19 = (bf16[128,1536]{1,0:T(8,128)(2,1)S(1)}, bf16[128,1536]{1,0:T(8,128)(2,1)S(1)}, u32[]{:S(2)}, u32[]{:S(2)}) collective-permute-start(bf16[128,1536]{1,0:T(8,128)(2,1)S(1)} %shard_map.102.refs_4_), channel_id=1, source_target_pairs={{0,16},{16,0},{32,48},{48,32},{1,17},{17,1},{33,49},{49,33},{2,18}... | collective-permute-start | bytes 1179656 | tf_op jit(solution)/shard_map/ppermute | solution.py:284
  164.5 2.1 %collective-permute-start.21 = (bf16[128,1536]{1,0:T(8,128)(2,1)S(1)}, bf16[128,1536]{1,0:T(8,128)(2,1)S(1)}, u32[]{:S(2)}, u32[]{:S(2)}) collective-permute-start(bf16[128,1536]{1,0:T(8,128)(2,1)S(1)} %collective-permute-done.19.refs_5_), channel_id=1, source_target_pairs={{0,8},{8,0},{1,9},{9,1},{2,10},{10,2},{3,11},{11,3},{4,12},{12,4},... | collective-permute-start | bytes 1179656 | tf_op jit(solution)/shard_map/ppermute | solution.py:280
  165.3 1.9 %collective-permute-start.20 = (bf16[128,1536]{1,0:T(8,128)(2,1)S(1)}, bf16[128,1536]{1,0:T(8,128)(2,1)S(1)}, u32[]{:S(2)}, u32[]{:S(2)}) collective-permute-start(bf16[128,1536]{1,0:T(8,128)(2,1)S(1)} %shard_map.102.refs_4_), channel_id=1, source_target_pairs={{0,8},{8,0},{1,9},{9,1},{2,10},{10,2},{3,11},{11,3},{4,12},{12,4},... | collective-permute-start | bytes 1179656 | tf_op jit(solution)/shard_map/ppermute | solution.py:280
  (5 other events, 4.4 us)

commit v4 on v3

--- a/solution.py
+++ b/solution.py
@@ -258,7 +258,7 @@
         functools.partial(stats_kernel, norm, offset, len(rows), more),
         grid=(features // tile,),
         out_shape=(
-            jax.ShapeDtypeStruct((block, features), f32),
+            pltpu.HBM((block, features), f32),
             jax.ShapeDtypeStruct((panel_rows, block), f32),
         ),
         in_specs=[SMEM]
@@ -271,6 +271,7 @@
             pltpu.VMEM((block, total), bf16),
             pltpu.SemaphoreType.DMA((len(rows),)),
         ],
+        input_output_aliases={1 + OWNERS + len(rows): 0, 2 + OWNERS + len(rows): 1} if more else {},
         compiler_params=params(40),
         cost_estimate=pl.CostEstimate(flops=1, bytes_accessed=1, transcendentals=0),
     )(quarter, *panels, *rows, *(before or ()))
@@ -282,6 +283,10 @@
 
 def y_moved(value, flip):
     return lax.ppermute(value, ("yh", "yl"), [(i, i ^ flip) for i in range(4)])
+
+
+def after(value, *events):
+    return lax.optimization_barrier((value, events))[0]
 
 
 def along_xz(value):
@@ -326,34 +331,34 @@
     sent_b = spread_rows(own_b, y_moved(across_b, 3), last)
     sent_c = spread_rows(own_c, y_moved(across_c, 3), begin)
     sent_d = spread_rows(own_d, y_moved(across_d, 3), rest)
-    tie = lax.optimization_barrier
 
     got_a = along_xz(sent_a)
-    got_a, sent_b, sent_c, sent_d, panels = tie((got_a, sent_b, sent_c, sent_d, panels))
+    got_a, sent_b, sent_c, sent_d, panels = lax.optimization_barrier((got_a, sent_b, sent_c, sent_d, panels))
     got_b = along_xz(sent_b)
     own_a, across_a = gathered(got_a, first, width_out, 2)
     beside_a, crossed_a = y_moved(own_a, 1), y_moved(across_a, 3)
-    got_b, sent_c, beside_a, crossed_a = tie((got_b, sent_c, beside_a, crossed_a))
-    got_c = along_xz(sent_c)
+    got_c = along_xz(after(sent_c, got_b, beside_a, crossed_a))
     relayed_a = y_moved(crossed_a, 1)
     (own_b,) = gathered(got_b, last, width_out, 1)
     beside_b = y_moved(own_b, 1)
-    got_c, sent_d, relayed_a = tie((got_c, sent_d, relayed_a))
+    rows_a = [own_a, beside_a, crossed_a]
+    rows_a = rows_a + [core_swapped(piece) for piece in rows_a]
+    begun_g = stats(quarter, panels, width_in // OWNERS, after(rows_a, own_b), norm, 1280)
+    got_c, sent_d, relayed_a = lax.optimization_barrier((got_c, sent_d, relayed_a))
+    swapped_a = core_swapped(relayed_a)
     got_d = along_xz(sent_d)
-    rows_g = [own_a, beside_a, crossed_a, relayed_a, own_b, beside_b]
-    rows_g = rows_g + [core_swapped(piece) for piece in rows_g]
-    (own_c,) = gathered(got_c, begin, width_in, 1)
+    (own_c,) = gathered(after(got_c, begun_g), begin, width_in, 1)
     beside_c = y_moved(own_c, 1)
-    grad_cov, grad_panel = stats(quarter, panels, width_in // OWNERS, rows_g, norm, 1280)
-    got_d, grad_cov, grad_panel = tie((got_d, grad_cov, grad_panel))
-    (own_d,) = gathered(got_d, rest, width_in, 1)
+    rows_b = [relayed_a, swapped_a, own_b, beside_b, core_swapped(own_b), core_swapped(beside_b)]
+    grad_cov, grad_panel = stats(quarter, panels, width_in // OWNERS, rows_b, norm, 1280, begun_g)
+    (own_d,) = gathered(after(got_d, grad_cov), rest, width_in, 1)
     beside_d = y_moved(own_d, 1)
+    own_c, beside_c = after((own_c, beside_c), own_d)
     rows_c = [own_c, beside_c, core_swapped(own_c), core_swapped(beside_c)]
-    own_d, rows_c = tie((own_d, rows_c))
-    partial = stats(quarter, panels, 0, rows_c, norm, 768)
-    beside_d, partial = tie((beside_d, partial))
+    begun_h = stats(quarter, panels, 0, rows_c, norm, 768)
+    beside_d = after(beside_d, begun_h)
     rows_d = [own_d, beside_d, core_swapped(own_d), core_swapped(beside_d)]
-    input_cov, input_panel = stats(quarter, panels, 0, rows_d, norm, 768, partial)
+    input_cov, input_panel = stats(quarter, panels, 0, rows_d, norm, 768, begun_h)
     return (input_cov[None], grad_cov[None], input_panel[None], grad_panel[None])
 
 

time: 172 us -> 158 us (0.919)
  waiting for transfers between devices: 61 us -> 47.8 us
  Pallas kernels: 34.9 us -> 41 us
  starting transfers between devices: 67.3 us -> 63 us
  local copies, waits for them, and re-layouts: 7.13 us -> 4.13 us
    ppermute x9, waiting for transfers between devices: 54.8 us -> 40 us  [y_moved(): return lax.ppermute(value, ('yh', 'yl'), [(i, i ^ flip) for i in range(4)])]
    ppermute x10, starting transfers between devices: 15.9 us -> 8.24 us  [core_swapped(): return lax.ppermute(value, 'core', [(0, 1), (1, 0)])]
    pallas_call x3 -> x4, Pallas kernels: 22.5 us -> 28.7 us  [stats(): pl.pallas_call(functools.partial(stats_kernel, norm, offset, len(rows), m...]
    ppermute x10, waiting for transfers between devices: 1.93 us -> 7.75 us  [core_swapped(): return lax.ppermute(value, 'core', [(0, 1), (1, 0)])]
    all_to_all x4, starting transfers between devices: 35 us -> 39.7 us  [along_xz(): return lax.all_to_all(value, ('x', 'z'), 0, 0, tiled=True)]
    all_to_all x4, waiting for transfers between devices: 4.32 us -> 0.02 us  [along_xz(): return lax.all_to_all(value, ('x', 'z'), 0, 0, tiled=True)]
    unnamed x22 -> x18, local copies, waits for them, and re-layouts: 7.13 us -> 4.13 us
  transfers between devices with their start and end apart: 26 -> 26, of which waited for: 9 -> 14; matrix products, arithmetic and copies ran while one was open for 0% -> 0% of each run, Pallas kernels for 17% -> 21%
where the time goes in v4:
time: 158 us; the launch traced here: 157 us
  starting transfers between devices  63 us (40%)
  waiting for transfers between devices  47.8 us (30%)
  Pallas kernels  41 us (26%)
  local copies, waits for them, and re-layouts  4.13 us (3%)
    ppermute x9, waiting for transfers between devices, y_moved(): return lax.ppermute(value, ('yh', 'yl'), [(i, i ^ flip) for i in range(4)])  40 us
    all_to_all x4, starting transfers between devices, along_xz(): return lax.all_to_all(value, ('x', 'z'), 0, 0, tiled=True)  39.7 us
    pallas_call x4, Pallas kernels, stats(): pl.pallas_call(functools.partial(stats_kernel, norm, offset, len(rows), m...  28.7 us
    ppermute x9, starting transfers between devices, y_moved(): return lax.ppermute(value, ('yh', 'yl'), [(i, i ^ flip) for i in range(4)])  11.5 us
    ppermute x10, starting transfers between devices, core_swapped(): return lax.ppermute(value, 'core', [(0, 1), (1, 0)])  8.24 us
    ppermute x10, waiting for transfers between devices, core_swapped(): return lax.ppermute(value, 'core', [(0, 1), (1, 0)])  7.75 us
    pallas_call x3, Pallas kernels, spread_rows(): pl.pallas_call(functools.partial(spread_kernel, width), out_shape=block_s...  4.43 us
    unnamed x18, local copies, waits for them, and re-layouts  4.13 us
  transfers between devices with their start and end apart: 26, of which 14 were waited for; matrix products, arithmetic and copies ran while one was open for 0% of the time, Pallas kernels for 21%

profile of v4, /device:TPU:1, one launch (start us, length us, event | category | flops | bytes accessed | tf_op | source)
XLA Modules:
  0.0 156.9 jit_solution(6797327554582510544)
XLA Ops:
  3.1 2.5 %shard_map.93 = bf16[32,16,1280]{2,1,0:T(8,128)(2,1)} custom-call(s32[1,1]{1,0:T(1,128)} %bitcast.1.half_ref, s32[6,128]{1,0:T(8,128)S(1)} %bitcast.12, f32[6,128]{1,0:T(8,128)S(1)} %bitcast.15, bf16[128,2560]{1,0:T(8,128)(2,1)S(1)} %copy-done), custom_call_target="tpu_custom_call" | custom-call | tf_op jit(solution)/shard_map/pallas_call | solution.py:306
  5.6 12.0 %all-to-all-start = ((bf16[32,16,1280]{2,1,0:T(8,128)(2,1)}), bf16[32,16,1280]{2,1,0:T(8,128)(2,1)S(1)}, u32[]{:S(2)}, u32[]{:S(2)}) async-start(bf16[32,16,1280]{2,1,0:T(8,128)(2,1)} %shard_map.93), calls=%async_computation | async-start | bytes 2621440 | tf_op jit(solution)/shard_map/all_to_all | solution.py:293
  17.7 1.7 %copy-done.2 = bf16[128,6,1536]{2,0,1:T(8,128)(2,1)S(1)} copy-done((bf16[128,6,1536]{2,0,1:T(8,128)(2,1)S(1)}, bf16[128,6,1536]{2,0,1:T(8,128)(2,1)}, u32[]{:S(2)}) %copy-start.2) | copy-done | bytes 2359320
  19.3 2.1 %shard_map.96 = (bf16[128,1536]{1,0:T(8,128)(2,1)S(1)}, bf16[128,1536]{1,0:T(8,128)(2,1)S(1)}, bf16[64,1536]{1,0:T(8,128)(2,1)S(1)}, bf16[64,1536]{1,0:T(8,128)(2,1)S(1)}) custom-call(s32[1,1]{1,0:T(1,128)} %bitcast.1.half_ref, s32[6,128]{1,0:T(8,128)S(1)} %bitcast.13, bf16[6,128,1536]{2,1,0:T(8,128)(2,1)S(1)} %bitcast.11), custom_call_target="tpu_custom_call" | custom-call | tf_op jit(solution)/shard_map/pallas_call | solution.py:320
  21.4 2.8 %collective-permute-start.1 = (bf16[128,1536]{1,0:T(8,128)(2,1)S(1)}, bf16[128,1536]{1,0:T(8,128)(2,1)S(1)}, u32[]{:S(2)}, u32[]{:S(2)}) collective-permute-start(bf16[128,1536]{1,0:T(8,128)(2,1)S(1)} %get-tuple-element.46), channel_id=1, source_target_pairs={{0,48},{16,32},{32,16},{48,0},{1,49},{17,33},{33,17},{49,1},{2,50}... | collective-permute-start | bytes 1179656 | tf_op jit(solution)/shard_map/ppermute | solution.py:285
  24.9 2.6 %collective-permute-start.2 = (bf16[64,1536]{1,0:T(8,128)(2,1)S(1)}, bf16[64,1536]{1,0:T(8,128)(2,1)S(1)}, u32[]{:S(2)}, u32[]{:S(2)}) collective-permute-start(bf16[64,1536]{1,0:T(8,128)(2,1)S(1)} %get-tuple-element.48), channel_id=1, source_target_pairs={{0,48},{16,32},{32,16},{48,0},{1,49},{17,33},{33,17},{49,1},{2,50}... | collective-permute-start | bytes 589832 | tf_op jit(solution)/shard_map/ppermute | solution.py:285
  27.6 1.9 %collective-permute-start.3 = (f32[32,1024]{1,0:T(8,128)S(1)}, f32[32,1024]{1,0:T(8,128)S(1)}, u32[]{:S(2)}, u32[]{:S(2)}) collective-permute-start(f32[32,1024]{1,0:T(8,128)S(1)} %pad_maximum_fusion.refs_0_), channel_id=1, source_target_pairs={{0,8},{8,0},{16,24},{24,16},{1,9},{9,1},{17,25},{25,17},{2,10},{10... | collective-permute-start | bytes 393224 | tf_op jit(solution)/shard_map/ppermute | solution.py:329
  29.5 14.3 %collective-permute-done.2.across_ref = bf16[64,1536]{1,0:T(8,128)(2,1)S(1)} collective-permute-done((bf16[64,1536]{1,0:T(8,128)(2,1)S(1)}, bf16[64,1536]{1,0:T(8,128)(2,1)S(1)}, u32[]{:S(2)}, u32[]{:S(2)}) %collective-permute-start.2) | collective-permute-done | bytes 196640 | tf_op jit(solution)/shard_map/ppermute | solution.py:285
  43.8 1.7 %collective-permute-start.5 = (f32[32,1024]{1,0:T(8,128)S(1)}, f32[32,1024]{1,0:T(8,128)S(1)}, u32[]{:S(2)}, u32[]{:S(2)}) collective-permute-start(f32[32,1024]{1,0:T(8,128)S(1)} %pad_maximum_fusion.refs_0_), channel_id=1, source_target_pairs={{0,24},{8,16},{16,8},{24,0},{1,25},{9,17},{17,9},{25,1},{2,26},{10... | collective-permute-start | bytes 393224 | tf_op jit(solution)/shard_map/ppermute | solution.py:329
  46.8 1.7 %shard_map.95 = bf16[32,16,640]{2,1,0:T(8,128)(2,1)} custom-call(bf16[64,2560]{1,0:T(8,128)(2,1)S(1)} %get-tuple-element.43.own_ref, bf16[64,2560]{1,0:T(8,128)(2,1)S(1)} %collective-permute-done.across_ref), custom_call_target="tpu_custom_call" | custom-call | flops 1 | bytes 1 | tf_op jit(solution)/shard_map/pallas_call | solution.py:143
  48.5 1.5 shard_map.97
  49.9 9.2 %all-to-all-start.1 = ((bf16[32,16,640]{2,1,0:T(8,128)(2,1)}), bf16[32,16,640]{2,1,0:T(8,128)(2,1)S(1)}, u32[]{:S(2)}, u32[]{:S(2)}) async-start(bf16[32,16,640]{2,1,0:T(8,128)(2,1)} %shard_map.95), calls=%async_computation.1 | async-start | bytes 1310720 | tf_op jit(solution)/shard_map/all_to_all | solution.py:293
  60.5 1.4 collective-permute-start.6
  62.0 2.7 %collective-permute-start.7 = (bf16[128,2560]{1,0:T(8,128)(2,1)S(1)}, bf16[128,2560]{1,0:T(8,128)(2,1)}, u32[]{:S(2)}, u32[]{:S(2)}) collective-permute-start(bf16[128,2560]{1,0:T(8,128)(2,1)S(1)} %get-tuple-element.57), channel_id=1, source_target_pairs={{0,48},{16,32},{32,16},{48,0},{1,49},{17,33},{33,17},{49,1},{2,50}... | collective-permute-start | bytes 1966088 | tf_op jit(solution)/shard_map/ppermute | solution.py:285
  64.7 11.9 %collective-permute-done.6.refs_5_ = bf16[128,2560]{1,0:T(8,128)(2,1)} collective-permute-done((bf16[128,2560]{1,0:T(8,128)(2,1)}, bf16[128,2560]{1,0:T(8,128)(2,1)}, u32[]{:S(2)}, u32[]{:S(2)}) %collective-permute-start.6) | collective-permute-done | bytes 655392 | tf_op jit(solution)/shard_map/ppermute | solution.py:285
  76.6 2.8 %collective-permute-done.7.refs_6_ = bf16[128,2560]{1,0:T(8,128)(2,1)} collective-permute-done((bf16[128,2560]{1,0:T(8,128)(2,1)S(1)}, bf16[128,2560]{1,0:T(8,128)(2,1)}, u32[]{:S(2)}, u32[]{:S(2)}) %collective-permute-start.7) | collective-permute-done | bytes 655392 | tf_op jit(solution)/shard_map/ppermute | solution.py:285
  79.3 8.9 %all-to-all-start.2 = ((bf16[32,16,768]{2,1,0:T(8,128)(2,1)}), bf16[32,16,768]{2,1,0:T(8,128)(2,1)S(1)}, u32[]{:S(2)}, u32[]{:S(2)}) async-start(bf16[32,16,768]{2,1,0:T(8,128)(2,1)} %shard_map.97), calls=%async_computation.2 | async-start | bytes 1572864 | tf_op jit(solution)/shard_map/all_to_all | solution.py:293
  88.3 1.8 %collective-permute-start.13 = (bf16[128,2560]{1,0:T(8,128)(2,1)}, bf16[128,2560]{1,0:T(8,128)(2,1)}, u32[]{:S(2)}, u32[]{:S(2)}) collective-permute-start(bf16[128,2560]{1,0:T(8,128)(2,1)} %get-tuple-element.62.refs_4_), channel_id=1, source_target_pairs={{0,8},{8,0},{1,9},{9,1},{2,10},{10,2},{3,11},{11,3},{4,12},{12,4},... | collective-permute-start | bytes 1966088 | tf_op jit(solution)/shard_map/ppermute | solution.py:281
  91.1 1.6 %collective-permute-start.10 = (bf16[128,2560]{1,0:T(8,128)(2,1)S(1)}, bf16[128,2560]{1,0:T(8,128)(2,1)}, u32[]{:S(2)}, u32[]{:S(2)}) collective-permute-start(bf16[128,2560]{1,0:T(8,128)(2,1)S(1)} %shard_map.100.refs_6_), channel_id=1, source_target_pairs={{0,16},{16,0},{32,48},{48,32},{1,17},{17,1},{33,49},{49,33},{2,18}... | collective-permute-start | bytes 1966088 | tf_op jit(solution)/shard_map/ppermute | solution.py:285
  94.0 8.8 %shard_map.101 = (f32[640,2560]{1,0:T(8,128)}, f32[32,640]{1,0:T(8,128)}) custom-call(s32[1,1]{1,0:T(1,128)} %bitcast.q_ref, f32[32,1024]{1,0:T(8,128)S(1)} %pad_maximum_fusion.refs_0_, f32[32,1024]{1,0:T(8,128)S(1)} %collective-permute-done.3.refs_1_, f32[32,1024]{1,0:T(8,128)S(1)} %collective-permute-done.4.refs_2_, ...), custom_call_target="tpu_custom_call" | custom-call | flops 1 | bytes 1 | tf_op jit(solution)/shard_map/pallas_call | solution.py:257
  102.8 4.3 %collective-permute-done.8.refs_4_ = bf16[128,2560]{1,0:T(8,128)(2,1)} collective-permute-done((bf16[128,2560]{1,0:T(8,128)(2,1)}, bf16[128,2560]{1,0:T(8,128)(2,1)}, u32[]{:S(2)}, u32[]{:S(2)}) %collective-permute-start.8) | collective-permute-done | bytes 655392 | tf_op jit(solution)/shard_map/ppermute | solution.py:285
  107.8 9.5 %all-to-all-start.3 = ((bf16[32,16,384]{2,1,0:T(8,128)(2,1)}), bf16[32,16,384]{2,1,0:T(8,128)(2,1)S(1)}, u32[]{:S(2)}, u32[]{:S(2)}) async-start(bf16[32,16,384]{2,1,0:T(8,128)(2,1)} %shard_map.98), calls=%async_computation.3 | async-start | bytes 786432 | tf_op jit(solution)/shard_map/all_to_all | solution.py:293
  117.3 1.6 %collective-permute-start.11 = (bf16[128,2560]{1,0:T(8,128)(2,1)S(1)}, bf16[128,2560]{1,0:T(8,128)(2,1)S(1)}, u32[]{:S(2)}, u32[]{:S(2)}) collective-permute-start(bf16[128,2560]{1,0:T(8,128)(2,1)S(1)} %shard_map.100.refs_6_), channel_id=1, source_target_pairs={{0,8},{8,0},{1,9},{9,1},{2,10},{10,2},{3,11},{11,3},{4,12},{12,4},... | collective-permute-start | bytes 1966088 | tf_op jit(solution)/shard_map/ppermute | solution.py:281
  118.9 2.3 %collective-permute-done.10.refs_7_ = bf16[128,2560]{1,0:T(8,128)(2,1)} collective-permute-done((bf16[128,2560]{1,0:T(8,128)(2,1)S(1)}, bf16[128,2560]{1,0:T(8,128)(2,1)}, u32[]{:S(2)}, u32[]{:S(2)}) %collective-permute-start.10) | collective-permute-done | bytes 655392 | tf_op jit(solution)/shard_map/ppermute | solution.py:285
  122.6 1.9 %collective-permute-done.12.refs_9_ = bf16[128,2560]{1,0:T(8,128)(2,1)S(1)} collective-permute-done((bf16[128,2560]{1,0:T(8,128)(2,1)}, bf16[128,2560]{1,0:T(8,128)(2,1)S(1)}, u32[]{:S(2)}, u32[]{:S(2)}) %collective-permute-start.12) | collective-permute-done | bytes 655392 | tf_op jit(solution)/shard_map/ppermute | solution.py:281
  125.4 10.4 %shard_map.102 = (f32[640,2560]{1,0:T(8,128)}, f32[32,640]{1,0:T(8,128)}) custom-call(s32[1,1]{1,0:T(1,128)} %bitcast.q_ref, f32[32,1024]{1,0:T(8,128)S(1)} %pad_maximum_fusion.refs_0_, f32[32,1024]{1,0:T(8,128)S(1)} %collective-permute-done.3.refs_1_, ...), custom_call_target="tpu_custom_call", output_to_operand_aliasing={{0}: (11, {}), {1}: (12, {})} | custom-call | flops 1 | bytes 1 | tf_op jit(solution)/shard_map/pallas_call | solution.py:257
  136.3 1.7 %collective-permute-done.17.refs_5_ = bf16[256,1536]{1,0:T(8,128)(2,1)S(1)} collective-permute-done((bf16[256,1536]{1,0:T(8,128)(2,1)S(1)}, bf16[256,1536]{1,0:T(8,128)(2,1)S(1)}, u32[]{:S(2)}, u32[]{:S(2)}) %collective-permute-start.17) | collective-permute-done | bytes 786464 | tf_op jit(solution)/shard_map/ppermute | solution.py:285
  141.9 4.5 %shard_map.105 = (f32[384,1536]{1,0:T(8,128)}, f32[32,384]{1,0:T(8,128)}) custom-call(s32[1,1]{1,0:T(1,128)} %bitcast.q_ref, f32[32,1024]{1,0:T(8,128)S(1)} %pad_maximum_fusion.refs_0_, f32[32,1024]{1,0:T(8,128)S(1)} %collective-permute-done.3.refs_1_, f32[32,1024]{1,0:T(8,128)S(1)} %collective-permute-done.4.refs_2_, ...), custom_call_target="tpu_custom_call" | custom-call | flops 1 | bytes 1 | tf_op jit(solution)/shard_map/pallas_call | solution.py:257
  146.3 2.7 %collective-permute-done.16.refs_5_ = bf16[128,1536]{1,0:T(8,128)(2,1)S(1)} collective-permute-done((bf16[128,1536]{1,0:T(8,128)(2,1)S(1)}, bf16[128,1536]{1,0:T(8,128)(2,1)S(1)}, u32[]{:S(2)}, u32[]{:S(2)}) %collective-permute-start.16) | collective-permute-done | bytes 393248 | tf_op jit(solution)/shard_map/ppermute | solution.py:285
  149.0 1.4 collective-permute-start.21
  150.4 1.3 collective-permute-done.21.refs_7_
  151.7 5.0 %shard_map.106 = (f32[384,1536]{1,0:T(8,128)}, f32[32,384]{1,0:T(8,128)}) custom-call(s32[1,1]{1,0:T(1,128)} %bitcast.q_ref, f32[32,1024]{1,0:T(8,128)S(1)} %pad_maximum_fusion.refs_0_, f32[32,1024]{1,0:T(8,128)S(1)} %collective-permute-done.3.refs_1_, f32[32,1024]{1,0:T(8,128)S(1)} %collective-permute-done.4.refs_2_, ...), custom_call_target="tpu_custom_call", output_to_operand_aliasing={{0}: (9, {}), {1}: (10, {})} | custom-call | flops 1 | bytes 1 | tf_op jit(solution)/shard_map/pallas_call | solution.py:257
  (53 shorter events, 15.4 us)
Async XLA Ops:
  0.6 17.0 %copy-start.4 = (s32[128,6]{0,1:T(8,128)S(1)}, s32[128,6]{0,1:T(8,128)}, u32[]{:S(2)}) copy-start(s32[128,6]{0,1:T(8,128)} %param.9) | copy-start | bytes 9220
  5.6 18.7 %copy-start.1 = (bf16[128,2560]{1,0:T(8,128)(2,1)S(1)}, bf16[128,2560]{1,0:T(8,128)(2,1)}, u32[]{:S(2)}) copy-start(bf16[128,2560]{1,0:T(8,128)(2,1)} %grads_ref.3) | copy-start | bytes 1966084
  5.6 18.7 %copy-start.6 = (f32[128,6]{0,1:T(8,128)S(1)}, f32[128,6]{0,1:T(8,128)}, u32[]{:S(2)}) copy-start(f32[128,6]{0,1:T(8,128)} %param.8) | copy-start | bytes 9220
  5.6 22.0 %copy-start.7 = (f32[1,32,640]{2,1,0:T(8,128)S(1)}, f32[1,32,640]{2,1,0:T(8,128)}, u32[]{:S(2)}) copy-start(f32[1,32,640]{2,1,0:T(8,128)} %param.11) | copy-start | bytes 245764
  5.6 22.0 %copy-start.8 = (f32[1,32,384]{2,1,0:T(8,128)S(1)}, f32[1,32,384]{2,1,0:T(8,128)}, u32[]{:S(2)}) copy-start(f32[1,32,384]{2,1,0:T(8,128)} %param.10) | copy-start | bytes 147460
  5.6 44.3 %all-to-all-start = ((bf16[32,16,1280]{2,1,0:T(8,128)(2,1)}), bf16[32,16,1280]{2,1,0:T(8,128)(2,1)S(1)}, u32[]{:S(2)}, u32[]{:S(2)}) async-start(bf16[32,16,1280]{2,1,0:T(8,128)(2,1)} %shard_map.93), calls=%async_computation | async-start | bytes 2621440 | tf_op jit(solution)/shard_map/all_to_all | solution.py:293
  17.6 1.7 %copy-start.2 = (bf16[128,6,1536]{2,0,1:T(8,128)(2,1)S(1)}, bf16[128,6,1536]{2,0,1:T(8,128)(2,1)}, u32[]{:S(2)}) copy-start(bf16[128,6,1536]{2,0,1:T(8,128)(2,1)} %param.6) | copy-start | bytes 7077892
  21.4 27.0 %collective-permute-start.1 = (bf16[128,1536]{1,0:T(8,128)(2,1)S(1)}, bf16[128,1536]{1,0:T(8,128)(2,1)S(1)}, u32[]{:S(2)}, u32[]{:S(2)}) collective-permute-start(bf16[128,1536]{1,0:T(8,128)(2,1)S(1)} %get-tuple-element.46), channel_id=1, source_target_pairs={{0,48},{16,32},{32,16},{48,0},{1,49},{17,33},{33,17},{49,1},{2,50}... | collective-permute-start | bytes 1179656 | tf_op jit(solution)/shard_map/ppermute | solution.py:285
  24.8 22.0 %collective-permute-start = (bf16[64,2560]{1,0:T(8,128)(2,1)S(1)}, bf16[64,2560]{1,0:T(8,128)(2,1)S(1)}, u32[]{:S(2)}, u32[]{:S(2)}) collective-permute-start(bf16[64,2560]{1,0:T(8,128)(2,1)S(1)} %get-tuple-element.44), channel_id=1, source_target_pairs={{0,48},{16,32},{32,16},{48,0},{1,49},{17,33},{33,17},{49,1},{2,50}... | collective-permute-start | bytes 983048 | tf_op jit(solution)/shard_map/ppermute | solution.py:285
  24.9 18.9 %collective-permute-start.2 = (bf16[64,1536]{1,0:T(8,128)(2,1)S(1)}, bf16[64,1536]{1,0:T(8,128)(2,1)S(1)}, u32[]{:S(2)}, u32[]{:S(2)}) collective-permute-start(bf16[64,1536]{1,0:T(8,128)(2,1)S(1)} %get-tuple-element.48), channel_id=1, source_target_pairs={{0,48},{16,32},{32,16},{48,0},{1,49},{17,33},{33,17},{49,1},{2,50}... | collective-permute-start | bytes 589832 | tf_op jit(solution)/shard_map/ppermute | solution.py:285
  27.6 22.3 %collective-permute-start.3 = (f32[32,1024]{1,0:T(8,128)S(1)}, f32[32,1024]{1,0:T(8,128)S(1)}, u32[]{:S(2)}, u32[]{:S(2)}) collective-permute-start(f32[32,1024]{1,0:T(8,128)S(1)} %pad_maximum_fusion.refs_0_), channel_id=1, source_target_pairs={{0,8},{8,0},{16,24},{24,16},{1,9},{9,1},{17,25},{25,17},{2,10},{10... | collective-permute-start | bytes 393224 | tf_op jit(solution)/shard_map/ppermute | solution.py:329
  29.5 20.5 %collective-permute-start.4 = (f32[32,1024]{1,0:T(8,128)S(1)}, f32[32,1024]{1,0:T(8,128)S(1)}, u32[]{:S(2)}, u32[]{:S(2)}) collective-permute-start(f32[32,1024]{1,0:T(8,128)S(1)} %pad_maximum_fusion.refs_0_), channel_id=1, source_target_pairs={{0,16},{8,24},{16,0},{24,8},{1,17},{9,25},{17,1},{25,9},{2,18},{10... | collective-permute-start | bytes 393224 | tf_op jit(solution)/shard_map/ppermute | solution.py:329
  43.8 6.1 %collective-permute-start.5 = (f32[32,1024]{1,0:T(8,128)S(1)}, f32[32,1024]{1,0:T(8,128)S(1)}, u32[]{:S(2)}, u32[]{:S(2)}) collective-permute-start(f32[32,1024]{1,0:T(8,128)S(1)} %pad_maximum_fusion.refs_0_), channel_id=1, source_target_pairs={{0,24},{8,16},{16,8},{24,0},{1,25},{9,17},{17,9},{25,1},{2,26},{10... | collective-permute-start | bytes 393224 | tf_op jit(solution)/shard_map/ppermute | solution.py:329
  49.9 29.4 %all-to-all-start.1 = ((bf16[32,16,640]{2,1,0:T(8,128)(2,1)}), bf16[32,16,640]{2,1,0:T(8,128)(2,1)S(1)}, u32[]{:S(2)}, u32[]{:S(2)}) async-start(bf16[32,16,640]{2,1,0:T(8,128)(2,1)} %shard_map.95), calls=%async_computation.1 | async-start | bytes 1310720 | tf_op jit(solution)/shard_map/all_to_all | solution.py:293
  60.5 16.0 %collective-permute-start.6 = (bf16[128,2560]{1,0:T(8,128)(2,1)}, bf16[128,2560]{1,0:T(8,128)(2,1)}, u32[]{:S(2)}, u32[]{:S(2)}) collective-permute-start(bf16[128,2560]{1,0:T(8,128)(2,1)} %get-tuple-element.62.refs_4_), channel_id=1, source_target_pairs={{0,16},{16,0},{32,48},{48,32},{1,17},{17,1},{33,49},{49,33},{2,18}... | collective-permute-start | bytes 1966088 | tf_op jit(solution)/shard_map/ppermute | solution.py:285
  62.0 17.4 %collective-permute-start.7 = (bf16[128,2560]{1,0:T(8,128)(2,1)S(1)}, bf16[128,2560]{1,0:T(8,128)(2,1)}, u32[]{:S(2)}, u32[]{:S(2)}) collective-permute-start(bf16[128,2560]{1,0:T(8,128)(2,1)S(1)} %get-tuple-element.57), channel_id=1, source_target_pairs={{0,48},{16,32},{32,16},{48,0},{1,49},{17,33},{33,17},{49,1},{2,50}... | collective-permute-start | bytes 1966088 | tf_op jit(solution)/shard_map/ppermute | solution.py:285
  79.3 27.8 %all-to-all-start.2 = ((bf16[32,16,768]{2,1,0:T(8,128)(2,1)}), bf16[32,16,768]{2,1,0:T(8,128)(2,1)S(1)}, u32[]{:S(2)}, u32[]{:S(2)}) async-start(bf16[32,16,768]{2,1,0:T(8,128)(2,1)} %shard_map.97), calls=%async_computation.2 | async-start | bytes 1572864 | tf_op jit(solution)/shard_map/all_to_all | solution.py:293
  88.3 4.5 %collective-permute-start.13 = (bf16[128,2560]{1,0:T(8,128)(2,1)}, bf16[128,2560]{1,0:T(8,128)(2,1)}, u32[]{:S(2)}, u32[]{:S(2)}) collective-permute-start(bf16[128,2560]{1,0:T(8,128)(2,1)} %get-tuple-element.62.refs_4_), channel_id=1, source_target_pairs={{0,8},{8,0},{1,9},{9,1},{2,10},{10,2},{3,11},{11,3},{4,12},{12,4},... | collective-permute-start | bytes 1966088 | tf_op jit(solution)/shard_map/ppermute | solution.py:281
  90.0 3.0 %collective-permute-start.14 = (bf16[128,2560]{1,0:T(8,128)(2,1)}, bf16[128,2560]{1,0:T(8,128)(2,1)}, u32[]{:S(2)}, u32[]{:S(2)}) collective-permute-start(bf16[128,2560]{1,0:T(8,128)(2,1)} %collective-permute-done.6.refs_5_), channel_id=1, source_target_pairs={{0,8},{8,0},{1,9},{9,1},{2,10},{10,2},{3,11},{11,3},{4,12},{12,4},... | collective-permute-start | bytes 1966088 | tf_op jit(solution)/shard_map/ppermute | solution.py:281
  90.2 3.8 %collective-permute-start.15 = (bf16[128,2560]{1,0:T(8,128)(2,1)}, bf16[128,2560]{1,0:T(8,128)(2,1)}, u32[]{:S(2)}, u32[]{:S(2)}) collective-permute-start(bf16[128,2560]{1,0:T(8,128)(2,1)} %collective-permute-done.7.refs_6_), channel_id=1, source_target_pairs={{0,8},{8,0},{1,9},{9,1},{2,10},{10,2},{3,11},{11,3},{4,12},{12,4},... | collective-permute-start | bytes 1966088 | tf_op jit(solution)/shard_map/ppermute | solution.py:281
  90.6 16.6 %collective-permute-start.8 = (bf16[128,2560]{1,0:T(8,128)(2,1)}, bf16[128,2560]{1,0:T(8,128)(2,1)}, u32[]{:S(2)}, u32[]{:S(2)}) collective-permute-start(bf16[128,2560]{1,0:T(8,128)(2,1)} %collective-permute-done.7.refs_6_), channel_id=1, source_target_pairs={{0,16},{16,0},{32,48},{48,32},{1,17},{17,1},{33,49},{49,33},{2,18}... | collective-permute-start | bytes 1966088 | tf_op jit(solution)/shard_map/ppermute | solution.py:285
  91.1 30.1 %collective-permute-start.10 = (bf16[128,2560]{1,0:T(8,128)(2,1)S(1)}, bf16[128,2560]{1,0:T(8,128)(2,1)}, u32[]{:S(2)}, u32[]{:S(2)}) collective-permute-start(bf16[128,2560]{1,0:T(8,128)(2,1)S(1)} %shard_map.100.refs_6_), channel_id=1, source_target_pairs={{0,16},{16,0},{32,48},{48,32},{1,17},{17,1},{33,49},{49,33},{2,18}... | collective-permute-start | bytes 1966088 | tf_op jit(solution)/shard_map/ppermute | solution.py:285
  107.6 30.4 %collective-permute-start.17 = (bf16[256,1536]{1,0:T(8,128)(2,1)S(1)}, bf16[256,1536]{1,0:T(8,128)(2,1)S(1)}, u32[]{:S(2)}, u32[]{:S(2)}) collective-permute-start(bf16[256,1536]{1,0:T(8,128)(2,1)S(1)} %shard_map.104.refs_4_), channel_id=1, source_target_pairs={{0,16},{16,0},{32,48},{48,32},{1,17},{17,1},{33,49},{49,33},{2,18}... | collective-permute-start | bytes 2359304 | tf_op jit(solution)/shard_map/ppermute | solution.py:285
  107.8 28.0 %all-to-all-start.3 = ((bf16[32,16,384]{2,1,0:T(8,128)(2,1)}), bf16[32,16,384]{2,1,0:T(8,128)(2,1)S(1)}, u32[]{:S(2)}, u32[]{:S(2)}) async-start(bf16[32,16,384]{2,1,0:T(8,128)(2,1)} %shard_map.98), calls=%async_computation.3 | async-start | bytes 786432 | tf_op jit(solution)/shard_map/all_to_all | solution.py:293
  117.3 5.2 %collective-permute-start.11 = (bf16[128,2560]{1,0:T(8,128)(2,1)S(1)}, bf16[128,2560]{1,0:T(8,128)(2,1)S(1)}, u32[]{:S(2)}, u32[]{:S(2)}) collective-permute-start(bf16[128,2560]{1,0:T(8,128)(2,1)S(1)} %shard_map.100.refs_6_), channel_id=1, source_target_pairs={{0,8},{8,0},{1,9},{9,1},{2,10},{10,2},{3,11},{11,3},{4,12},{12,4},... | collective-permute-start | bytes 1966088 | tf_op jit(solution)/shard_map/ppermute | solution.py:281
  121.2 3.3 %collective-permute-start.12 = (bf16[128,2560]{1,0:T(8,128)(2,1)}, bf16[128,2560]{1,0:T(8,128)(2,1)S(1)}, u32[]{:S(2)}, u32[]{:S(2)}) collective-permute-start(bf16[128,2560]{1,0:T(8,128)(2,1)} %collective-permute-done.10.refs_7_), channel_id=1, source_target_pairs={{0,8},{8,0},{1,9},{9,1},{2,10},{10,2},{3,11},{11,3},{4,12},{12,4},... | collective-permute-start | bytes 1966088 | tf_op jit(solution)/shard_map/ppermute | solution.py:281
  122.6 2.9 %collective-permute-start.9 = (bf16[128,2560]{1,0:T(8,128)(2,1)}, bf16[128,2560]{1,0:T(8,128)(2,1)S(1)}, u32[]{:S(2)}, u32[]{:S(2)}) collective-permute-start(bf16[128,2560]{1,0:T(8,128)(2,1)} %collective-permute-done.8.refs_4_), channel_id=1, source_target_pairs={{0,8},{8,0},{1,9},{9,1},{2,10},{10,2},{3,11},{11,3},{4,12},{12,4},... | collective-permute-start | bytes 1966088 | tf_op jit(solution)/shard_map/ppermute | solution.py:281
  138.0 2.8 %collective-permute-start.18 = (bf16[256,1536]{1,0:T(8,128)(2,1)S(1)}, bf16[256,1536]{1,0:T(8,128)(2,1)S(1)}, u32[]{:S(2)}, u32[]{:S(2)}) collective-permute-start(bf16[256,1536]{1,0:T(8,128)(2,1)S(1)} %shard_map.104.refs_4_), channel_id=1, source_target_pairs={{0,8},{8,0},{1,9},{9,1},{2,10},{10,2},{3,11},{11,3},{4,12},{12,4},... | collective-permute-start | bytes 2359304 | tf_op jit(solution)/shard_map/ppermute | solution.py:281
  138.8 3.0 %collective-permute-start.19 = (bf16[256,1536]{1,0:T(8,128)(2,1)S(1)}, bf16[256,1536]{1,0:T(8,128)(2,1)S(1)}, u32[]{:S(2)}, u32[]{:S(2)}) collective-permute-start(bf16[256,1536]{1,0:T(8,128)(2,1)S(1)} %collective-permute-done.17.refs_5_), channel_id=1, source_target_pairs={{0,8},{8,0},{1,9},{9,1},{2,10},{10,2},{3,11},{11,3},{4,12},{12,4},... | collective-permute-start | bytes 2359304 | tf_op jit(solution)/shard_map/ppermute | solution.py:281
  138.8 10.2 %collective-permute-start.16 = (bf16[128,1536]{1,0:T(8,128)(2,1)S(1)}, bf16[128,1536]{1,0:T(8,128)(2,1)S(1)}, u32[]{:S(2)}, u32[]{:S(2)}) collective-permute-start(bf16[128,1536]{1,0:T(8,128)(2,1)S(1)} %shard_map.103.refs_4_), channel_id=1, source_target_pairs={{0,16},{16,0},{32,48},{48,32},{1,17},{17,1},{33,49},{49,33},{2,18}... | collective-permute-start | bytes 1179656 | tf_op jit(solution)/shard_map/ppermute | solution.py:285
  138.8 11.5 %collective-permute-start.20 = (bf16[128,1536]{1,0:T(8,128)(2,1)S(1)}, bf16[128,1536]{1,0:T(8,128)(2,1)S(1)}, u32[]{:S(2)}, u32[]{:S(2)}) collective-permute-start(bf16[128,1536]{1,0:T(8,128)(2,1)S(1)} %shard_map.103.refs_4_), channel_id=1, source_target_pairs={{0,8},{8,0},{1,9},{9,1},{2,10},{10,2},{3,11},{11,3},{4,12},{12,4},... | collective-permute-start | bytes 1179656 | tf_op jit(solution)/shard_map/ppermute | solution.py:281
  149.0 2.7 %collective-permute-start.21 = (bf16[128,1536]{1,0:T(8,128)(2,1)S(1)}, bf16[128,1536]{1,0:T(8,128)(2,1)S(1)}, u32[]{:S(2)}, u32[]{:S(2)}) collective-permute-start(bf16[128,1536]{1,0:T(8,128)(2,1)S(1)} %collective-permute-done.16.refs_5_), channel_id=1, source_target_pairs={{0,8},{8,0},{1,9},{9,1},{2,10},{10,2},{3,11},{11,3},{4,12},{12,4},... | collective-permute-start | bytes 1179656 | tf_op jit(solution)/shard_map/ppermute | solution.py:281
  (3 other events, 2.5 us)

commit v5 on v4

--- a/solution.py
+++ b/solution.py
@@ -17,8 +17,7 @@
 SPLITS = {2: (4, 1), 4: (2, 2), 6: (4, 2)}
 GRAD_FIRST = (0, 4)
 GRAD_LAST = (4, 6)
-HIDDEN_FIRST = (0, 4)
-HIDDEN_LAST = (4, 6)
+HIDDEN = (0, 6)
 f32 = jnp.float32
 bf16 = jnp.bfloat16
 VMEM = pl.BlockSpec(memory_space=pltpu.VMEM)
@@ -100,29 +99,23 @@
     return (gate * picked).astype(bf16)
 
 
-def first_grads_kernel(half_ref, routes_ref, gates_ref, grads_ref, out_ref):
-    packed = packed_grads(slot_table(routes_ref), half_ref, gates_ref, grads_ref, *GRAD_FIRST)
-    rows = packed.shape[0] // 2
-    spread(packed[:rows], packed[rows:], GRAD_FIRST[1] - GRAD_FIRST[0], out_ref)
-
-
-def last_grads_kernel(half_ref, routes_ref, gates_ref, grads_ref, own_ref, across_ref):
-    packed = packed_grads(slot_table(routes_ref), half_ref, gates_ref, grads_ref, *GRAD_LAST)
-    rows = own_ref.shape[0]
-    own_ref[...] = packed[:rows]
-    across_ref[...] = packed[rows:]
-
-
-def hidden_kernel(half_ref, routes_ref, hidden_ref, *outs):
+def hidden_kernel(half_ref, routes_ref, hidden_ref, out_ref):
+    rows = FLIGHT * (HIDDEN[1] - HIDDEN[0])
+    picked = None
+    for k, target in enumerate(targets(slot_table(routes_ref), half_ref[0, 0], *HIDDEN)):
+        part = jnp.dot(one_hot(rows, target), hidden_ref[k], preferred_element_type=f32)
+        picked = part if picked is None else picked + part
+    packed = picked.astype(bf16)
+    spread(packed[: rows // 2], packed[rows // 2 :], HIDDEN[1] - HIDDEN[0], out_ref)
+
+
+def grads_kernel(half_ref, routes_ref, gates_ref, grads_ref, *outs):
     table = slot_table(routes_ref)
-    for number, (first, last) in enumerate((HIDDEN_FIRST, HIDDEN_LAST)):
-        rows = DESTS * (last - first)
-        picked = None
-        for k, target in enumerate(targets(table, half_ref[0, 0], first, last)):
-            part = jnp.dot(one_hot(2 * rows, target), hidden_ref[k], preferred_element_type=f32)
-            picked = part if picked is None else picked + part
-        outs[2 * number][...] = picked[:rows].astype(bf16)
-        outs[2 * number + 1][...] = picked[rows:].astype(bf16)
+    for number, (first, last) in enumerate((GRAD_FIRST, GRAD_LAST)):
+        packed = packed_grads(table, half_ref, gates_ref, grads_ref, first, last)
+        rows = packed.shape[0] // 2
+        outs[2 * number][...] = packed[:rows]
+        outs[2 * number + 1][...] = packed[rows:]
 
 
 def block_shape(width, features):
@@ -301,64 +294,52 @@
     gates_t = gates.T
     my_half = lax.axis_index("yh").astype(jnp.int32).reshape(1, 1)
     quarter = (lax.axis_index("yl") * 2 + lax.axis_index("core")).astype(jnp.int32).reshape(1, 1)
-    first, last = GRAD_FIRST[1] - GRAD_FIRST[0], GRAD_LAST[1] - GRAD_LAST[0]
-    begin, rest = HIDDEN_FIRST[1] - HIDDEN_FIRST[0], HIDDEN_LAST[1] - HIDDEN_LAST[0]
-    sent_a = pl.pallas_call(
-        first_grads_kernel,
-        out_shape=block_shape(first, width_out),
-        in_specs=[SMEM, VMEM, VMEM, VMEM],
+    whole, first, last = (end - start for start, end in (HIDDEN, GRAD_FIRST, GRAD_LAST))
+    sent_h = pl.pallas_call(
+        hidden_kernel,
+        out_shape=block_shape(whole, width_in),
+        in_specs=[SMEM, VMEM, VMEM],
         out_specs=VMEM,
         compiler_params=params(32),
-    )(my_half, routes_t, gates_t, out_grads)
-    own_b, across_b = pl.pallas_call(
-        last_grads_kernel,
-        out_shape=(rows_shape(last, width_out),) * 2,
+    )(my_half, routes_t, hidden_rows.transpose(1, 0, 2))
+    own_b, across_b, own_c, across_c = pl.pallas_call(
+        grads_kernel,
+        out_shape=(rows_shape(first, width_out),) * 2 + (rows_shape(last, width_out),) * 2,
         in_specs=[SMEM, VMEM, VMEM, VMEM],
-        out_specs=(VMEM, VMEM),
+        out_specs=(VMEM,) * 4,
         compiler_params=params(32),
     )(my_half, routes_t, gates_t, out_grads)
-    own_c, across_c, own_d, across_d = pl.pallas_call(
-        hidden_kernel,
-        out_shape=(rows_shape(begin, width_in),) * 2 + (rows_shape(rest, width_in),) * 2,
-        in_specs=[SMEM, VMEM, VMEM],
-        out_specs=(VMEM,) * 4,
-        compiler_params=params(32),
-    )(my_half, routes_t, hidden_rows.transpose(1, 0, 2))
     panel = jnp.concatenate([panel_a[0], panel_g[0]], axis=1)
     panels = [panel] + [
         lax.ppermute(panel, ("yl", "core"), [(i, i ^ away) for i in range(OWNERS)]) for away in range(1, OWNERS)
     ]
-    sent_b = spread_rows(own_b, y_moved(across_b, 3), last)
-    sent_c = spread_rows(own_c, y_moved(across_c, 3), begin)
-    sent_d = spread_rows(own_d, y_moved(across_d, 3), rest)
-
-    got_a = along_xz(sent_a)
-    got_a, sent_b, sent_c, sent_d, panels = lax.optimization_barrier((got_a, sent_b, sent_c, sent_d, panels))
+    sent_b = spread_rows(own_b, y_moved(across_b, 3), first)
+    sent_c = spread_rows(own_c, y_moved(across_c, 3), last)
+    at = width_in // OWNERS
+
+    got_h = along_xz(sent_h)
+    got_h, sent_b, sent_c, panels = lax.optimization_barrier((got_h, sent_b, sent_c, panels))
     got_b = along_xz(sent_b)
-    own_a, across_a = gathered(got_a, first, width_out, 2)
-    beside_a, crossed_a = y_moved(own_a, 1), y_moved(across_a, 3)
-    got_c = along_xz(after(sent_c, got_b, beside_a, crossed_a))
-    relayed_a = y_moved(crossed_a, 1)
-    (own_b,) = gathered(got_b, last, width_out, 1)
+    own_h, across_h = gathered(got_h, whole, width_in, 2)
+    beside_h, crossed_h = y_moved(own_h, 1), y_moved(across_h, 3)
+    relayed_h = y_moved(crossed_h, 1)
+    got_b = after(got_b, beside_h, relayed_h)
+    sent_c = after(sent_c, got_b)
+    rows_h = [own_h, beside_h, crossed_h, relayed_h]
+    rows_h = rows_h + [core_swapped(piece) for piece in rows_h]
+    (own_b,) = gathered(got_b, first, width_out, 1)
     beside_b = y_moved(own_b, 1)
-    rows_a = [own_a, beside_a, crossed_a]
-    rows_a = rows_a + [core_swapped(piece) for piece in rows_a]
-    begun_g = stats(quarter, panels, width_in // OWNERS, after(rows_a, own_b), norm, 1280)
-    got_c, sent_d, relayed_a = lax.optimization_barrier((got_c, sent_d, relayed_a))
-    swapped_a = core_swapped(relayed_a)
-    got_d = along_xz(sent_d)
-    (own_c,) = gathered(after(got_c, begun_g), begin, width_in, 1)
+    got_c = along_xz(sent_c)
+    input_cov, input_panel = stats(quarter, panels, 0, after(rows_h, own_b), norm, 768)
+    rows_b = after([own_b, core_swapped(own_b)], input_cov)
+    begun_g = stats(quarter, panels, at, rows_b, norm, 1280)
+    swapped_b = core_swapped(after(beside_b, begun_g))
+    (own_c,) = gathered(after(got_c, begun_g), last, width_out, 1)
     beside_c = y_moved(own_c, 1)
-    rows_b = [relayed_a, swapped_a, own_b, beside_b, core_swapped(own_b), core_swapped(beside_b)]
-    grad_cov, grad_panel = stats(quarter, panels, width_in // OWNERS, rows_b, norm, 1280, begun_g)
-    (own_d,) = gathered(after(got_d, grad_cov), rest, width_in, 1)
-    beside_d = y_moved(own_d, 1)
-    own_c, beside_c = after((own_c, beside_c), own_d)
-    rows_c = [own_c, beside_c, core_swapped(own_c), core_swapped(beside_c)]
-    begun_h = stats(quarter, panels, 0, rows_c, norm, 768)
-    beside_d = after(beside_d, begun_h)
-    rows_d = [own_d, beside_d, core_swapped(own_d), core_swapped(beside_d)]
-    input_cov, input_panel = stats(quarter, panels, 0, rows_d, norm, 768, begun_h)
+    rows_d = after([beside_b, swapped_b, own_c, core_swapped(own_c)], own_c)
+    going_g = stats(quarter, panels, at, rows_d, norm, 1280, begun_g)
+    beside_c = after(beside_c, going_g)
+    grad_cov, grad_panel = stats(quarter, panels, at, [beside_c, core_swapped(beside_c)], norm, 1280, going_g)
     return (input_cov[None], grad_cov[None], input_panel[None], grad_panel[None])
 
 

time: 158 us -> 151 us (0.956)
  starting transfers between devices: 63 us -> 45.5 us
  waiting for transfers between devices: 47.8 us -> 56.2 us
  Pallas kernels: 41 us -> 43.1 us
    all_to_all x4 -> x3, starting transfers between devices: 39.7 us -> 28.6 us  [along_xz(): return lax.all_to_all(value, ('x', 'z'), 0, 0, tiled=True)]
    ppermute x9 -> x7, waiting for transfers between devices: 40 us -> 48.7 us  [y_moved(): return lax.ppermute(value, ('yh', 'yl'), [(i, i ^ flip) for i in range(4)])]
    ppermute x9 -> x7, starting transfers between devices: 11.5 us -> 5.99 us  [y_moved(): return lax.ppermute(value, ('yh', 'yl'), [(i, i ^ flip) for i in range(4)])]
    pallas_call x4, Pallas kernels: 28.7 us -> 30.6 us  [stats(): pl.pallas_call(functools.partial(stats_kernel, norm, offset, len(rows), m...]
    pallas_call x3 -> x2, Pallas kernels: 4.43 us -> 3.56 us  [spread_rows(): pl.pallas_call(functools.partial(spread_kernel, width), out_shape=block_s...]
    pallas_call x4 -> x3, Pallas kernels: 2.73 us -> 3.29 us  [gathered(): pl.pallas_call(functools.partial(gather_kernel, width), out_shape=(jax.Sh...]
    ppermute x10 -> x8, starting transfers between devices: 8.24 us -> 7.71 us  [core_swapped(): return lax.ppermute(value, 'core', [(0, 1), (1, 0)])]
    pallas_call x3 -> x2, Pallas kernels: 5.15 us -> 5.66 us  [the longest x1 4.77 us: per_device(): pl.pallas_call(hidden_kernel, out_shape=block_shape(whole, width_in), in_...]
  transfers between devices with their start and end apart: 26 -> 21, of which waited for: 14 -> 11; matrix products, arithmetic and copies ran while one was open for 0% -> 0% of each run, Pallas kernels for 21% -> 21%
where the time goes in v5:
time: 151 us; the launch traced here: 150 us
  waiting for transfers between devices  56.2 us (37%)
  starting transfers between devices  45.5 us (30%)
  Pallas kernels  43.1 us (29%)
  local copies, waits for them, and re-layouts  4.26 us (3%)
    ppermute x7, waiting for transfers between devices, y_moved(): return lax.ppermute(value, ('yh', 'yl'), [(i, i ^ flip) for i in range(4)])  48.7 us
    pallas_call x4, Pallas kernels, stats(): pl.pallas_call(functools.partial(stats_kernel, norm, offset, len(rows), m...  30.6 us
    all_to_all x3, starting transfers between devices, along_xz(): return lax.all_to_all(value, ('x', 'z'), 0, 0, tiled=True)  28.6 us
    ppermute x8, starting transfers between devices, core_swapped(): return lax.ppermute(value, 'core', [(0, 1), (1, 0)])  7.71 us
    ppermute x8, waiting for transfers between devices, core_swapped(): return lax.ppermute(value, 'core', [(0, 1), (1, 0)])  7.53 us
    ppermute x7, starting transfers between devices, y_moved(): return lax.ppermute(value, ('yh', 'yl'), [(i, i ^ flip) for i in range(4)])  5.99 us
    pallas_call x1, Pallas kernels, per_device(): pl.pallas_call(hidden_kernel, out_shape=block_shape(whole, width_in), in_...  4.77 us
    unnamed x20, local copies, waits for them, and re-layouts  4.26 us
  transfers between devices with their start and end apart: 21, of which 11 were waited for; matrix products, arithmetic and copies ran while one was open for 0% of the time, Pallas kernels for 21%

profile of v5, /device:TPU:1, one launch (start us, length us, event | category | flops | bytes accessed | tf_op | source)
XLA Modules:
  0.0 150.0 jit_solution(5083069714134847033)
XLA Ops:
  0.6 1.7 %copy-done = bf16[128,6,1536]{2,0,1:T(8,128)(2,1)S(1)} copy-done((bf16[128,6,1536]{2,0,1:T(8,128)(2,1)S(1)}, bf16[128,6,1536]{2,0,1:T(8,128)(2,1)}, u32[]{:S(2)}) %copy-start) | copy-done | bytes 2359320
  3.0 4.8 %shard_map.93 = bf16[32,48,384]{2,1,0:T(8,128)(2,1)} custom-call(s32[1,1]{1,0:T(1,128)} %bitcast.1.half_ref, s32[6,128]{1,0:T(8,128)S(1)} %bitcast.12, bf16[6,128,1536]{2,1,0:T(8,128)(2,1)S(1)} %bitcast.11), custom_call_target="tpu_custom_call" | custom-call | tf_op jit(solution)/shard_map/pallas_call | solution.py:298
  7.8 12.0 %all-to-all-start = ((bf16[32,48,384]{2,1,0:T(8,128)(2,1)}), bf16[32,48,384]{2,1,0:T(8,128)(2,1)S(1)}, u32[]{:S(2)}, u32[]{:S(2)}) async-start(bf16[32,48,384]{2,1,0:T(8,128)(2,1)} %shard_map.93), calls=%async_computation | async-start | bytes 2359296 | tf_op jit(solution)/shard_map/all_to_all | solution.py:286
  19.8 0.9 shard_map.94
  20.7 2.8 %collective-permute-start = (bf16[128,2560]{1,0:T(8,128)(2,1)S(1)}, bf16[128,2560]{1,0:T(8,128)(2,1)S(1)}, u32[]{:S(2)}, u32[]{:S(2)}) collective-permute-start(bf16[128,2560]{1,0:T(8,128)(2,1)S(1)} %get-tuple-element.45), channel_id=1, source_target_pairs={{0,48},{16,32},{32,16},{48,0},{1,49},{17,33},{33,17},{49,1},{2,50}... | collective-permute-start | bytes 1966088 | tf_op jit(solution)/shard_map/ppermute | solution.py:278
  23.6 1.4 collective-permute-start.2
  25.2 1.6 %collective-permute-start.4 = (f32[32,1024]{1,0:T(8,128)S(1)}, f32[32,1024]{1,0:T(8,128)S(1)}, u32[]{:S(2)}, u32[]{:S(2)}) collective-permute-start(f32[32,1024]{1,0:T(8,128)S(1)} %pad_maximum_fusion.refs_0_), channel_id=1, source_target_pairs={{0,24},{8,16},{16,8},{24,0},{1,25},{9,17},{17,9},{25,1},{2,26},{10... | collective-permute-start | bytes 393224 | tf_op jit(solution)/shard_map/ppermute | solution.py:314
  26.8 17.6 %collective-permute-done.1.across_ref = bf16[64,2560]{1,0:T(8,128)(2,1)S(1)} collective-permute-done((bf16[64,2560]{1,0:T(8,128)(2,1)S(1)}, bf16[64,2560]{1,0:T(8,128)(2,1)S(1)}, u32[]{:S(2)}, u32[]{:S(2)}) %collective-permute-start.1) | collective-permute-done | bytes 327712 | tf_op jit(solution)/shard_map/ppermute | solution.py:278
  44.4 1.7 %shard_map.96 = bf16[32,16,640]{2,1,0:T(8,128)(2,1)} custom-call(bf16[64,2560]{1,0:T(8,128)(2,1)S(1)} %get-tuple-element.46.own_ref, bf16[64,2560]{1,0:T(8,128)(2,1)S(1)} %collective-permute-done.1.across_ref), custom_call_target="tpu_custom_call" | custom-call | flops 1 | bytes 1 | tf_op jit(solution)/shard_map/pallas_call | solution.py:136
  46.1 1.9 %shard_map.95 = bf16[32,16,1280]{2,1,0:T(8,128)(2,1)} custom-call(bf16[128,2560]{1,0:T(8,128)(2,1)S(1)} %get-tuple-element.44.own_ref, bf16[128,2560]{1,0:T(8,128)(2,1)S(1)} %collective-permute-done.across_ref), custom_call_target="tpu_custom_call" | custom-call | flops 1 | bytes 1 | tf_op jit(solution)/shard_map/pallas_call | solution.py:136
  48.0 8.9 %all-to-all-start.1 = ((bf16[32,16,1280]{2,1,0:T(8,128)(2,1)}), bf16[32,16,1280]{2,1,0:T(8,128)(2,1)S(1)}, u32[]{:S(2)}, u32[]{:S(2)}) async-start(bf16[32,16,1280]{2,1,0:T(8,128)(2,1)} %shard_map.95), calls=%async_computation.1 | async-start | bytes 2621440 | tf_op jit(solution)/shard_map/all_to_all | solution.py:286
  57.0 2.2 %shard_map.97 = (bf16[192,1536]{1,0:T(8,128)(2,1)}, bf16[192,1536]{1,0:T(8,128)(2,1)S(1)}) custom-call(bf16[32,48,384]{2,1,0:T(8,128)(2,1)S(1)} %all-to-all-done.in_ref), custom_call_target="tpu_custom_call" | custom-call | flops 1 | bytes 1 | tf_op jit(solution)/shard_map/pallas_call | solution.py:174
  59.2 2.6 %collective-permute-start.6 = (bf16[192,1536]{1,0:T(8,128)(2,1)S(1)}, bf16[192,1536]{1,0:T(8,128)(2,1)S(1)}, u32[]{:S(2)}, u32[]{:S(2)}) collective-permute-start(bf16[192,1536]{1,0:T(8,128)(2,1)S(1)} %get-tuple-element.54), channel_id=1, source_target_pairs={{0,48},{16,32},{32,16},{48,0},{1,49},{17,33},{33,17},{49,1},{2,50}... | collective-permute-start | bytes 1769480 | tf_op jit(solution)/shard_map/ppermute | solution.py:278
  61.8 11.1 %collective-permute-done.6.refs_6_ = bf16[192,1536]{1,0:T(8,128)(2,1)S(1)} collective-permute-done((bf16[192,1536]{1,0:T(8,128)(2,1)S(1)}, bf16[192,1536]{1,0:T(8,128)(2,1)S(1)}, u32[]{:S(2)}, u32[]{:S(2)}) %collective-permute-start.6) | collective-permute-done | bytes 589856 | tf_op jit(solution)/shard_map/ppermute | solution.py:278
  72.9 1.2 collective-permute-done.5.refs_5_
  74.1 0.8 copy-done.4
  74.9 13.1 %collective-permute-done.7.refs_7_ = bf16[192,1536]{1,0:T(8,128)(2,1)} collective-permute-done((bf16[192,1536]{1,0:T(8,128)(2,1)S(1)}, bf16[192,1536]{1,0:T(8,128)(2,1)}, u32[]{:S(2)}, u32[]{:S(2)}) %collective-permute-start.7) | collective-permute-done | bytes 589856 | tf_op jit(solution)/shard_map/ppermute | solution.py:278
  88.6 4.1 %collective-permute-start.12 = (bf16[256,2560]{1,0:T(8,128)(2,1)S(1)}, bf16[256,2560]{1,0:T(8,128)(2,1)}, u32[]{:S(2)}, u32[]{:S(2)}) collective-permute-start(bf16[256,2560]{1,0:T(8,128)(2,1)S(1)} %shard_map.98.refs_4_), channel_id=1, source_target_pairs={{0,8},{8,0},{1,9},{9,1},{2,10},{10,2},{3,11},{11,3},{4,12},{12,4},... | collective-permute-start | bytes 3932168 | tf_op jit(solution)/shard_map/ppermute | solution.py:274
  93.3 7.6 %all-to-all-start.2 = ((bf16[32,16,640]{2,1,0:T(8,128)(2,1)}), bf16[32,16,640]{2,1,0:T(8,128)(2,1)S(1)}, u32[]{:S(2)}, u32[]{:S(2)}) async-start(bf16[32,16,640]{2,1,0:T(8,128)(2,1)} %shard_map.96), calls=%async_computation.2 | async-start | bytes 1310720 | tf_op jit(solution)/shard_map/all_to_all | solution.py:286
  102.0 1.5 collective-permute-done.9.refs_9_
  103.4 1.5 collective-permute-done.10.refs_10_
  105.1 1.1 copy-done.5
  106.2 7.6 %shard_map.99 = (f32[384,1536]{1,0:T(8,128)}, f32[32,384]{1,0:T(8,128)}) custom-call(s32[1,1]{1,0:T(1,128)} %bitcast.q_ref, f32[32,1024]{1,0:T(8,128)S(1)} %pad_maximum_fusion.refs_0_, f32[32,1024]{1,0:T(8,128)S(1)} %collective-permute-done.2.refs_1_, f32[32,1024]{1,0:T(8,128)S(1)} %collective-permute-done.3.refs_2_, ...), custom_call_target="tpu_custom_call" | custom-call | flops 1 | bytes 1 | tf_op jit(solution)/shard_map/pallas_call | solution.py:250
  113.8 6.6 %shard_map.100 = (f32[640,2560]{1,0:T(8,128)}, f32[32,640]{1,0:T(8,128)}) custom-call(s32[1,1]{1,0:T(1,128)} %bitcast.q_ref, f32[32,1024]{1,0:T(8,128)S(1)} %pad_maximum_fusion.refs_0_, f32[32,1024]{1,0:T(8,128)S(1)} %collective-permute-done.2.refs_1_, f32[32,1024]{1,0:T(8,128)S(1)} %collective-permute-done.3.refs_2_, ...), custom_call_target="tpu_custom_call" | custom-call | flops 1 | bytes 1 | tf_op jit(solution)/shard_map/pallas_call | solution.py:250
  120.4 2.8 %collective-permute-done.14.refs_4_ = bf16[256,2560]{1,0:T(8,128)(2,1)} collective-permute-done((bf16[256,2560]{1,0:T(8,128)(2,1)S(1)}, bf16[256,2560]{1,0:T(8,128)(2,1)}, u32[]{:S(2)}, u32[]{:S(2)}) %collective-permute-start.14) | collective-permute-done | bytes 1310752 | tf_op jit(solution)/shard_map/ppermute | solution.py:278
  123.1 0.9 collective-permute-start.15
  125.0 2.7 %collective-permute-done.16.refs_7_ = bf16[128,2560]{1,0:T(8,128)(2,1)S(1)} collective-permute-done((bf16[128,2560]{1,0:T(8,128)(2,1)S(1)}, bf16[128,2560]{1,0:T(8,128)(2,1)S(1)}, u32[]{:S(2)}, u32[]{:S(2)}) %collective-permute-start.16) | collective-permute-done | bytes 655392 | tf_op jit(solution)/shard_map/ppermute | solution.py:274
  127.6 10.2 %shard_map.102 = (f32[640,2560]{1,0:T(8,128)}, f32[32,640]{1,0:T(8,128)}) custom-call(s32[1,1]{1,0:T(1,128)} %bitcast.q_ref, f32[32,1024]{1,0:T(8,128)S(1)} %pad_maximum_fusion.refs_0_, f32[32,1024]{1,0:T(8,128)S(1)} %collective-permute-done.2.refs_1_, f32[32,1024]{1,0:T(8,128)S(1)} %collective-permute-done.3.refs_2_, ...), custom_call_target="tpu_custom_call", output_to_operand_aliasing={{0}: (9, {}), {1}: (10, {})} | custom-call | flops 1 | bytes 1 | tf_op jit(solution)/shard_map/pallas_call | solution.py:250
  137.9 2.8 %collective-permute-done.13.refs_4_ = bf16[128,2560]{1,0:T(8,128)(2,1)S(1)} collective-permute-done((bf16[128,2560]{1,0:T(8,128)(2,1)S(1)}, bf16[128,2560]{1,0:T(8,128)(2,1)S(1)}, u32[]{:S(2)}, u32[]{:S(2)}) %collective-permute-start.13) | collective-permute-done | bytes 655392 | tf_op jit(solution)/shard_map/ppermute | solution.py:278
  140.7 1.2 collective-permute-start.17
  141.9 1.7 %collective-permute-done.17.refs_5_ = bf16[128,2560]{1,0:T(8,128)(2,1)S(1)} collective-permute-done((bf16[128,2560]{1,0:T(8,128)(2,1)S(1)}, bf16[128,2560]{1,0:T(8,128)(2,1)S(1)}, u32[]{:S(2)}, u32[]{:S(2)}) %collective-permute-start.17) | collective-permute-done | bytes 655392 | tf_op jit(solution)/shard_map/ppermute | solution.py:274
  143.7 6.2 %shard_map.103 = (f32[640,2560]{1,0:T(8,128)}, f32[32,640]{1,0:T(8,128)}) custom-call(s32[1,1]{1,0:T(1,128)} %bitcast.q_ref, f32[32,1024]{1,0:T(8,128)S(1)} %pad_maximum_fusion.refs_0_, f32[32,1024]{1,0:T(8,128)S(1)} %collective-permute-done.2.refs_1_, f32[32,1024]{1,0:T(8,128)S(1)} %collective-permute-done.3.refs_2_, ...), custom_call_target="tpu_custom_call", output_to_operand_aliasing={{0}: (7, {}), {1}: (8, {})} | custom-call | flops 1 | bytes 1 | tf_op jit(solution)/shard_map/pallas_call | solution.py:250
  (42 shorter events, 4.2 us)
Async XLA Ops:
  0.6 1.7 %copy-start = (bf16[128,6,1536]{2,0,1:T(8,128)(2,1)S(1)}, bf16[128,6,1536]{2,0,1:T(8,128)(2,1)}, u32[]{:S(2)}) copy-start(bf16[128,6,1536]{2,0,1:T(8,128)(2,1)} %param.6) | copy-start | bytes 7077892
  2.3 0.7 copy-start.6
  7.8 12.0 %copy-start.1 = (bf16[128,2560]{1,0:T(8,128)(2,1)S(1)}, bf16[128,2560]{1,0:T(8,128)(2,1)}, u32[]{:S(2)}) copy-start(bf16[128,2560]{1,0:T(8,128)(2,1)} %grads_ref.1) | copy-start | bytes 1966084
  7.8 12.0 %copy-start.7 = (f32[128,6]{0,1:T(8,128)S(1)}, f32[128,6]{0,1:T(8,128)}, u32[]{:S(2)}) copy-start(f32[128,6]{0,1:T(8,128)} %param.8) | copy-start | bytes 9220
  7.8 15.9 %copy-start.8 = (f32[1,32,640]{2,1,0:T(8,128)S(1)}, f32[1,32,640]{2,1,0:T(8,128)}, u32[]{:S(2)}) copy-start(f32[1,32,640]{2,1,0:T(8,128)} %param.11) | copy-start | bytes 245764
  7.8 15.9 %copy-start.9 = (f32[1,32,384]{2,1,0:T(8,128)S(1)}, f32[1,32,384]{2,1,0:T(8,128)}, u32[]{:S(2)}) copy-start(f32[1,32,384]{2,1,0:T(8,128)} %param.10) | copy-start | bytes 147460
  7.8 40.2 %all-to-all-start = ((bf16[32,48,384]{2,1,0:T(8,128)(2,1)}), bf16[32,48,384]{2,1,0:T(8,128)(2,1)S(1)}, u32[]{:S(2)}, u32[]{:S(2)}) async-start(bf16[32,48,384]{2,1,0:T(8,128)(2,1)} %shard_map.93), calls=%async_computation | async-start | bytes 2359296 | tf_op jit(solution)/shard_map/all_to_all | solution.py:286
  20.7 25.4 %collective-permute-start = (bf16[128,2560]{1,0:T(8,128)(2,1)S(1)}, bf16[128,2560]{1,0:T(8,128)(2,1)S(1)}, u32[]{:S(2)}, u32[]{:S(2)}) collective-permute-start(bf16[128,2560]{1,0:T(8,128)(2,1)S(1)} %get-tuple-element.45), channel_id=1, source_target_pairs={{0,48},{16,32},{32,16},{48,0},{1,49},{17,33},{33,17},{49,1},{2,50}... | collective-permute-start | bytes 1966088 | tf_op jit(solution)/shard_map/ppermute | solution.py:278
  23.5 20.9 %collective-permute-start.1 = (bf16[64,2560]{1,0:T(8,128)(2,1)S(1)}, bf16[64,2560]{1,0:T(8,128)(2,1)S(1)}, u32[]{:S(2)}, u32[]{:S(2)}) collective-permute-start(bf16[64,2560]{1,0:T(8,128)(2,1)S(1)} %get-tuple-element.47), channel_id=1, source_target_pairs={{0,48},{16,32},{32,16},{48,0},{1,49},{17,33},{33,17},{49,1},{2,50}... | collective-permute-start | bytes 983048 | tf_op jit(solution)/shard_map/ppermute | solution.py:278
  23.6 24.4 %collective-permute-start.2 = (f32[32,1024]{1,0:T(8,128)S(1)}, f32[32,1024]{1,0:T(8,128)S(1)}, u32[]{:S(2)}, u32[]{:S(2)}) collective-permute-start(f32[32,1024]{1,0:T(8,128)S(1)} %pad_maximum_fusion.refs_0_), channel_id=1, source_target_pairs={{0,8},{8,0},{16,24},{24,16},{1,9},{9,1},{17,25},{25,17},{2,10},{10... | collective-permute-start | bytes 393224 | tf_op jit(solution)/shard_map/ppermute | solution.py:314
  25.1 22.9 %collective-permute-start.3 = (f32[32,1024]{1,0:T(8,128)S(1)}, f32[32,1024]{1,0:T(8,128)S(1)}, u32[]{:S(2)}, u32[]{:S(2)}) collective-permute-start(f32[32,1024]{1,0:T(8,128)S(1)} %pad_maximum_fusion.refs_0_), channel_id=1, source_target_pairs={{0,16},{8,24},{16,0},{24,8},{1,17},{9,25},{17,1},{25,9},{2,18},{10... | collective-permute-start | bytes 393224 | tf_op jit(solution)/shard_map/ppermute | solution.py:314
  25.2 22.8 %collective-permute-start.4 = (f32[32,1024]{1,0:T(8,128)S(1)}, f32[32,1024]{1,0:T(8,128)S(1)}, u32[]{:S(2)}, u32[]{:S(2)}) collective-permute-start(f32[32,1024]{1,0:T(8,128)S(1)} %pad_maximum_fusion.refs_0_), channel_id=1, source_target_pairs={{0,24},{8,16},{16,8},{24,0},{1,25},{9,17},{17,9},{25,1},{2,26},{10... | collective-permute-start | bytes 393224 | tf_op jit(solution)/shard_map/ppermute | solution.py:314
  48.0 40.0 %all-to-all-start.1 = ((bf16[32,16,1280]{2,1,0:T(8,128)(2,1)}), bf16[32,16,1280]{2,1,0:T(8,128)(2,1)S(1)}, u32[]{:S(2)}, u32[]{:S(2)}) async-start(bf16[32,16,1280]{2,1,0:T(8,128)(2,1)} %shard_map.95), calls=%async_computation.1 | async-start | bytes 2621440 | tf_op jit(solution)/shard_map/all_to_all | solution.py:286
  59.2 13.7 %collective-permute-start.6 = (bf16[192,1536]{1,0:T(8,128)(2,1)S(1)}, bf16[192,1536]{1,0:T(8,128)(2,1)S(1)}, u32[]{:S(2)}, u32[]{:S(2)}) collective-permute-start(bf16[192,1536]{1,0:T(8,128)(2,1)S(1)} %get-tuple-element.54), channel_id=1, source_target_pairs={{0,48},{16,32},{32,16},{48,0},{1,49},{17,33},{33,17},{49,1},{2,50}... | collective-permute-start | bytes 1769480 | tf_op jit(solution)/shard_map/ppermute | solution.py:278
  61.8 12.3 %collective-permute-start.5 = (bf16[192,1536]{1,0:T(8,128)(2,1)}, bf16[192,1536]{1,0:T(8,128)(2,1)S(1)}, u32[]{:S(2)}, u32[]{:S(2)}) collective-permute-start(bf16[192,1536]{1,0:T(8,128)(2,1)} %get-tuple-element.57.refs_4_), channel_id=1, source_target_pairs={{0,16},{16,0},{32,48},{48,32},{1,17},{17,1},{33,49},{49,33},{2,18}... | collective-permute-start | bytes 1769480 | tf_op jit(solution)/shard_map/ppermute | solution.py:278
  72.9 1.3 copy-start.2
  72.9 15.2 %collective-permute-start.7 = (bf16[192,1536]{1,0:T(8,128)(2,1)S(1)}, bf16[192,1536]{1,0:T(8,128)(2,1)}, u32[]{:S(2)}, u32[]{:S(2)}) collective-permute-start(bf16[192,1536]{1,0:T(8,128)(2,1)S(1)} %collective-permute-done.6.refs_6_), channel_id=1, source_target_pairs={{0,16},{16,0},{32,48},{48,32},{1,17},{17,1},{33,49},{49,33},{2,18}... | collective-permute-start | bytes 1769480 | tf_op jit(solution)/shard_map/ppermute | solution.py:278
  74.1 0.8 copy-start.4
  88.6 12.8 %copy-start.3 = (bf16[192,1536]{1,0:T(8,128)(2,1)S(1)}, bf16[192,1536]{1,0:T(8,128)(2,1)}, u32[]{:S(2)}) copy-start(bf16[192,1536]{1,0:T(8,128)(2,1)} %copy-done.2) | copy-start | bytes 1769476
  88.6 25.1 %collective-permute-start.12 = (bf16[256,2560]{1,0:T(8,128)(2,1)S(1)}, bf16[256,2560]{1,0:T(8,128)(2,1)}, u32[]{:S(2)}, u32[]{:S(2)}) collective-permute-start(bf16[256,2560]{1,0:T(8,128)(2,1)S(1)} %shard_map.98.refs_4_), channel_id=1, source_target_pairs={{0,8},{8,0},{1,9},{9,1},{2,10},{10,2},{3,11},{11,3},{4,12},{12,4},... | collective-permute-start | bytes 3932168 | tf_op jit(solution)/shard_map/ppermute | solution.py:274
  92.7 30.4 %collective-permute-start.14 = (bf16[256,2560]{1,0:T(8,128)(2,1)S(1)}, bf16[256,2560]{1,0:T(8,128)(2,1)}, u32[]{:S(2)}, u32[]{:S(2)}) collective-permute-start(bf16[256,2560]{1,0:T(8,128)(2,1)S(1)} %shard_map.98.refs_4_), channel_id=1, source_target_pairs={{0,16},{16,0},{32,48},{48,32},{1,17},{17,1},{33,49},{49,33},{2,18}... | collective-permute-start | bytes 3932168 | tf_op jit(solution)/shard_map/ppermute | solution.py:278
  92.9 8.7 %collective-permute-start.8 = (bf16[192,1536]{1,0:T(8,128)(2,1)}, bf16[192,1536]{1,0:T(8,128)(2,1)}, u32[]{:S(2)}, u32[]{:S(2)}) collective-permute-start(bf16[192,1536]{1,0:T(8,128)(2,1)} %get-tuple-element.57.refs_4_), channel_id=1, source_target_pairs={{0,8},{8,0},{1,9},{9,1},{2,10},{10,2},{3,11},{11,3},{4,12},{12,4},... | collective-permute-start | bytes 1769480 | tf_op jit(solution)/shard_map/ppermute | solution.py:274
  93.3 30.8 %all-to-all-start.2 = ((bf16[32,16,640]{2,1,0:T(8,128)(2,1)}), bf16[32,16,640]{2,1,0:T(8,128)(2,1)S(1)}, u32[]{:S(2)}, u32[]{:S(2)}) async-start(bf16[32,16,640]{2,1,0:T(8,128)(2,1)} %shard_map.96), calls=%async_computation.2 | async-start | bytes 1310720 | tf_op jit(solution)/shard_map/all_to_all | solution.py:286
  100.9 2.5 %collective-permute-start.9 = (bf16[192,1536]{1,0:T(8,128)(2,1)}, bf16[192,1536]{1,0:T(8,128)(2,1)}, u32[]{:S(2)}, u32[]{:S(2)}) collective-permute-start(bf16[192,1536]{1,0:T(8,128)(2,1)} %copy-done.4), channel_id=1, source_target_pairs={{0,8},{8,0},{1,9},{9,1},{2,10},{10,2},{3,11},{11,3},{4,12},{12,4},... | collective-permute-start | bytes 1769480 | tf_op jit(solution)/shard_map/ppermute | solution.py:274
  101.4 3.4 %collective-permute-start.10 = (bf16[192,1536]{1,0:T(8,128)(2,1)S(1)}, bf16[192,1536]{1,0:T(8,128)(2,1)}, u32[]{:S(2)}, u32[]{:S(2)}) collective-permute-start(bf16[192,1536]{1,0:T(8,128)(2,1)S(1)} %copy-done.3), channel_id=1, source_target_pairs={{0,8},{8,0},{1,9},{9,1},{2,10},{10,2},{3,11},{11,3},{4,12},{12,4},... | collective-permute-start | bytes 1769480 | tf_op jit(solution)/shard_map/ppermute | solution.py:274
  101.6 3.5 %collective-permute-start.11 = (bf16[192,1536]{1,0:T(8,128)(2,1)}, bf16[192,1536]{1,0:T(8,128)(2,1)}, u32[]{:S(2)}, u32[]{:S(2)}) collective-permute-start(bf16[192,1536]{1,0:T(8,128)(2,1)} %collective-permute-done.7.refs_7_), channel_id=1, source_target_pairs={{0,8},{8,0},{1,9},{9,1},{2,10},{10,2},{3,11},{11,3},{4,12},{12,4},... | collective-permute-start | bytes 1769480 | tf_op jit(solution)/shard_map/ppermute | solution.py:274
  105.1 1.1 copy-start.5
  123.1 4.5 %collective-permute-start.15 = (bf16[256,2560]{1,0:T(8,128)(2,1)}, bf16[256,2560]{1,0:T(8,128)(2,1)S(1)}, u32[]{:S(2)}, u32[]{:S(2)}) collective-permute-start(bf16[256,2560]{1,0:T(8,128)(2,1)} %collective-permute-done.14.refs_4_), channel_id=1, source_target_pairs={{0,8},{8,0},{1,9},{9,1},{2,10},{10,2},{3,11},{11,3},{4,12},{12,4},... | collective-permute-start | bytes 3932168 | tf_op jit(solution)/shard_map/ppermute | solution.py:274
  124.6 3.0 %collective-permute-start.16 = (bf16[128,2560]{1,0:T(8,128)(2,1)S(1)}, bf16[128,2560]{1,0:T(8,128)(2,1)S(1)}, u32[]{:S(2)}, u32[]{:S(2)}) collective-permute-start(bf16[128,2560]{1,0:T(8,128)(2,1)S(1)} %shard_map.101.refs_6_), channel_id=1, source_target_pairs={{0,8},{8,0},{1,9},{9,1},{2,10},{10,2},{3,11},{11,3},{4,12},{12,4},... | collective-permute-start | bytes 1966088 | tf_op jit(solution)/shard_map/ppermute | solution.py:274
  124.7 16.0 %collective-permute-start.13 = (bf16[128,2560]{1,0:T(8,128)(2,1)S(1)}, bf16[128,2560]{1,0:T(8,128)(2,1)S(1)}, u32[]{:S(2)}, u32[]{:S(2)}) collective-permute-start(bf16[128,2560]{1,0:T(8,128)(2,1)S(1)} %shard_map.101.refs_6_), channel_id=1, source_target_pairs={{0,16},{16,0},{32,48},{48,32},{1,17},{17,1},{33,49},{49,33},{2,18}... | collective-permute-start | bytes 1966088 | tf_op jit(solution)/shard_map/ppermute | solution.py:278
  140.7 3.0 %collective-permute-start.17 = (bf16[128,2560]{1,0:T(8,128)(2,1)S(1)}, bf16[128,2560]{1,0:T(8,128)(2,1)S(1)}, u32[]{:S(2)}, u32[]{:S(2)}) collective-permute-start(bf16[128,2560]{1,0:T(8,128)(2,1)S(1)} %collective-permute-done.13.refs_4_), channel_id=1, source_target_pairs={{0,8},{8,0},{1,9},{9,1},{2,10},{10,2},{3,11},{11,3},{4,12},{12,4},... | collective-permute-start | bytes 1966088 | tf_op jit(solution)/shard_map/ppermute | solution.py:274

commit v6 on v5

--- a/solution.py
+++ b/solution.py
@@ -74,14 +74,12 @@
     rest = source - half * (per * width)
     dest = lax.div(rest, width)
     start = dest * block + half * width + rest - dest * width
-    moves = [one_hot(per * block, start + cut * 2 * width) for cut in range(cuts)]
+    move = jnp.concatenate([one_hot(per * block, start + cut * 2 * width) for cut in range(cuts)], axis=1)
     for group in range(groups):
         here = slice(group * per * width, (group + 1) * per * width)
         both = jnp.concatenate([own[here, :], across[here, :]], axis=0)
-        total = None
-        for cut, move in enumerate(moves):
-            part = jnp.dot(move, both[:, cut * lanes : (cut + 1) * lanes], preferred_element_type=f32)
-            total = part if total is None else total + part
+        stacked = jnp.concatenate([both[:, cut * lanes : (cut + 1) * lanes] for cut in range(cuts)], axis=0)
+        total = jnp.dot(move, stacked, preferred_element_type=f32)
         out_ref[group * per : (group + 1) * per] = total.astype(bf16).reshape(per, block, lanes)
 
 
@@ -101,11 +99,10 @@
 
 def hidden_kernel(half_ref, routes_ref, hidden_ref, out_ref):
     rows = FLIGHT * (HIDDEN[1] - HIDDEN[0])
-    picked = None
-    for k, target in enumerate(targets(slot_table(routes_ref), half_ref[0, 0], *HIDDEN)):
-        part = jnp.dot(one_hot(rows, target), hidden_ref[k], preferred_element_type=f32)
-        picked = part if picked is None else picked + part
-    packed = picked.astype(bf16)
+    places = targets(slot_table(routes_ref), half_ref[0, 0], *HIDDEN)
+    picks = jnp.concatenate([one_hot(rows, target) for target in places], axis=1)
+    entries = hidden_ref[...].reshape(picks.shape[1], hidden_ref.shape[2])
+    packed = jnp.dot(picks, entries, preferred_element_type=f32).astype(bf16)
     spread(packed[: rows // 2], packed[rows // 2 :], HIDDEN[1] - HIDDEN[0], out_ref)
 
 

time: 151 us -> 149 us (0.987)
  Pallas kernels: 43.1 us -> 41.2 us
    ppermute x7, starting transfers between devices: 5.99 us -> 7.7 us  [y_moved(): return lax.ppermute(value, ('yh', 'yl'), [(i, i ^ flip) for i in range(4)])]
where the time goes in v6:
time: 149 us; the launch traced here: 148 us
  waiting for transfers between devices  55 us (37%)
  starting transfers between devices  46.5 us (31%)
  Pallas kernels  41.2 us (28%)
  local copies, waits for them, and re-layouts  4.26 us (3%)
    ppermute x7, waiting for transfers between devices, y_moved(): return lax.ppermute(value, ('yh', 'yl'), [(i, i ^ flip) for i in range(4)])  48.2 us
    pallas_call x4, Pallas kernels, stats(): pl.pallas_call(functools.partial(stats_kernel, norm, offset, len(rows), m...  30.6 us
    all_to_all x3, starting transfers between devices, along_xz(): return lax.all_to_all(value, ('x', 'z'), 0, 0, tiled=True)  27.8 us
    ppermute x8, starting transfers between devices, core_swapped(): return lax.ppermute(value, 'core', [(0, 1), (1, 0)])  7.83 us
    ppermute x7, starting transfers between devices, y_moved(): return lax.ppermute(value, ('yh', 'yl'), [(i, i ^ flip) for i in range(4)])  7.7 us
    ppermute x8, waiting for transfers between devices, core_swapped(): return lax.ppermute(value, 'core', [(0, 1), (1, 0)])  6.82 us
    unnamed x20, local copies, waits for them, and re-layouts  4.26 us
    pallas_call x1, Pallas kernels, per_device(): pl.pallas_call(hidden_kernel, out_shape=block_shape(whole, width_in), in_...  3.48 us
  transfers between devices with their start and end apart: 21, of which 11 were waited for; matrix products, arithmetic and copies ran while one was open for 0% of the time, Pallas kernels for 21%

profile of v6, /device:TPU:1, one launch (start us, length us, event | category | flops | bytes accessed | tf_op | source)
XLA Modules:
  0.0 147.9 jit_solution(11275044152847172846)
XLA Ops:
  0.6 1.7 %copy-done = bf16[128,6,1536]{2,0,1:T(8,128)(2,1)S(1)} copy-done((bf16[128,6,1536]{2,0,1:T(8,128)(2,1)S(1)}, bf16[128,6,1536]{2,0,1:T(8,128)(2,1)}, u32[]{:S(2)}) %copy-start) | copy-done | bytes 2359320
  3.0 3.5 %shard_map.93 = bf16[32,48,384]{2,1,0:T(8,128)(2,1)} custom-call(s32[1,1]{1,0:T(1,128)} %bitcast.1.half_ref, s32[6,128]{1,0:T(8,128)S(1)} %bitcast.12, bf16[6,128,1536]{2,1,0:T(8,128)(2,1)S(1)} %bitcast.11), custom_call_target="tpu_custom_call" | custom-call | tf_op jit(solution)/shard_map/pallas_call | solution.py:295
  6.5 12.0 %all-to-all-start = ((bf16[32,48,384]{2,1,0:T(8,128)(2,1)}), bf16[32,48,384]{2,1,0:T(8,128)(2,1)S(1)}, u32[]{:S(2)}, u32[]{:S(2)}) async-start(bf16[32,48,384]{2,1,0:T(8,128)(2,1)} %shard_map.93), calls=%async_computation | async-start | bytes 2359296 | tf_op jit(solution)/shard_map/all_to_all | solution.py:283
  19.4 2.8 %collective-permute-start = (bf16[128,2560]{1,0:T(8,128)(2,1)S(1)}, bf16[128,2560]{1,0:T(8,128)(2,1)S(1)}, u32[]{:S(2)}, u32[]{:S(2)}) collective-permute-start(bf16[128,2560]{1,0:T(8,128)(2,1)S(1)} %get-tuple-element.45), channel_id=1, source_target_pairs={{0,48},{16,32},{32,16},{48,0},{1,49},{17,33},{33,17},{49,1},{2,50}... | collective-permute-start | bytes 1966088 | tf_op jit(solution)/shard_map/ppermute | solution.py:275
  22.4 1.4 collective-permute-start.2
  23.9 1.6 %collective-permute-start.4 = (f32[32,1024]{1,0:T(8,128)S(1)}, f32[32,1024]{1,0:T(8,128)S(1)}, u32[]{:S(2)}, u32[]{:S(2)}) collective-permute-start(f32[32,1024]{1,0:T(8,128)S(1)} %pad_maximum_fusion.refs_0_), channel_id=1, source_target_pairs={{0,24},{8,16},{16,8},{24,0},{1,25},{9,17},{17,9},{25,1},{2,26},{10... | collective-permute-start | bytes 393224 | tf_op jit(solution)/shard_map/ppermute | solution.py:311
  25.5 17.6 %collective-permute-done.1.across_ref = bf16[64,2560]{1,0:T(8,128)(2,1)S(1)} collective-permute-done((bf16[64,2560]{1,0:T(8,128)(2,1)S(1)}, bf16[64,2560]{1,0:T(8,128)(2,1)S(1)}, u32[]{:S(2)}, u32[]{:S(2)}) %collective-permute-start.1) | collective-permute-done | bytes 327712 | tf_op jit(solution)/shard_map/ppermute | solution.py:275
  43.2 1.4 shard_map.96
  44.6 1.6 %shard_map.95 = bf16[32,16,1280]{2,1,0:T(8,128)(2,1)} custom-call(bf16[128,2560]{1,0:T(8,128)(2,1)S(1)} %get-tuple-element.44.own_ref, bf16[128,2560]{1,0:T(8,128)(2,1)S(1)} %collective-permute-done.across_ref), custom_call_target="tpu_custom_call" | custom-call | flops 1 | bytes 1 | tf_op jit(solution)/shard_map/pallas_call | solution.py:133
  46.2 8.9 %all-to-all-start.1 = ((bf16[32,16,1280]{2,1,0:T(8,128)(2,1)}), bf16[32,16,1280]{2,1,0:T(8,128)(2,1)S(1)}, u32[]{:S(2)}, u32[]{:S(2)}) async-start(bf16[32,16,1280]{2,1,0:T(8,128)(2,1)} %shard_map.95), calls=%async_computation.1 | async-start | bytes 2621440 | tf_op jit(solution)/shard_map/all_to_all | solution.py:283
  55.1 2.2 %shard_map.97 = (bf16[192,1536]{1,0:T(8,128)(2,1)}, bf16[192,1536]{1,0:T(8,128)(2,1)S(1)}) custom-call(bf16[32,48,384]{2,1,0:T(8,128)(2,1)S(1)} %all-to-all-done.in_ref), custom_call_target="tpu_custom_call" | custom-call | flops 1 | bytes 1 | tf_op jit(solution)/shard_map/pallas_call | solution.py:171
  57.3 2.6 %collective-permute-start.6 = (bf16[192,1536]{1,0:T(8,128)(2,1)S(1)}, bf16[192,1536]{1,0:T(8,128)(2,1)S(1)}, u32[]{:S(2)}, u32[]{:S(2)}) collective-permute-start(bf16[192,1536]{1,0:T(8,128)(2,1)S(1)} %get-tuple-element.54), channel_id=1, source_target_pairs={{0,48},{16,32},{32,16},{48,0},{1,49},{17,33},{33,17},{49,1},{2,50}... | collective-permute-start | bytes 1769480 | tf_op jit(solution)/shard_map/ppermute | solution.py:275
  59.9 11.1 %collective-permute-done.6.refs_6_ = bf16[192,1536]{1,0:T(8,128)(2,1)S(1)} collective-permute-done((bf16[192,1536]{1,0:T(8,128)(2,1)S(1)}, bf16[192,1536]{1,0:T(8,128)(2,1)S(1)}, u32[]{:S(2)}, u32[]{:S(2)}) %collective-permute-start.6) | collective-permute-done | bytes 589856 | tf_op jit(solution)/shard_map/ppermute | solution.py:275
  71.2 1.0 collective-permute-done.5.refs_5_
  73.0 13.1 %collective-permute-done.7.refs_7_ = bf16[192,1536]{1,0:T(8,128)(2,1)} collective-permute-done((bf16[192,1536]{1,0:T(8,128)(2,1)S(1)}, bf16[192,1536]{1,0:T(8,128)(2,1)}, u32[]{:S(2)}, u32[]{:S(2)}) %collective-permute-start.7) | collective-permute-done | bytes 589856 | tf_op jit(solution)/shard_map/ppermute | solution.py:275
  86.7 4.0 %collective-permute-start.12 = (bf16[256,2560]{1,0:T(8,128)(2,1)S(1)}, bf16[256,2560]{1,0:T(8,128)(2,1)}, u32[]{:S(2)}, u32[]{:S(2)}) collective-permute-start(bf16[256,2560]{1,0:T(8,128)(2,1)S(1)} %shard_map.98.refs_4_), channel_id=1, source_target_pairs={{0,8},{8,0},{1,9},{9,1},{2,10},{10,2},{3,11},{11,3},{4,12},{12,4},... | collective-permute-start | bytes 3932168 | tf_op jit(solution)/shard_map/ppermute | solution.py:271
  90.7 1.0 collective-permute-start.14
  92.2 6.8 %all-to-all-start.2 = ((bf16[32,16,640]{2,1,0:T(8,128)(2,1)}), bf16[32,16,640]{2,1,0:T(8,128)(2,1)S(1)}, u32[]{:S(2)}, u32[]{:S(2)}) async-start(bf16[32,16,640]{2,1,0:T(8,128)(2,1)} %shard_map.96), calls=%async_computation.2 | async-start | bytes 1310720 | tf_op jit(solution)/shard_map/all_to_all | solution.py:283
  99.9 1.5 %collective-permute-done.9.refs_9_ = bf16[192,1536]{1,0:T(8,128)(2,1)} collective-permute-done((bf16[192,1536]{1,0:T(8,128)(2,1)}, bf16[192,1536]{1,0:T(8,128)(2,1)}, u32[]{:S(2)}, u32[]{:S(2)}) %collective-permute-start.9) | collective-permute-done | bytes 589856 | tf_op jit(solution)/shard_map/ppermute | solution.py:271
  101.5 1.5 collective-permute-done.10.refs_10_
  103.1 1.1 copy-done.5
  104.2 7.6 %shard_map.99 = (f32[384,1536]{1,0:T(8,128)}, f32[32,384]{1,0:T(8,128)}) custom-call(s32[1,1]{1,0:T(1,128)} %bitcast.q_ref, f32[32,1024]{1,0:T(8,128)S(1)} %pad_maximum_fusion.refs_0_, f32[32,1024]{1,0:T(8,128)S(1)} %collective-permute-done.2.refs_1_, f32[32,1024]{1,0:T(8,128)S(1)} %collective-permute-done.3.refs_2_, ...), custom_call_target="tpu_custom_call" | custom-call | flops 1 | bytes 1 | tf_op jit(solution)/shard_map/pallas_call | solution.py:247
  111.8 6.6 %shard_map.100 = (f32[640,2560]{1,0:T(8,128)}, f32[32,640]{1,0:T(8,128)}) custom-call(s32[1,1]{1,0:T(1,128)} %bitcast.q_ref, f32[32,1024]{1,0:T(8,128)S(1)} %pad_maximum_fusion.refs_0_, f32[32,1024]{1,0:T(8,128)S(1)} %collective-permute-done.2.refs_1_, f32[32,1024]{1,0:T(8,128)S(1)} %collective-permute-done.3.refs_2_, ...), custom_call_target="tpu_custom_call" | custom-call | flops 1 | bytes 1 | tf_op jit(solution)/shard_map/pallas_call | solution.py:247
  118.4 2.5 %collective-permute-done.14.refs_4_ = bf16[256,2560]{1,0:T(8,128)(2,1)} collective-permute-done((bf16[256,2560]{1,0:T(8,128)(2,1)S(1)}, bf16[256,2560]{1,0:T(8,128)(2,1)}, u32[]{:S(2)}, u32[]{:S(2)}) %collective-permute-start.14) | collective-permute-done | bytes 1310752 | tf_op jit(solution)/shard_map/ppermute | solution.py:275
  120.8 1.1 collective-permute-start.15
  122.7 1.0 collective-permute-start.13
  123.7 1.9 %collective-permute-done.16.refs_7_ = bf16[128,2560]{1,0:T(8,128)(2,1)S(1)} collective-permute-done((bf16[128,2560]{1,0:T(8,128)(2,1)S(1)}, bf16[128,2560]{1,0:T(8,128)(2,1)S(1)}, u32[]{:S(2)}, u32[]{:S(2)}) %collective-permute-start.16) | collective-permute-done | bytes 655392 | tf_op jit(solution)/shard_map/ppermute | solution.py:271
  125.6 10.2 %shard_map.102 = (f32[640,2560]{1,0:T(8,128)}, f32[32,640]{1,0:T(8,128)}) custom-call(s32[1,1]{1,0:T(1,128)} %bitcast.q_ref, f32[32,1024]{1,0:T(8,128)S(1)} %pad_maximum_fusion.refs_0_, f32[32,1024]{1,0:T(8,128)S(1)} %collective-permute-done.2.refs_1_, f32[32,1024]{1,0:T(8,128)S(1)} %collective-permute-done.3.refs_2_, ...), custom_call_target="tpu_custom_call", output_to_operand_aliasing={{0}: (9, {}), {1}: (10, {})} | custom-call | flops 1 | bytes 1 | tf_op jit(solution)/shard_map/pallas_call | solution.py:247
  135.8 2.8 %collective-permute-done.13.refs_4_ = bf16[128,2560]{1,0:T(8,128)(2,1)S(1)} collective-permute-done((bf16[128,2560]{1,0:T(8,128)(2,1)S(1)}, bf16[128,2560]{1,0:T(8,128)(2,1)S(1)}, u32[]{:S(2)}, u32[]{:S(2)}) %collective-permute-start.13) | collective-permute-done | bytes 655392 | tf_op jit(solution)/shard_map/ppermute | solution.py:275
  138.6 1.2 collective-permute-start.17
  139.9 1.7 %collective-permute-done.17.refs_5_ = bf16[128,2560]{1,0:T(8,128)(2,1)S(1)} collective-permute-done((bf16[128,2560]{1,0:T(8,128)(2,1)S(1)}, bf16[128,2560]{1,0:T(8,128)(2,1)S(1)}, u32[]{:S(2)}, u32[]{:S(2)}) %collective-permute-start.17) | collective-permute-done | bytes 655392 | tf_op jit(solution)/shard_map/ppermute | solution.py:271
  141.6 6.2 %shard_map.103 = (f32[640,2560]{1,0:T(8,128)}, f32[32,640]{1,0:T(8,128)}) custom-call(s32[1,1]{1,0:T(1,128)} %bitcast.q_ref, f32[32,1024]{1,0:T(8,128)S(1)} %pad_maximum_fusion.refs_0_, f32[32,1024]{1,0:T(8,128)S(1)} %collective-permute-done.2.refs_1_, f32[32,1024]{1,0:T(8,128)S(1)} %collective-permute-done.3.refs_2_, ...), custom_call_target="tpu_custom_call", output_to_operand_aliasing={{0}: (7, {}), {1}: (8, {})} | custom-call | flops 1 | bytes 1 | tf_op jit(solution)/shard_map/pallas_call | solution.py:247
  (42 shorter events, 5.7 us)
Async XLA Ops:
  0.6 1.7 %copy-start = (bf16[128,6,1536]{2,0,1:T(8,128)(2,1)S(1)}, bf16[128,6,1536]{2,0,1:T(8,128)(2,1)}, u32[]{:S(2)}) copy-start(bf16[128,6,1536]{2,0,1:T(8,128)(2,1)} %param.6) | copy-start | bytes 7077892
  2.3 0.7 copy-start.6
  6.5 12.0 %copy-start.1 = (bf16[128,2560]{1,0:T(8,128)(2,1)S(1)}, bf16[128,2560]{1,0:T(8,128)(2,1)}, u32[]{:S(2)}) copy-start(bf16[128,2560]{1,0:T(8,128)(2,1)} %grads_ref.1) | copy-start | bytes 1966084
  6.5 12.1 %copy-start.7 = (f32[128,6]{0,1:T(8,128)S(1)}, f32[128,6]{0,1:T(8,128)}, u32[]{:S(2)}) copy-start(f32[128,6]{0,1:T(8,128)} %param.8) | copy-start | bytes 9220
  6.5 15.9 %copy-start.8 = (f32[1,32,640]{2,1,0:T(8,128)S(1)}, f32[1,32,640]{2,1,0:T(8,128)}, u32[]{:S(2)}) copy-start(f32[1,32,640]{2,1,0:T(8,128)} %param.11) | copy-start | bytes 245764
  6.5 15.9 %copy-start.9 = (f32[1,32,384]{2,1,0:T(8,128)S(1)}, f32[1,32,384]{2,1,0:T(8,128)}, u32[]{:S(2)}) copy-start(f32[1,32,384]{2,1,0:T(8,128)} %param.10) | copy-start | bytes 147460
  6.5 39.7 %all-to-all-start = ((bf16[32,48,384]{2,1,0:T(8,128)(2,1)}), bf16[32,48,384]{2,1,0:T(8,128)(2,1)S(1)}, u32[]{:S(2)}, u32[]{:S(2)}) async-start(bf16[32,48,384]{2,1,0:T(8,128)(2,1)} %shard_map.93), calls=%async_computation | async-start | bytes 2359296 | tf_op jit(solution)/shard_map/all_to_all | solution.py:283
  19.4 25.1 %collective-permute-start = (bf16[128,2560]{1,0:T(8,128)(2,1)S(1)}, bf16[128,2560]{1,0:T(8,128)(2,1)S(1)}, u32[]{:S(2)}, u32[]{:S(2)}) collective-permute-start(bf16[128,2560]{1,0:T(8,128)(2,1)S(1)} %get-tuple-element.45), channel_id=1, source_target_pairs={{0,48},{16,32},{32,16},{48,0},{1,49},{17,33},{33,17},{49,1},{2,50}... | collective-permute-start | bytes 1966088 | tf_op jit(solution)/shard_map/ppermute | solution.py:275
  22.2 20.9 %collective-permute-start.1 = (bf16[64,2560]{1,0:T(8,128)(2,1)S(1)}, bf16[64,2560]{1,0:T(8,128)(2,1)S(1)}, u32[]{:S(2)}, u32[]{:S(2)}) collective-permute-start(bf16[64,2560]{1,0:T(8,128)(2,1)S(1)} %get-tuple-element.47), channel_id=1, source_target_pairs={{0,48},{16,32},{32,16},{48,0},{1,49},{17,33},{33,17},{49,1},{2,50}... | collective-permute-start | bytes 983048 | tf_op jit(solution)/shard_map/ppermute | solution.py:275
  22.4 23.8 %collective-permute-start.2 = (f32[32,1024]{1,0:T(8,128)S(1)}, f32[32,1024]{1,0:T(8,128)S(1)}, u32[]{:S(2)}, u32[]{:S(2)}) collective-permute-start(f32[32,1024]{1,0:T(8,128)S(1)} %pad_maximum_fusion.refs_0_), channel_id=1, source_target_pairs={{0,8},{8,0},{16,24},{24,16},{1,9},{9,1},{17,25},{25,17},{2,10},{10... | collective-permute-start | bytes 393224 | tf_op jit(solution)/shard_map/ppermute | solution.py:311
  23.8 22.3 %collective-permute-start.3 = (f32[32,1024]{1,0:T(8,128)S(1)}, f32[32,1024]{1,0:T(8,128)S(1)}, u32[]{:S(2)}, u32[]{:S(2)}) collective-permute-start(f32[32,1024]{1,0:T(8,128)S(1)} %pad_maximum_fusion.refs_0_), channel_id=1, source_target_pairs={{0,16},{8,24},{16,0},{24,8},{1,17},{9,25},{17,1},{25,9},{2,18},{10... | collective-permute-start | bytes 393224 | tf_op jit(solution)/shard_map/ppermute | solution.py:311
  23.9 22.2 %collective-permute-start.4 = (f32[32,1024]{1,0:T(8,128)S(1)}, f32[32,1024]{1,0:T(8,128)S(1)}, u32[]{:S(2)}, u32[]{:S(2)}) collective-permute-start(f32[32,1024]{1,0:T(8,128)S(1)} %pad_maximum_fusion.refs_0_), channel_id=1, source_target_pairs={{0,24},{8,16},{16,8},{24,0},{1,25},{9,17},{17,9},{25,1},{2,26},{10... | collective-permute-start | bytes 393224 | tf_op jit(solution)/shard_map/ppermute | solution.py:311
  46.2 40.0 %all-to-all-start.1 = ((bf16[32,16,1280]{2,1,0:T(8,128)(2,1)}), bf16[32,16,1280]{2,1,0:T(8,128)(2,1)S(1)}, u32[]{:S(2)}, u32[]{:S(2)}) async-start(bf16[32,16,1280]{2,1,0:T(8,128)(2,1)} %shard_map.95), calls=%async_computation.1 | async-start | bytes 2621440 | tf_op jit(solution)/shard_map/all_to_all | solution.py:283
  57.3 13.7 %collective-permute-start.6 = (bf16[192,1536]{1,0:T(8,128)(2,1)S(1)}, bf16[192,1536]{1,0:T(8,128)(2,1)S(1)}, u32[]{:S(2)}, u32[]{:S(2)}) collective-permute-start(bf16[192,1536]{1,0:T(8,128)(2,1)S(1)} %get-tuple-element.54), channel_id=1, source_target_pairs={{0,48},{16,32},{32,16},{48,0},{1,49},{17,33},{33,17},{49,1},{2,50}... | collective-permute-start | bytes 1769480 | tf_op jit(solution)/shard_map/ppermute | solution.py:275
  59.9 12.3 %collective-permute-start.5 = (bf16[192,1536]{1,0:T(8,128)(2,1)}, bf16[192,1536]{1,0:T(8,128)(2,1)S(1)}, u32[]{:S(2)}, u32[]{:S(2)}) collective-permute-start(bf16[192,1536]{1,0:T(8,128)(2,1)} %get-tuple-element.57.refs_4_), channel_id=1, source_target_pairs={{0,16},{16,0},{32,48},{48,32},{1,17},{17,1},{33,49},{49,33},{2,18}... | collective-permute-start | bytes 1769480 | tf_op jit(solution)/shard_map/ppermute | solution.py:275
  71.0 1.2 copy-start.2
  71.0 15.2 %collective-permute-start.7 = (bf16[192,1536]{1,0:T(8,128)(2,1)S(1)}, bf16[192,1536]{1,0:T(8,128)(2,1)}, u32[]{:S(2)}, u32[]{:S(2)}) collective-permute-start(bf16[192,1536]{1,0:T(8,128)(2,1)S(1)} %collective-permute-done.6.refs_6_), channel_id=1, source_target_pairs={{0,16},{16,0},{32,48},{48,32},{1,17},{17,1},{33,49},{49,33},{2,18}... | collective-permute-start | bytes 1769480 | tf_op jit(solution)/shard_map/ppermute | solution.py:275
  72.2 0.8 copy-start.4
  86.7 12.7 %copy-start.3 = (bf16[192,1536]{1,0:T(8,128)(2,1)S(1)}, bf16[192,1536]{1,0:T(8,128)(2,1)}, u32[]{:S(2)}) copy-start(bf16[192,1536]{1,0:T(8,128)(2,1)} %copy-done.2) | copy-start | bytes 1769476
  86.7 25.1 %collective-permute-start.12 = (bf16[256,2560]{1,0:T(8,128)(2,1)S(1)}, bf16[256,2560]{1,0:T(8,128)(2,1)}, u32[]{:S(2)}, u32[]{:S(2)}) collective-permute-start(bf16[256,2560]{1,0:T(8,128)(2,1)S(1)} %shard_map.98.refs_4_), channel_id=1, source_target_pairs={{0,8},{8,0},{1,9},{9,1},{2,10},{10,2},{3,11},{11,3},{4,12},{12,4},... | collective-permute-start | bytes 3932168 | tf_op jit(solution)/shard_map/ppermute | solution.py:271
  90.7 30.2 %collective-permute-start.14 = (bf16[256,2560]{1,0:T(8,128)(2,1)S(1)}, bf16[256,2560]{1,0:T(8,128)(2,1)}, u32[]{:S(2)}, u32[]{:S(2)}) collective-permute-start(bf16[256,2560]{1,0:T(8,128)(2,1)S(1)} %shard_map.98.refs_4_), channel_id=1, source_target_pairs={{0,16},{16,0},{32,48},{48,32},{1,17},{17,1},{33,49},{49,33},{2,18}... | collective-permute-start | bytes 3932168 | tf_op jit(solution)/shard_map/ppermute | solution.py:275
  91.6 8.0 %collective-permute-start.8 = (bf16[192,1536]{1,0:T(8,128)(2,1)}, bf16[192,1536]{1,0:T(8,128)(2,1)}, u32[]{:S(2)}, u32[]{:S(2)}) collective-permute-start(bf16[192,1536]{1,0:T(8,128)(2,1)} %get-tuple-element.57.refs_4_), channel_id=1, source_target_pairs={{0,8},{8,0},{1,9},{9,1},{2,10},{10,2},{3,11},{11,3},{4,12},{12,4},... | collective-permute-start | bytes 1769480 | tf_op jit(solution)/shard_map/ppermute | solution.py:271
  92.2 29.8 %all-to-all-start.2 = ((bf16[32,16,640]{2,1,0:T(8,128)(2,1)}), bf16[32,16,640]{2,1,0:T(8,128)(2,1)S(1)}, u32[]{:S(2)}, u32[]{:S(2)}) async-start(bf16[32,16,640]{2,1,0:T(8,128)(2,1)} %shard_map.96), calls=%async_computation.2 | async-start | bytes 1310720 | tf_op jit(solution)/shard_map/all_to_all | solution.py:283
  99.0 2.4 %collective-permute-start.9 = (bf16[192,1536]{1,0:T(8,128)(2,1)}, bf16[192,1536]{1,0:T(8,128)(2,1)}, u32[]{:S(2)}, u32[]{:S(2)}) collective-permute-start(bf16[192,1536]{1,0:T(8,128)(2,1)} %copy-done.4), channel_id=1, source_target_pairs={{0,8},{8,0},{1,9},{9,1},{2,10},{10,2},{3,11},{11,3},{4,12},{12,4},... | collective-permute-start | bytes 1769480 | tf_op jit(solution)/shard_map/ppermute | solution.py:271
  99.4 3.5 %collective-permute-start.10 = (bf16[192,1536]{1,0:T(8,128)(2,1)S(1)}, bf16[192,1536]{1,0:T(8,128)(2,1)}, u32[]{:S(2)}, u32[]{:S(2)}) collective-permute-start(bf16[192,1536]{1,0:T(8,128)(2,1)S(1)} %copy-done.3), channel_id=1, source_target_pairs={{0,8},{8,0},{1,9},{9,1},{2,10},{10,2},{3,11},{11,3},{4,12},{12,4},... | collective-permute-start | bytes 1769480 | tf_op jit(solution)/shard_map/ppermute | solution.py:271
  99.6 3.5 %collective-permute-start.11 = (bf16[192,1536]{1,0:T(8,128)(2,1)}, bf16[192,1536]{1,0:T(8,128)(2,1)}, u32[]{:S(2)}, u32[]{:S(2)}) collective-permute-start(bf16[192,1536]{1,0:T(8,128)(2,1)} %collective-permute-done.7.refs_7_), channel_id=1, source_target_pairs={{0,8},{8,0},{1,9},{9,1},{2,10},{10,2},{3,11},{11,3},{4,12},{12,4},... | collective-permute-start | bytes 1769480 | tf_op jit(solution)/shard_map/ppermute | solution.py:271
  103.1 1.1 copy-start.5
  120.8 4.7 %collective-permute-start.15 = (bf16[256,2560]{1,0:T(8,128)(2,1)}, bf16[256,2560]{1,0:T(8,128)(2,1)S(1)}, u32[]{:S(2)}, u32[]{:S(2)}) collective-permute-start(bf16[256,2560]{1,0:T(8,128)(2,1)} %collective-permute-done.14.refs_4_), channel_id=1, source_target_pairs={{0,8},{8,0},{1,9},{9,1},{2,10},{10,2},{3,11},{11,3},{4,12},{12,4},... | collective-permute-start | bytes 3932168 | tf_op jit(solution)/shard_map/ppermute | solution.py:271
  122.6 3.0 %collective-permute-start.16 = (bf16[128,2560]{1,0:T(8,128)(2,1)S(1)}, bf16[128,2560]{1,0:T(8,128)(2,1)S(1)}, u32[]{:S(2)}, u32[]{:S(2)}) collective-permute-start(bf16[128,2560]{1,0:T(8,128)(2,1)S(1)} %shard_map.101.refs_6_), channel_id=1, source_target_pairs={{0,8},{8,0},{1,9},{9,1},{2,10},{10,2},{3,11},{11,3},{4,12},{12,4},... | collective-permute-start | bytes 1966088 | tf_op jit(solution)/shard_map/ppermute | solution.py:271
  122.7 16.0 %collective-permute-start.13 = (bf16[128,2560]{1,0:T(8,128)(2,1)S(1)}, bf16[128,2560]{1,0:T(8,128)(2,1)S(1)}, u32[]{:S(2)}, u32[]{:S(2)}) collective-permute-start(bf16[128,2560]{1,0:T(8,128)(2,1)S(1)} %shard_map.101.refs_6_), channel_id=1, source_target_pairs={{0,16},{16,0},{32,48},{48,32},{1,17},{17,1},{33,49},{49,33},{2,18}... | collective-permute-start | bytes 1966088 | tf_op jit(solution)/shard_map/ppermute | solution.py:275
  138.6 3.0 %collective-permute-start.17 = (bf16[128,2560]{1,0:T(8,128)(2,1)S(1)}, bf16[128,2560]{1,0:T(8,128)(2,1)S(1)}, u32[]{:S(2)}, u32[]{:S(2)}) collective-permute-start(bf16[128,2560]{1,0:T(8,128)(2,1)S(1)} %collective-permute-done.13.refs_4_), channel_id=1, source_target_pairs={{0,8},{8,0},{1,9},{9,1},{2,10},{10,2},{3,11},{11,3},{4,12},{12,4},... | collective-permute-start | bytes 1966088 | tf_op jit(solution)/shard_map/ppermute | solution.py:271

commit v7 on v6

--- a/solution.py
+++ b/solution.py
@@ -294,10 +294,15 @@
     whole, first, last = (end - start for start, end in (HIDDEN, GRAD_FIRST, GRAD_LAST))
     sent_h = pl.pallas_call(
         hidden_kernel,
+        grid=(1,),
         out_shape=block_shape(whole, width_in),
-        in_specs=[SMEM, VMEM, VMEM],
-        out_specs=VMEM,
-        compiler_params=params(32),
+        in_specs=[
+            SMEM,
+            pl.BlockSpec((slots, tok), lambda n: (0, 0)),
+            pl.BlockSpec((slots, tok, width_in), lambda n: (0, 0, 0)),
+        ],
+        out_specs=pl.BlockSpec(block_shape(whole, width_in).shape, lambda n: (0, 0, 0)),
+        compiler_params=params(62),
     )(my_half, routes_t, hidden_rows.transpose(1, 0, 2))
     own_b, across_b, own_c, across_c = pl.pallas_call(
         grads_kernel,

time: 149 us -> 148 us (level)
  local copies, waits for them, and re-layouts: 4.26 us -> 1.92 us
  Pallas kernels: 41.2 us -> 42.9 us
    unnamed x20 -> x18, local copies, waits for them, and re-layouts: 4.26 us -> 1.92 us
    pallas_call x1, Pallas kernels: 3.48 us -> 5.16 us  [per_device(): pl.pallas_call(hidden_kernel, grid=(1,), out_shape=block_shape(whole, wid...]
where the time goes in v7:
time: 148 us; the launch traced here: 147 us
  waiting for transfers between devices  54.9 us (37%)
  starting transfers between devices  46.5 us (31%)
  Pallas kernels  42.9 us (29%)
  local copies, waits for them, and re-layouts  1.92 us (1%)
    ppermute x7, waiting for transfers between devices, y_moved(): return lax.ppermute(value, ('yh', 'yl'), [(i, i ^ flip) for i in range(4)])  48.1 us
    pallas_call x4, Pallas kernels, stats(): pl.pallas_call(functools.partial(stats_kernel, norm, offset, len(rows), m...  30.6 us
    all_to_all x3, starting transfers between devices, along_xz(): return lax.all_to_all(value, ('x', 'z'), 0, 0, tiled=True)  27.8 us
    ppermute x7, starting transfers between devices, y_moved(): return lax.ppermute(value, ('yh', 'yl'), [(i, i ^ flip) for i in range(4)])  7.85 us
    ppermute x8, starting transfers between devices, core_swapped(): return lax.ppermute(value, 'core', [(0, 1), (1, 0)])  7.77 us
    ppermute x8, waiting for transfers between devices, core_swapped(): return lax.ppermute(value, 'core', [(0, 1), (1, 0)])  6.77 us
    pallas_call x1, Pallas kernels, per_device(): pl.pallas_call(hidden_kernel, grid=(1,), out_shape=block_shape(whole, wid...  5.16 us
    pallas_call x3, Pallas kernels, gathered(): pl.pallas_call(functools.partial(gather_kernel, width), out_shape=(jax.Sh...  3.29 us
  transfers between devices with their start and end apart: 21, of which 11 were waited for; matrix products, arithmetic and copies ran while one was open for 0% of the time, Pallas kernels for 21%

profile of v7, /device:TPU:1, one launch (start us, length us, event | category | flops | bytes accessed | tf_op | source)
XLA Modules:
  0.0 147.3 jit_solution(11543494432937627939)
XLA Ops:
  0.6 5.2 %shard_map.93 = bf16[32,48,384]{2,1,0:T(8,128)(2,1)} custom-call(s32[1,1]{1,0:T(1,128)} %bitcast.1.half_ref, s32[6,128]{1,0:T(8,128)} %bitcast.11, bf16[6,128,1536]{2,1,0:T(8,128)(2,1)} %bitcast.15), custom_call_target="tpu_custom_call" | custom-call | tf_op jit(solution)/shard_map/pallas_call | solution.py:295
  5.8 12.0 %all-to-all-start = ((bf16[32,48,384]{2,1,0:T(8,128)(2,1)}), bf16[32,48,384]{2,1,0:T(8,128)(2,1)S(1)}, u32[]{:S(2)}, u32[]{:S(2)}) async-start(bf16[32,48,384]{2,1,0:T(8,128)(2,1)} %shard_map.93), calls=%async_computation | async-start | bytes 2359296 | tf_op jit(solution)/shard_map/all_to_all | solution.py:283
  17.9 0.9 shard_map.94
  18.8 2.8 %collective-permute-start = (bf16[128,2560]{1,0:T(8,128)(2,1)S(1)}, bf16[128,2560]{1,0:T(8,128)(2,1)S(1)}, u32[]{:S(2)}, u32[]{:S(2)}) collective-permute-start(bf16[128,2560]{1,0:T(8,128)(2,1)S(1)} %get-tuple-element.45), channel_id=1, source_target_pairs={{0,48},{16,32},{32,16},{48,0},{1,49},{17,33},{33,17},{49,1},{2,50}... | collective-permute-start | bytes 1966088 | tf_op jit(solution)/shard_map/ppermute | solution.py:275
  21.7 1.4 collective-permute-start.2
  23.3 1.6 %collective-permute-start.4 = (f32[32,1024]{1,0:T(8,128)S(1)}, f32[32,1024]{1,0:T(8,128)S(1)}, u32[]{:S(2)}, u32[]{:S(2)}) collective-permute-start(f32[32,1024]{1,0:T(8,128)S(1)} %pad_maximum_fusion.refs_0_), channel_id=1, source_target_pairs={{0,24},{8,16},{16,8},{24,0},{1,25},{9,17},{17,9},{25,1},{2,26},{10... | collective-permute-start | bytes 393224 | tf_op jit(solution)/shard_map/ppermute | solution.py:316
  24.9 17.6 %collective-permute-done.1.across_ref = bf16[64,2560]{1,0:T(8,128)(2,1)S(1)} collective-permute-done((bf16[64,2560]{1,0:T(8,128)(2,1)S(1)}, bf16[64,2560]{1,0:T(8,128)(2,1)S(1)}, u32[]{:S(2)}, u32[]{:S(2)}) %collective-permute-start.1) | collective-permute-done | bytes 327712 | tf_op jit(solution)/shard_map/ppermute | solution.py:275
  42.5 1.4 shard_map.96
  43.9 1.6 %shard_map.95 = bf16[32,16,1280]{2,1,0:T(8,128)(2,1)} custom-call(bf16[128,2560]{1,0:T(8,128)(2,1)S(1)} %get-tuple-element.44.own_ref, bf16[128,2560]{1,0:T(8,128)(2,1)S(1)} %collective-permute-done.across_ref), custom_call_target="tpu_custom_call" | custom-call | flops 1 | bytes 1 | tf_op jit(solution)/shard_map/pallas_call | solution.py:133
  45.5 8.9 %all-to-all-start.1 = ((bf16[32,16,1280]{2,1,0:T(8,128)(2,1)}), bf16[32,16,1280]{2,1,0:T(8,128)(2,1)S(1)}, u32[]{:S(2)}, u32[]{:S(2)}) async-start(bf16[32,16,1280]{2,1,0:T(8,128)(2,1)} %shard_map.95), calls=%async_computation.1 | async-start | bytes 2621440 | tf_op jit(solution)/shard_map/all_to_all | solution.py:283
  54.4 2.2 %shard_map.97 = (bf16[192,1536]{1,0:T(8,128)(2,1)}, bf16[192,1536]{1,0:T(8,128)(2,1)S(1)}) custom-call(bf16[32,48,384]{2,1,0:T(8,128)(2,1)S(1)} %all-to-all-done.in_ref), custom_call_target="tpu_custom_call" | custom-call | flops 1 | bytes 1 | tf_op jit(solution)/shard_map/pallas_call | solution.py:171
  56.6 2.6 %collective-permute-start.6 = (bf16[192,1536]{1,0:T(8,128)(2,1)S(1)}, bf16[192,1536]{1,0:T(8,128)(2,1)S(1)}, u32[]{:S(2)}, u32[]{:S(2)}) collective-permute-start(bf16[192,1536]{1,0:T(8,128)(2,1)S(1)} %get-tuple-element.54), channel_id=1, source_target_pairs={{0,48},{16,32},{32,16},{48,0},{1,49},{17,33},{33,17},{49,1},{2,50}... | collective-permute-start | bytes 1769480 | tf_op jit(solution)/shard_map/ppermute | solution.py:275
  59.3 11.0 %collective-permute-done.6.refs_6_ = bf16[192,1536]{1,0:T(8,128)(2,1)S(1)} collective-permute-done((bf16[192,1536]{1,0:T(8,128)(2,1)S(1)}, bf16[192,1536]{1,0:T(8,128)(2,1)S(1)}, u32[]{:S(2)}, u32[]{:S(2)}) %collective-permute-start.6) | collective-permute-done | bytes 589856 | tf_op jit(solution)/shard_map/ppermute | solution.py:275
  70.5 1.1 collective-permute-done.5.refs_5_
  72.4 13.1 %collective-permute-done.7.refs_7_ = bf16[192,1536]{1,0:T(8,128)(2,1)} collective-permute-done((bf16[192,1536]{1,0:T(8,128)(2,1)S(1)}, bf16[192,1536]{1,0:T(8,128)(2,1)}, u32[]{:S(2)}, u32[]{:S(2)}) %collective-permute-start.7) | collective-permute-done | bytes 589856 | tf_op jit(solution)/shard_map/ppermute | solution.py:275
  86.1 3.9 %collective-permute-start.12 = (bf16[256,2560]{1,0:T(8,128)(2,1)S(1)}, bf16[256,2560]{1,0:T(8,128)(2,1)}, u32[]{:S(2)}, u32[]{:S(2)}) collective-permute-start(bf16[256,2560]{1,0:T(8,128)(2,1)S(1)} %shard_map.98.refs_4_), channel_id=1, source_target_pairs={{0,8},{8,0},{1,9},{9,1},{2,10},{10,2},{3,11},{11,3},{4,12},{12,4},... | collective-permute-start | bytes 3932168 | tf_op jit(solution)/shard_map/ppermute | solution.py:271
  90.0 1.0 collective-permute-start.14
  91.5 6.8 %all-to-all-start.2 = ((bf16[32,16,640]{2,1,0:T(8,128)(2,1)}), bf16[32,16,640]{2,1,0:T(8,128)(2,1)S(1)}, u32[]{:S(2)}, u32[]{:S(2)}) async-start(bf16[32,16,640]{2,1,0:T(8,128)(2,1)} %shard_map.96), calls=%async_computation.2 | async-start | bytes 1310720 | tf_op jit(solution)/shard_map/all_to_all | solution.py:283
  99.3 1.5 %collective-permute-done.9.refs_9_ = bf16[192,1536]{1,0:T(8,128)(2,1)} collective-permute-done((bf16[192,1536]{1,0:T(8,128)(2,1)}, bf16[192,1536]{1,0:T(8,128)(2,1)}, u32[]{:S(2)}, u32[]{:S(2)}) %collective-permute-start.9) | collective-permute-done | bytes 589856 | tf_op jit(solution)/shard_map/ppermute | solution.py:271
  100.8 1.5 %collective-permute-done.10.refs_10_ = bf16[192,1536]{1,0:T(8,128)(2,1)} collective-permute-done((bf16[192,1536]{1,0:T(8,128)(2,1)S(1)}, bf16[192,1536]{1,0:T(8,128)(2,1)}, u32[]{:S(2)}, u32[]{:S(2)}) %collective-permute-start.10) | collective-permute-done | bytes 589856 | tf_op jit(solution)/shard_map/ppermute | solution.py:271
  102.5 1.1 copy-done.4
  103.6 7.6 %shard_map.99 = (f32[384,1536]{1,0:T(8,128)}, f32[32,384]{1,0:T(8,128)}) custom-call(s32[1,1]{1,0:T(1,128)} %bitcast.q_ref, f32[32,1024]{1,0:T(8,128)S(1)} %pad_maximum_fusion.refs_0_, f32[32,1024]{1,0:T(8,128)S(1)} %collective-permute-done.2.refs_1_, f32[32,1024]{1,0:T(8,128)S(1)} %collective-permute-done.3.refs_2_, ...), custom_call_target="tpu_custom_call" | custom-call | flops 1 | bytes 1 | tf_op jit(solution)/shard_map/pallas_call | solution.py:247
  111.1 6.6 %shard_map.100 = (f32[640,2560]{1,0:T(8,128)}, f32[32,640]{1,0:T(8,128)}) custom-call(s32[1,1]{1,0:T(1,128)} %bitcast.q_ref, f32[32,1024]{1,0:T(8,128)S(1)} %pad_maximum_fusion.refs_0_, f32[32,1024]{1,0:T(8,128)S(1)} %collective-permute-done.2.refs_1_, f32[32,1024]{1,0:T(8,128)S(1)} %collective-permute-done.3.refs_2_, ...), custom_call_target="tpu_custom_call" | custom-call | flops 1 | bytes 1 | tf_op jit(solution)/shard_map/pallas_call | solution.py:247
  117.7 2.4 %collective-permute-done.14.refs_4_ = bf16[256,2560]{1,0:T(8,128)(2,1)} collective-permute-done((bf16[256,2560]{1,0:T(8,128)(2,1)S(1)}, bf16[256,2560]{1,0:T(8,128)(2,1)}, u32[]{:S(2)}, u32[]{:S(2)}) %collective-permute-start.14) | collective-permute-done | bytes 1310752 | tf_op jit(solution)/shard_map/ppermute | solution.py:275
  120.2 1.1 collective-permute-start.15
  122.0 1.1 collective-permute-start.13
  123.1 1.8 %collective-permute-done.16.refs_7_ = bf16[128,2560]{1,0:T(8,128)(2,1)S(1)} collective-permute-done((bf16[128,2560]{1,0:T(8,128)(2,1)S(1)}, bf16[128,2560]{1,0:T(8,128)(2,1)S(1)}, u32[]{:S(2)}, u32[]{:S(2)}) %collective-permute-start.16) | collective-permute-done | bytes 655392 | tf_op jit(solution)/shard_map/ppermute | solution.py:271
  124.9 10.2 %shard_map.102 = (f32[640,2560]{1,0:T(8,128)}, f32[32,640]{1,0:T(8,128)}) custom-call(s32[1,1]{1,0:T(1,128)} %bitcast.q_ref, f32[32,1024]{1,0:T(8,128)S(1)} %pad_maximum_fusion.refs_0_, f32[32,1024]{1,0:T(8,128)S(1)} %collective-permute-done.2.refs_1_, f32[32,1024]{1,0:T(8,128)S(1)} %collective-permute-done.3.refs_2_, ...), custom_call_target="tpu_custom_call", output_to_operand_aliasing={{0}: (9, {}), {1}: (10, {})} | custom-call | flops 1 | bytes 1 | tf_op jit(solution)/shard_map/pallas_call | solution.py:247
  135.1 2.8 %collective-permute-done.13.refs_4_ = bf16[128,2560]{1,0:T(8,128)(2,1)S(1)} collective-permute-done((bf16[128,2560]{1,0:T(8,128)(2,1)S(1)}, bf16[128,2560]{1,0:T(8,128)(2,1)S(1)}, u32[]{:S(2)}, u32[]{:S(2)}) %collective-permute-start.13) | collective-permute-done | bytes 655392 | tf_op jit(solution)/shard_map/ppermute | solution.py:275
  138.0 1.2 collective-permute-start.17
  139.2 1.7 %collective-permute-done.17.refs_5_ = bf16[128,2560]{1,0:T(8,128)(2,1)S(1)} collective-permute-done((bf16[128,2560]{1,0:T(8,128)(2,1)S(1)}, bf16[128,2560]{1,0:T(8,128)(2,1)S(1)}, u32[]{:S(2)}, u32[]{:S(2)}) %collective-permute-start.17) | collective-permute-done | bytes 655392 | tf_op jit(solution)/shard_map/ppermute | solution.py:271
  140.9 6.2 %shard_map.103 = (f32[640,2560]{1,0:T(8,128)}, f32[32,640]{1,0:T(8,128)}) custom-call(s32[1,1]{1,0:T(1,128)} %bitcast.q_ref, f32[32,1024]{1,0:T(8,128)S(1)} %pad_maximum_fusion.refs_0_, f32[32,1024]{1,0:T(8,128)S(1)} %collective-permute-done.2.refs_1_, f32[32,1024]{1,0:T(8,128)S(1)} %collective-permute-done.3.refs_2_, ...), custom_call_target="tpu_custom_call", output_to_operand_aliasing={{0}: (7, {}), {1}: (8, {})} | custom-call | flops 1 | bytes 1 | tf_op jit(solution)/shard_map/pallas_call | solution.py:247
  (40 shorter events, 4.2 us)
Async XLA Ops:
  5.8 12.0 %copy-start = (bf16[128,2560]{1,0:T(8,128)(2,1)S(1)}, bf16[128,2560]{1,0:T(8,128)(2,1)}, u32[]{:S(2)}) copy-start(bf16[128,2560]{1,0:T(8,128)(2,1)} %grads_ref.1) | copy-start | bytes 1966084
  5.8 12.1 %copy-start.5 = (s32[128,6]{0,1:T(8,128)S(1)}, s32[128,6]{0,1:T(8,128)}, u32[]{:S(2)}) copy-start(s32[128,6]{0,1:T(8,128)} %param.9) | copy-start | bytes 9220
  5.8 12.1 %copy-start.6 = (f32[128,6]{0,1:T(8,128)S(1)}, f32[128,6]{0,1:T(8,128)}, u32[]{:S(2)}) copy-start(f32[128,6]{0,1:T(8,128)} %param.8) | copy-start | bytes 9220
  5.8 15.9 %copy-start.7 = (f32[1,32,640]{2,1,0:T(8,128)S(1)}, f32[1,32,640]{2,1,0:T(8,128)}, u32[]{:S(2)}) copy-start(f32[1,32,640]{2,1,0:T(8,128)} %param.11) | copy-start | bytes 245764
  5.8 15.9 %copy-start.8 = (f32[1,32,384]{2,1,0:T(8,128)S(1)}, f32[1,32,384]{2,1,0:T(8,128)}, u32[]{:S(2)}) copy-start(f32[1,32,384]{2,1,0:T(8,128)} %param.10) | copy-start | bytes 147460
  5.8 39.7 %all-to-all-start = ((bf16[32,48,384]{2,1,0:T(8,128)(2,1)}), bf16[32,48,384]{2,1,0:T(8,128)(2,1)S(1)}, u32[]{:S(2)}, u32[]{:S(2)}) async-start(bf16[32,48,384]{2,1,0:T(8,128)(2,1)} %shard_map.93), calls=%async_computation | async-start | bytes 2359296 | tf_op jit(solution)/shard_map/all_to_all | solution.py:283
  18.8 25.2 %collective-permute-start = (bf16[128,2560]{1,0:T(8,128)(2,1)S(1)}, bf16[128,2560]{1,0:T(8,128)(2,1)S(1)}, u32[]{:S(2)}, u32[]{:S(2)}) collective-permute-start(bf16[128,2560]{1,0:T(8,128)(2,1)S(1)} %get-tuple-element.45), channel_id=1, source_target_pairs={{0,48},{16,32},{32,16},{48,0},{1,49},{17,33},{33,17},{49,1},{2,50}... | collective-permute-start | bytes 1966088 | tf_op jit(solution)/shard_map/ppermute | solution.py:275
  21.6 20.9 %collective-permute-start.1 = (bf16[64,2560]{1,0:T(8,128)(2,1)S(1)}, bf16[64,2560]{1,0:T(8,128)(2,1)S(1)}, u32[]{:S(2)}, u32[]{:S(2)}) collective-permute-start(bf16[64,2560]{1,0:T(8,128)(2,1)S(1)} %get-tuple-element.47), channel_id=1, source_target_pairs={{0,48},{16,32},{32,16},{48,0},{1,49},{17,33},{33,17},{49,1},{2,50}... | collective-permute-start | bytes 983048 | tf_op jit(solution)/shard_map/ppermute | solution.py:275
  21.7 23.8 %collective-permute-start.2 = (f32[32,1024]{1,0:T(8,128)S(1)}, f32[32,1024]{1,0:T(8,128)S(1)}, u32[]{:S(2)}, u32[]{:S(2)}) collective-permute-start(f32[32,1024]{1,0:T(8,128)S(1)} %pad_maximum_fusion.refs_0_), channel_id=1, source_target_pairs={{0,8},{8,0},{16,24},{24,16},{1,9},{9,1},{17,25},{25,17},{2,10},{10... | collective-permute-start | bytes 393224 | tf_op jit(solution)/shard_map/ppermute | solution.py:316
  23.1 22.4 %collective-permute-start.3 = (f32[32,1024]{1,0:T(8,128)S(1)}, f32[32,1024]{1,0:T(8,128)S(1)}, u32[]{:S(2)}, u32[]{:S(2)}) collective-permute-start(f32[32,1024]{1,0:T(8,128)S(1)} %pad_maximum_fusion.refs_0_), channel_id=1, source_target_pairs={{0,16},{8,24},{16,0},{24,8},{1,17},{9,25},{17,1},{25,9},{2,18},{10... | collective-permute-start | bytes 393224 | tf_op jit(solution)/shard_map/ppermute | solution.py:316
  23.3 22.2 %collective-permute-start.4 = (f32[32,1024]{1,0:T(8,128)S(1)}, f32[32,1024]{1,0:T(8,128)S(1)}, u32[]{:S(2)}, u32[]{:S(2)}) collective-permute-start(f32[32,1024]{1,0:T(8,128)S(1)} %pad_maximum_fusion.refs_0_), channel_id=1, source_target_pairs={{0,24},{8,16},{16,8},{24,0},{1,25},{9,17},{17,9},{25,1},{2,26},{10... | collective-permute-start | bytes 393224 | tf_op jit(solution)/shard_map/ppermute | solution.py:316
  45.5 40.0 %all-to-all-start.1 = ((bf16[32,16,1280]{2,1,0:T(8,128)(2,1)}), bf16[32,16,1280]{2,1,0:T(8,128)(2,1)S(1)}, u32[]{:S(2)}, u32[]{:S(2)}) async-start(bf16[32,16,1280]{2,1,0:T(8,128)(2,1)} %shard_map.95), calls=%async_computation.1 | async-start | bytes 2621440 | tf_op jit(solution)/shard_map/all_to_all | solution.py:283
  56.6 13.6 %collective-permute-start.6 = (bf16[192,1536]{1,0:T(8,128)(2,1)S(1)}, bf16[192,1536]{1,0:T(8,128)(2,1)S(1)}, u32[]{:S(2)}, u32[]{:S(2)}) collective-permute-start(bf16[192,1536]{1,0:T(8,128)(2,1)S(1)} %get-tuple-element.54), channel_id=1, source_target_pairs={{0,48},{16,32},{32,16},{48,0},{1,49},{17,33},{33,17},{49,1},{2,50}... | collective-permute-start | bytes 1769480 | tf_op jit(solution)/shard_map/ppermute | solution.py:275
  59.3 12.3 %collective-permute-start.5 = (bf16[192,1536]{1,0:T(8,128)(2,1)}, bf16[192,1536]{1,0:T(8,128)(2,1)S(1)}, u32[]{:S(2)}, u32[]{:S(2)}) collective-permute-start(bf16[192,1536]{1,0:T(8,128)(2,1)} %get-tuple-element.57.refs_4_), channel_id=1, source_target_pairs={{0,16},{16,0},{32,48},{48,32},{1,17},{17,1},{33,49},{49,33},{2,18}... | collective-permute-start | bytes 1769480 | tf_op jit(solution)/shard_map/ppermute | solution.py:275
  70.3 1.3 copy-start.1
  70.3 15.3 %collective-permute-start.7 = (bf16[192,1536]{1,0:T(8,128)(2,1)S(1)}, bf16[192,1536]{1,0:T(8,128)(2,1)}, u32[]{:S(2)}, u32[]{:S(2)}) collective-permute-start(bf16[192,1536]{1,0:T(8,128)(2,1)S(1)} %collective-permute-done.6.refs_6_), channel_id=1, source_target_pairs={{0,16},{16,0},{32,48},{48,32},{1,17},{17,1},{33,49},{49,33},{2,18}... | collective-permute-start | bytes 1769480 | tf_op jit(solution)/shard_map/ppermute | solution.py:275
  71.6 0.8 copy-start.3
  86.1 12.7 %copy-start.2 = (bf16[192,1536]{1,0:T(8,128)(2,1)S(1)}, bf16[192,1536]{1,0:T(8,128)(2,1)}, u32[]{:S(2)}) copy-start(bf16[192,1536]{1,0:T(8,128)(2,1)} %copy-done.1) | copy-start | bytes 1769476
  86.1 25.1 %collective-permute-start.12 = (bf16[256,2560]{1,0:T(8,128)(2,1)S(1)}, bf16[256,2560]{1,0:T(8,128)(2,1)}, u32[]{:S(2)}, u32[]{:S(2)}) collective-permute-start(bf16[256,2560]{1,0:T(8,128)(2,1)S(1)} %shard_map.98.refs_4_), channel_id=1, source_target_pairs={{0,8},{8,0},{1,9},{9,1},{2,10},{10,2},{3,11},{11,3},{4,12},{12,4},... | collective-permute-start | bytes 3932168 | tf_op jit(solution)/shard_map/ppermute | solution.py:271
  90.0 30.2 %collective-permute-start.14 = (bf16[256,2560]{1,0:T(8,128)(2,1)S(1)}, bf16[256,2560]{1,0:T(8,128)(2,1)}, u32[]{:S(2)}, u32[]{:S(2)}) collective-permute-start(bf16[256,2560]{1,0:T(8,128)(2,1)S(1)} %shard_map.98.refs_4_), channel_id=1, source_target_pairs={{0,16},{16,0},{32,48},{48,32},{1,17},{17,1},{33,49},{49,33},{2,18}... | collective-permute-start | bytes 3932168 | tf_op jit(solution)/shard_map/ppermute | solution.py:275
  91.0 8.0 %collective-permute-start.8 = (bf16[192,1536]{1,0:T(8,128)(2,1)}, bf16[192,1536]{1,0:T(8,128)(2,1)}, u32[]{:S(2)}, u32[]{:S(2)}) collective-permute-start(bf16[192,1536]{1,0:T(8,128)(2,1)} %get-tuple-element.57.refs_4_), channel_id=1, source_target_pairs={{0,8},{8,0},{1,9},{9,1},{2,10},{10,2},{3,11},{11,3},{4,12},{12,4},... | collective-permute-start | bytes 1769480 | tf_op jit(solution)/shard_map/ppermute | solution.py:271
  91.5 29.7 %all-to-all-start.2 = ((bf16[32,16,640]{2,1,0:T(8,128)(2,1)}), bf16[32,16,640]{2,1,0:T(8,128)(2,1)S(1)}, u32[]{:S(2)}, u32[]{:S(2)}) async-start(bf16[32,16,640]{2,1,0:T(8,128)(2,1)} %shard_map.96), calls=%async_computation.2 | async-start | bytes 1310720 | tf_op jit(solution)/shard_map/all_to_all | solution.py:283
  98.4 2.4 %collective-permute-start.9 = (bf16[192,1536]{1,0:T(8,128)(2,1)}, bf16[192,1536]{1,0:T(8,128)(2,1)}, u32[]{:S(2)}, u32[]{:S(2)}) collective-permute-start(bf16[192,1536]{1,0:T(8,128)(2,1)} %copy-done.3), channel_id=1, source_target_pairs={{0,8},{8,0},{1,9},{9,1},{2,10},{10,2},{3,11},{11,3},{4,12},{12,4},... | collective-permute-start | bytes 1769480 | tf_op jit(solution)/shard_map/ppermute | solution.py:271
  98.7 3.5 %collective-permute-start.10 = (bf16[192,1536]{1,0:T(8,128)(2,1)S(1)}, bf16[192,1536]{1,0:T(8,128)(2,1)}, u32[]{:S(2)}, u32[]{:S(2)}) collective-permute-start(bf16[192,1536]{1,0:T(8,128)(2,1)S(1)} %copy-done.2), channel_id=1, source_target_pairs={{0,8},{8,0},{1,9},{9,1},{2,10},{10,2},{3,11},{11,3},{4,12},{12,4},... | collective-permute-start | bytes 1769480 | tf_op jit(solution)/shard_map/ppermute | solution.py:271
  99.0 3.5 %collective-permute-start.11 = (bf16[192,1536]{1,0:T(8,128)(2,1)}, bf16[192,1536]{1,0:T(8,128)(2,1)}, u32[]{:S(2)}, u32[]{:S(2)}) collective-permute-start(bf16[192,1536]{1,0:T(8,128)(2,1)} %collective-permute-done.7.refs_7_), channel_id=1, source_target_pairs={{0,8},{8,0},{1,9},{9,1},{2,10},{10,2},{3,11},{11,3},{4,12},{12,4},... | collective-permute-start | bytes 1769480 | tf_op jit(solution)/shard_map/ppermute | solution.py:271
  102.5 1.1 copy-start.4
  120.2 4.7 %collective-permute-start.15 = (bf16[256,2560]{1,0:T(8,128)(2,1)}, bf16[256,2560]{1,0:T(8,128)(2,1)S(1)}, u32[]{:S(2)}, u32[]{:S(2)}) collective-permute-start(bf16[256,2560]{1,0:T(8,128)(2,1)} %collective-permute-done.14.refs_4_), channel_id=1, source_target_pairs={{0,8},{8,0},{1,9},{9,1},{2,10},{10,2},{3,11},{11,3},{4,12},{12,4},... | collective-permute-start | bytes 3932168 | tf_op jit(solution)/shard_map/ppermute | solution.py:271
  121.9 3.0 %collective-permute-start.16 = (bf16[128,2560]{1,0:T(8,128)(2,1)S(1)}, bf16[128,2560]{1,0:T(8,128)(2,1)S(1)}, u32[]{:S(2)}, u32[]{:S(2)}) collective-permute-start(bf16[128,2560]{1,0:T(8,128)(2,1)S(1)} %shard_map.101.refs_6_), channel_id=1, source_target_pairs={{0,8},{8,0},{1,9},{9,1},{2,10},{10,2},{3,11},{11,3},{4,12},{12,4},... | collective-permute-start | bytes 1966088 | tf_op jit(solution)/shard_map/ppermute | solution.py:271
  122.0 16.0 %collective-permute-start.13 = (bf16[128,2560]{1,0:T(8,128)(2,1)S(1)}, bf16[128,2560]{1,0:T(8,128)(2,1)S(1)}, u32[]{:S(2)}, u32[]{:S(2)}) collective-permute-start(bf16[128,2560]{1,0:T(8,128)(2,1)S(1)} %shard_map.101.refs_6_), channel_id=1, source_target_pairs={{0,16},{16,0},{32,48},{48,32},{1,17},{17,1},{33,49},{49,33},{2,18}... | collective-permute-start | bytes 1966088 | tf_op jit(solution)/shard_map/ppermute | solution.py:275
  138.0 3.0 %collective-permute-start.17 = (bf16[128,2560]{1,0:T(8,128)(2,1)S(1)}, bf16[128,2560]{1,0:T(8,128)(2,1)S(1)}, u32[]{:S(2)}, u32[]{:S(2)}) collective-permute-start(bf16[128,2560]{1,0:T(8,128)(2,1)S(1)} %collective-permute-done.13.refs_4_), channel_id=1, source_target_pairs={{0,8},{8,0},{1,9},{9,1},{2,10},{10,2},{3,11},{11,3},{4,12},{12,4},... | collective-permute-start | bytes 1966088 | tf_op jit(solution)/shard_map/ppermute | solution.py:271
